TPU v7x, 32 devices: a whole 2x2x4 slice. The times are simulated.
32 devices in a mesh: pb: 8 (over y, x, core), ka: 4 (over z).
Axes of the slice: x: 2, y: 2, z: 4, core: 2. Of those that a mesh axis runs over, the one named last changes fastest.
Arguments:
- queries: bfloat16 [4096, 4096], P('pb'), may hold values from -6 to 6
- key_rows: bfloat16 [4096, 512], P(('pb', 'ka')), may hold values from -6 to 6
- values: bfloat16 [4096, 512], P(('pb', 'ka')), may hold values from -6 to 6
- attn_out: bfloat16 [4096, 4096], P(('pb', 'ka')), may hold values from -6 to 6
- grad_out: bfloat16 [4096, 4096], P('pb'), may hold values from -6 to 6
- log_sums: float32 [32, 4096], P(None, ('pb', 'ka')), may hold values from 3 to 7
- key_gain: float32 [512], replicated, may hold values from 0.25 to 1.75
- value_gain: float32 [512], replicated, may hold values from 0.25 to 1.75
- doc_ids: int32 [32], replicated, may hold values from 0 to 3, never falling along the last dimension, each value on 1 to 16 neighbouring positions
- tile_mask: int32 [32, 32], replicated, may hold values 0 or 1
- block_order: int32 [32], replicated, may hold values from 0 to 31, each once
Outputs:
- grad_queries: bfloat16 [4096, 4096], P(('pb', 'ka'))
- grad_keys: bfloat16 [4096, 512], P(('pb', 'ka'))
- grad_values: bfloat16 [4096, 512], P(('pb', 'ka'))
- grad_key_gain: float32 [512], replicated
- grad_value_gain: float32 [512], replicated
Inputs may be any that keep to these rules, and one draw needn't show every extreme that they name: `doc_ids`: documents are numbered in sequence order; each spans 1 to 16 tiles, one exactly that many. `block_order`: each sequence tile once.
All inputs are finite; a program needn't handle non-finite values.
Results may differ from a plain program's by a relative error of at most 0.015.
Values may be sent and summed in bfloat16 or wider, within the bound.
No kernel may reach another device: no remote copies, remote signals or barrier semaphores. Data moves between devices by JAX's collectives and lax.ppermute only.
A program may use at most 192 MiB of HBM per device.

v0:
```python
import functools

import jax
import jax.numpy as jnp
from jax import lax
from jax.experimental import pallas as pl
from jax.experimental.pallas import tpu as pltpu
from jax.sharding import PartitionSpec as P

HEAD_DIM = 128
TILE = 128
SPARE = 16
LOG2E = 1.4426950408889634
ENTRY = 4
PARTS = 4
STAT_TERMS = 2
EARLY = 2
LAST_DIMS = (((1,), (1,)), ((), ()))
VMEM = pltpu.VMEM
SMEM = pltpu.SMEM
F32 = jnp.float32
BF16 = jnp.bfloat16


def split_float(x, count):
    terms = []
    for _ in range(count):
        terms.append(x.astype(BF16).astype(F32))
        x = x - terms[-1]
    return terms


def head_rows(heads_dev):
    return -(-heads_dev // 8) * 8


def extra_rows(heads_dev):
    return STAT_TERMS * head_rows(heads_dev)


def prepare_kernel(dims, key_ref, value_ref, attn_ref, grads_ref, lse_ref, *rest):
    count_ka, heads, heads_dev, share = dims
    outs, (attn, grad, kv, lse_pad, delta_pad, sems) = rest[:count_ka], rest[count_ka:]
    _, place_ka = places()
    rows8 = head_rows(heads_dev)
    part_heads = heads // PARTS
    rows = pl.ds(pl.multiple_of(place_ka * TILE, TILE), TILE)
    copies = []
    for part in range(PARTS):
        columns = pl.ds(part * part_heads * HEAD_DIM, part_heads * HEAD_DIM)
        copies.append((
            pltpu.make_async_copy(attn_ref.at[:, columns], attn.at[part], sems.at[0, part]),
            pltpu.make_async_copy(grads_ref.at[rows, columns], grad.at[part], sems.at[1, part]),
        ))
    copies.append((
        pltpu.make_async_copy(key_ref, kv.at[0], sems.at[2, 0]),
        pltpu.make_async_copy(value_ref, kv.at[1], sems.at[2, 1]),
        pltpu.make_async_copy(lse_ref, lse_pad.at[pl.ds(0, heads), :], sems.at[2, 2]),
    ))
    for pair in copies:
        for copy in pair:
            copy.start()
    lanes = lax.broadcasted_iota(jnp.int32, (TILE, TILE), 1)
    columns = jnp.zeros((TILE, TILE), F32)
    for part in range(PARTS):
        for copy in copies[part]:
            copy.wait()
        for head in range(part_heads):
            at = pl.ds(head * HEAD_DIM, HEAD_DIM)
            products = grad[part, :, at].astype(F32) * attn[part, :, at].astype(F32)
            total = jnp.sum(products, axis=1, keepdims=True)
            columns = jnp.where(lanes == part * part_heads + head, total, columns)
    delta_pad[...] = jnp.zeros_like(delta_pad)
    lse_pad[pl.ds(heads, 8), :] = jnp.zeros((8, TILE), F32)
    delta_pad[:heads, :] = columns.T[:heads, :]
    for copy in copies[-1]:
        copy.wait()
    for step in range(count_ka):
        target = lax.rem(place_ka + step, count_ka)
        kv_at = pl.ds(pl.multiple_of(target // share * HEAD_DIM, HEAD_DIM), HEAD_DIM)
        outs[step][:TILE, :HEAD_DIM] = kv[0, :, kv_at]
        outs[step][:TILE, HEAD_DIM:] = kv[1, :, kv_at]
        head_at = pl.ds(target * heads_dev, rows8)
        both = jnp.concatenate([lse_pad[head_at, :], delta_pad[head_at, :]], axis=1)
        outs[step][TILE:, :] = jnp.concatenate(split_float(both, STAT_TERMS), axis=0).astype(BF16)


def own_heads_kernel(queries_ref, grads_ref, out_ref, sems):
    _, place_ka = places()
    width = out_ref.shape[2]
    columns = pl.ds(pl.multiple_of(place_ka * width, HEAD_DIM), width)
    copies = [
        pltpu.make_async_copy(ref.at[:, columns], out_ref.at[number], sems.at[number])
        for number, ref in enumerate((queries_ref, grads_ref))
    ]
    for copy in copies:
        copy.start()
    for copy in copies:
        copy.wait()


def places():
    return lax.axis_index("pb"), lax.axis_index("ka")


def own_start(key_tiles, count_ka):
    return 3 + count_ka * key_tiles


def plan_kernel(dims, order_ref, doc_ref, mask_ref, table):
    count_chip, count_ka, order = dims
    place_pb, place_ka = places()
    own_at = own_start(count_chip * count_ka, count_ka)

    def walk(start, query_pb, key_pb, steps, units):
        def query_step(turn_q, units):
            step_q = jnp.int32(order[0])
            for number, step in enumerate(order):
                step_q = jnp.where(turn_q == number, step, step_q)
            tile_at = lax.rem(place_ka + step_q, count_ka)
            seq_q = order_ref[query_pb * count_ka + tile_at]
            doc_q = doc_ref[seq_q]

            def collect(number, units):
                for step in range(count_ka):
                    stored = (key_pb ^ (2 * number)) * count_ka + lax.rem(
                        place_ka - step + count_ka, count_ka
                    )
                    seq_k = order_ref[stored]
                    live = (mask_ref[seq_q, seq_k] == 1) & (doc_ref[seq_k] == doc_q) & (seq_q >= seq_k)
                    if start is not None:
                        base = ENTRY * (start + units)
                        table[base] = turn_q
                        table[base + 1] = tile_at
                        table[base + 2] = number * count_ka + step
                        table[base + 3] = jnp.where(seq_q == seq_k, 0, -TILE)
                    units = units + live.astype(jnp.int32)
                return units

            return lax.fori_loop(0, count_chip, collect, units)

        return lax.fori_loop(*steps, query_step, units)

    def close(start, units):
        base = ENTRY * (start + units)
        table[base] = 0
        table[base + 1] = 0
        table[base + 2] = 0
        table[base + 3] = TILE
        return (units + 1) // 2

    def steps_of(units):
        return (units + 1) // 2

    none = jnp.int32(0)
    sibling = place_pb ^ 1
    other_first = walk(2, place_pb, sibling, (0, EARLY), none)
    other = close(2, walk(2, place_pb, sibling, (EARLY, count_ka), other_first))
    own_first = walk(own_at, place_pb, place_pb, (0, EARLY), none)
    own = close(own_at, walk(own_at, place_pb, place_pb, (EARLY, count_ka), own_first))
    there = steps_of(walk(None, sibling, sibling, (0, EARLY), none))
    there = there + steps_of(walk(None, sibling, place_pb, (0, count_ka), none))
    lead = jnp.maximum(there - other - steps_of(own_first), 0)
    table[0] = steps_of(own_first)
    table[1] = jnp.minimum(steps_of(own_first) + lead, own)
    table[2] = own
    table[ENTRY] = steps_of(other_first)
    table[ENTRY + 1] = other


def attention_kernel(dims, *rest):
    count_chip, count_ka, heads_dev, share, stage = dims
    table, rest = rest[0], rest[1:]
    if stage < 2:
        (key_gain_ref, value_gain_ref), rest = rest[:2], rest[2:]
    (heads_ref, stats_ref), rest = rest[:2], rest[2:]
    if stage < 2:
        blocks, rest = rest[:count_chip], rest[count_chip:]
    if stage == 0:
        (dq_sum, *own), rest = rest[:6], rest[6:]
    elif stage == 1:
        (dq_start, dq_sum, *dq_early), other, rest = rest[:2 + EARLY], rest[2 + EARLY:7 + EARLY], rest[7 + EARLY:]
    elif stage == 2:
        (dq_start, *own_start_refs), rest = rest[:6], rest[6:]
        other_refs, rest = rest[:5], rest[5:]
        (dq_sum, *own_sums, kv_other, other_key_sum, other_value_sum), rest = rest[:6], rest[6:]
        own = own_start_refs[:3] + own_sums
        other = other_refs[:3] + (other_key_sum, other_value_sum)
    else:
        (dq_start, *own_start_refs), rest = rest[:6], rest[6:]
        dq_outs, rest = rest[:count_ka - EARLY], rest[count_ka - EARLY:]
        (*own_sums, dq_sum), rest = rest[:3], rest[3:]
        own = own_start_refs[:3] + own_sums
    lse_delta, weights_low, dscores_low = rest
    _, place_ka = places()
    rows8 = head_rows(heads_dev)
    spare = extra_rows(heads_dev)
    score_scale = HEAD_DIM ** -0.5

    if stage < 2:
        kv_at = pl.ds(pl.multiple_of(place_ka // share * HEAD_DIM, HEAD_DIM), HEAD_DIM)
        key_gain = key_gain_ref[:, kv_at]
        value_gain = value_gain_ref[:, kv_at]
        keys, values, keys_t, key_sum, value_sum = other if stage else own
        for number in range(count_chip):
            for step in range(count_ka):
                part = pl.ds(step * TILE, TILE)
                local = number * count_ka + step
                key_tile = (blocks[number][part, :HEAD_DIM].astype(F32) * key_gain).astype(BF16)
                value_tile = (blocks[number][part, HEAD_DIM:].astype(F32) * value_gain).astype(BF16)
                keys[local] = key_tile
                values[local] = value_tile
                keys_t[local] = key_tile.T
        key_sum[...] = jnp.zeros_like(key_sum)
        value_sum[...] = jnp.zeros_like(value_sum)
    else:
        for target, source in zip(own_sums, own_start_refs[3:]):
            target[...] = source[...]
    if stage == 0:
        dq_sum[...] = jnp.zeros_like(dq_sum)
    else:
        dq_sum[...] = dq_start[...]
    if stage == 2:
        other_key_sum[...] = other_refs[3][...]
        other_value_sum[...] = other_refs[4][...]

    for slot in range(count_ka):
        packed = stats_ref[pl.ds(slot * spare, spare), :].astype(F32)
        terms = [packed[term * rows8:(term + 1) * rows8] for term in range(STAT_TERMS)]
        total = sum(terms[1:], terms[0])
        lse_delta[slot, :, :TILE] = total[:, :TILE] * LOG2E
        lse_delta[slot, :, TILE:] = total[:, TILE:]

    reach = (lax.broadcasted_iota(jnp.int32, (TILE, TILE), 1)
             - lax.broadcasted_iota(jnp.int32, (TILE, TILE), 0))
    reach = jnp.concatenate([reach, reach], axis=1)

    def run(start, refs, first, last):
        keys, values, keys_t, key_sum, value_sum = refs

        def heads_of(kind, tile_at, heads):
            rows = pl.ds(pl.multiple_of(tile_at * TILE, TILE), TILE)
            return jnp.concatenate(
                [heads_ref[kind, rows, pl.ds(head * HEAD_DIM, HEAD_DIM)] for head in heads], axis=0
            )

        def unit_step(at, carry):
            terms = []
            for lane in range(2):
                base = ENTRY * (start + 2 * at + lane)
                turn_q, tile_at, key_at = table[base], table[base + 1], table[base + 2]
                slot = lax.rem(place_ka - tile_at + count_ka, count_ka)
                allowed = reach >= table[base + 3]
                for head in range(0, heads_dev, 2):
                    part = pl.ds(head * HEAD_DIM, 2 * HEAD_DIM)
                    both = (head, head + 1)
                    scores = lax.dot_general(
                        keys[key_at], heads_of(0, tile_at, both), LAST_DIMS, preferred_element_type=F32
                    )
                    dweights = lax.dot_general(
                        values[key_at], heads_of(1, tile_at, both), LAST_DIMS, preferred_element_type=F32
                    )
                    lse_row, delta_row = [
                        jnp.concatenate(
                            [lse_delta[slot, number:number + 1, lanes] for number in both], axis=1
                        )
                        for lanes in (slice(0, TILE), slice(TILE, 2 * TILE))
                    ]
                    weights = jnp.exp2(scores * (score_scale * LOG2E) - lse_row)
                    weights = jnp.where(allowed, weights, 0.0)
                    weights_low[lane, :, part] = weights.astype(BF16)
                    dscores_low[lane, :, part] = (weights * (dweights - delta_row)).astype(BF16)
                every = range(heads_dev)
                terms.append((
                    turn_q,
                    key_at,
                    jnp.dot(weights_low[lane], heads_of(1, tile_at, every), preferred_element_type=F32),
                    jnp.dot(dscores_low[lane], heads_of(0, tile_at, every), preferred_element_type=F32),
                    jnp.dot(keys_t[key_at], dscores_low[lane], preferred_element_type=F32),
                ))
            for turn_q, key_at, value_term, key_term, dq_term in terms:
                value_sum[key_at] += value_term
                key_sum[key_at] += key_term
                dq_sum[turn_q] += dq_term
            return carry

        lax.fori_loop(first, last, unit_step, 0)

    own_at = own_start(count_chip * count_ka, count_ka)
    if stage == 0:
        run(own_at, own, 0, table[0])
    elif stage == 1:
        run(2, other, 0, table[ENTRY])
        for number, dq_out in enumerate(dq_early):
            dq_out[...] = (dq_sum[number] * score_scale).astype(BF16)
    elif stage == 2:
        run(2, other, table[ENTRY], table[ENTRY + 1])
        run(own_at, own, table[0], table[1])
        for local in range(count_chip * count_ka):
            part = pl.ds(local * TILE, TILE)
            kv_other[part, :HEAD_DIM] = (other_key_sum[local] * score_scale).astype(BF16)
            kv_other[part, HEAD_DIM:] = other_value_sum[local].astype(BF16)
    else:
        run(own_at, own, table[1], table[2])
        for number, dq_out in enumerate(dq_outs, EARLY):
            dq_out[...] = (dq_sum[number] * score_scale).astype(BF16)


def merge_kernel(dims, key_sum, value_sum, kv_back, *rest):
    count_chip, count_ka = dims
    blocks, kv_outs = rest[:count_chip], rest[count_chip:]
    key_gains = jnp.zeros((8, HEAD_DIM), F32)
    value_gains = jnp.zeros((8, HEAD_DIM), F32)
    for number in range(count_chip):
        for step in range(count_ka):
            local = number * count_ka + step
            there = pl.ds(local * TILE, TILE)
            key_total = key_sum[local] * HEAD_DIM ** -0.5 + kv_back[there, :HEAD_DIM].astype(F32)
            value_total = value_sum[local] + kv_back[there, HEAD_DIM:].astype(F32)
            out_ref = kv_outs[number]
            part = pl.ds(step * TILE, TILE)
            out_ref[part, :HEAD_DIM] = key_total.astype(out_ref.dtype)
            out_ref[part, HEAD_DIM:] = value_total.astype(out_ref.dtype)
            key_raw = blocks[number][part, :HEAD_DIM].astype(F32)
            value_raw = blocks[number][part, HEAD_DIM:].astype(F32)
            key_gains += jnp.sum((key_total * key_raw).reshape(TILE // 8, 8, HEAD_DIM), axis=0)
            value_gains += jnp.sum((value_total * value_raw).reshape(TILE // 8, 8, HEAD_DIM), axis=0)
    gains = jnp.concatenate([jnp.sum(key_gains, axis=0, keepdims=True),
                             jnp.sum(value_gains, axis=0, keepdims=True)], axis=1)
    packed = pack_gains(gains)
    for out_ref in kv_outs:
        out_ref[count_ka * TILE:, :] = packed.astype(out_ref.dtype)


def pack_gains(gains):
    rows = lax.broadcasted_iota(jnp.int32, (SPARE, gains.shape[1]), 0)
    high, middle, low = split_float(gains, 3)
    packed = jnp.where(rows == 0, high, jnp.where(rows == 1, middle, low))
    return jnp.where(rows < 3, packed, 0.0)


def add_parts(parts, rows):
    total = parts[0][rows, :]
    for part in parts[1:]:
        total = total + part[rows, :].astype(F32)
    return total


def own_gain(key_gain_ref, value_gain_ref, share):
    kv_at = pl.ds(pl.multiple_of(places()[1] // share * HEAD_DIM, HEAD_DIM), HEAD_DIM)
    return jnp.concatenate([key_gain_ref[:, kv_at], value_gain_ref[:, kv_at]], axis=1)


def collect_kernel(dims, key_gain_ref, value_gain_ref, *rest):
    count_chip, count_ka, share = dims
    parts, outs = rest[:count_chip], rest[count_chip:]
    gain = own_gain(key_gain_ref, value_gain_ref, share)
    total = add_parts(parts, pl.ds(count_ka * TILE, SPARE))
    packed = pack_gains(jnp.sum(total, axis=0, keepdims=True))
    for step, out_ref in enumerate(outs):
        total = add_parts(parts, pl.ds(step * TILE, TILE))
        if share == 1:
            total = total * gain
        out_ref[:TILE, :] = total.astype(out_ref.dtype)
        out_ref[TILE:, :] = packed.astype(out_ref.dtype)


def place_kernel(dims, *rest):
    count_ka, steps = dims
    pieces, (dq_out, turned, sems) = rest[:count_ka], rest[count_ka:]
    copies = []
    for number, (step, piece) in enumerate(zip(steps, pieces)):
        width = piece.shape[1]
        source = lax.rem(places()[1] - step + count_ka, count_ka)
        columns = pl.ds(pl.multiple_of(source * width, HEAD_DIM), width)
        for head in range(width // HEAD_DIM):
            part = pl.ds(head * HEAD_DIM, HEAD_DIM)
            turned[number, :, part] = piece[:, part].T
        copies.append(pltpu.make_async_copy(turned.at[number], dq_out.at[:, columns], sems.at[number]))
        copies[-1].start()
    for copy in copies:
        copy.wait()


def gains_kernel(gains_ref, other_ref, key_gain_out, value_gain_out):
    key_gain_out[...] = gains_ref[0:1, :] + other_ref[0:1, :]
    value_gain_out[...] = gains_ref[1:2, :] + other_ref[1:2, :]


def finish_kernel(dims, key_gain_ref, value_gain_ref, *rest):
    count_ka, share = dims
    pieces, rest = rest[:count_ka], rest[count_ka:]
    dk_out, dv_out, gains_out, sums = rest
    _, place_ka = places()
    sums[...] = jnp.zeros_like(sums)
    for step in range(count_ka):
        source = lax.rem(place_ka + step, count_ka)
        sums[source // share] += pieces[step][...].astype(F32)
    for head in range(count_ka // share):
        part = pl.ds(head * HEAD_DIM, HEAD_DIM)
        key_total = sums[head, :TILE, :HEAD_DIM]
        value_total = sums[head, :TILE, HEAD_DIM:]
        if share > 1:
            key_total = key_total * key_gain_ref[:, part]
            value_total = value_total * value_gain_ref[:, part]
        dk_out[:, part] = key_total.astype(BF16)
        dv_out[:, part] = value_total.astype(BF16)
        gains = jnp.sum(sums[head, TILE:, :], axis=0, keepdims=True)
        gains_out[0:1, part] = gains[:, :HEAD_DIM]
        gains_out[1:2, part] = gains[:, HEAD_DIM:]


def in_vmem(count):
    return [pl.BlockSpec(memory_space=VMEM)] * count


def in_smem(count):
    return [pl.BlockSpec(memory_space=SMEM)] * count


def anywhere(count):
    return [pl.BlockSpec(memory_space=pl.ANY)] * count


def params(mib):
    return pltpu.CompilerParams(vmem_limit_bytes=mib * 1024 * 1024)


def shards(
    queries,
    key_rows,
    values,
    attn_out,
    grad_out,
    log_sums,
    key_gain,
    value_gain,
    doc_ids,
    tile_mask,
    block_order,
):
    count_pb = lax.axis_size("pb")
    count_ka = lax.axis_size("ka")
    rows_dev = key_rows.shape[0]
    query_rows = queries.shape[0]
    heads = log_sums.shape[0]
    feat_width = queries.shape[1]
    kv_heads = key_rows.shape[1] // HEAD_DIM
    heads_dev = heads // count_ka
    share = count_ka // kv_heads
    assert rows_dev == TILE and share * kv_heads == count_ka and count_pb & (count_pb - 1) == 0
    width = heads_dev * HEAD_DIM
    key_gain = key_gain.reshape(1, -1)
    value_gain = value_gain.reshape(1, -1)

    spare = extra_rows(heads_dev)
    count_chip = count_pb // 2

    def swap(array, number):
        return lax.ppermute(array, "pb", [(at, at ^ number) for at in range(count_pb)])

    def turn(array, step):
        return lax.ppermute(array, "ka", [(at, (at + step) % count_ka) for at in range(count_ka)])

    sends = pl.pallas_call(
        functools.partial(prepare_kernel, (count_ka, heads, heads_dev, share)),
        in_specs=anywhere(5),
        out_specs=in_vmem(count_ka),
        out_shape=[jax.ShapeDtypeStruct((TILE + spare, 2 * HEAD_DIM), BF16)] * count_ka,
        scratch_shapes=[VMEM((PARTS, TILE, feat_width // PARTS), BF16)] * 2
        + [VMEM((2, *key_rows.shape), BF16)]
        + [VMEM((heads + 8, TILE), F32)] * 2
        + [pltpu.SemaphoreType.DMA((3, PARTS))],
        compiler_params=params(57),
        name="prepare",
    )(key_rows, values, attn_out, grad_out, log_sums)
    messages = [sends[0]] + [turn(sends[step], step) for step in range(1, count_ka)]

    later_queries, _ = lax.optimization_barrier((queries, sends[0]))
    own_queries = pl.pallas_call(
        own_heads_kernel,
        in_specs=anywhere(2),
        out_specs=in_vmem(1)[0],
        out_shape=jax.ShapeDtypeStruct((2, query_rows, width), BF16),
        scratch_shapes=[pltpu.SemaphoreType.DMA((2,))],
        compiler_params=params(48),
        cost_estimate=pl.CostEstimate(flops=0, bytes_accessed=8 * query_rows * width, transcendentals=0),
        name="own_heads",
    )(later_queries, grad_out)
    messages, own_queries = lax.optimization_barrier((messages, own_queries))
    own_block = jnp.concatenate([message[:TILE] for message in messages], axis=0)
    blocks = [own_block] + [swap(own_block, 2 * number) for number in range(1, count_chip)]
    other_blocks = [swap(block, 1) for block in blocks]
    own_stats = jnp.concatenate([message[TILE:] for message in messages], axis=0)
    later_order, _ = lax.optimization_barrier((block_order, own_block))

    key_tiles = count_chip * count_ka
    sum_shape = jax.ShapeDtypeStruct((key_tiles, TILE, HEAD_DIM), F32)
    key_shape = jax.ShapeDtypeStruct((key_tiles, TILE, HEAD_DIM), BF16)
    kv_shape = (query_rows + SPARE, 2 * HEAD_DIM)
    half = count_ka // 2
    early = (half, 1)
    late = tuple(step for step in range(count_ka) if step not in early)
    order = early + late
    entries = own_start(key_tiles, count_ka) + 1 + count_ka * key_tiles
    table = pl.pallas_call(
        functools.partial(plan_kernel, (count_chip, count_ka, order)),
        in_specs=in_smem(3),
        out_specs=in_smem(1)[0],
        out_shape=jax.ShapeDtypeStruct((ENTRY * entries,), jnp.int32),
        cost_estimate=pl.CostEstimate(flops=0, bytes_accessed=1 << 22, transcendentals=0),
        name="plan",
    )(later_order, doc_ids, tile_mask)

    def attend(stage, outs, scratch, *operands):
        return pl.pallas_call(
            functools.partial(attention_kernel, (count_chip, count_ka, heads_dev, share, stage)),
            in_specs=in_smem(1) + in_vmem(len(operands)),
            out_specs=in_vmem(len(outs)),
            out_shape=outs,
            scratch_shapes=scratch + [
                VMEM((count_ka, head_rows(heads_dev), 2 * TILE), F32),
                VMEM((2, TILE, width), BF16),
                VMEM((2, TILE, width), BF16),
            ],
            compiler_params=params(14 + key_tiles * 11 // 16),
            cost_estimate=pl.CostEstimate(
                flops=5 * count_ka * key_tiles * TILE * TILE * width, bytes_accessed=1 << 20, transcendentals=0
            ),
            name=("attention_first", "attention_leaving", "attention_other", "attention_own")[stage],
        )(table, *operands)

    dq_sums = jax.ShapeDtypeStruct((count_ka, HEAD_DIM, width), F32)
    dq_tile = jax.ShapeDtypeStruct((HEAD_DIM, width), BF16)
    state = [key_shape] * 3 + [sum_shape] * 2
    dq_sum, *own = attend(0, [dq_sums] + state, [], key_gain, value_gain, own_queries, own_stats, *blocks)
    dq_sum, *other = attend(
        1, [dq_sums] + [dq_tile] * EARLY + state, [],
        key_gain, value_gain, own_queries, own_stats, *other_blocks, dq_sum,
    )
    dq_parts = [None] * count_ka
    for step, tile in zip(early, other):
        dq_parts[step] = turn(tile, step)
    other = other[EARLY:]
    dq_sum, *own[3:], kv_other = attend(
        2, [dq_sums] + [sum_shape] * 2 + [jax.ShapeDtypeStruct((key_tiles * TILE, 2 * HEAD_DIM), BF16)],
        [VMEM(sum_shape.shape, F32)] * 2,
        own_queries, own_stats, dq_sum, *own, *other,
    )
    kv_back = swap(kv_other, 1)
    *dq_late, key_sum, value_sum = attend(
        3, [dq_tile] * len(late) + [sum_shape] * 2, [VMEM(dq_sums.shape, F32)],
        own_queries, own_stats, dq_sum, *own,
    )
    kv_own = pl.pallas_call(
        functools.partial(merge_kernel, (count_chip, count_ka)),
        in_specs=in_vmem(3 + count_chip),
        out_specs=in_vmem(count_chip),
        out_shape=[jax.ShapeDtypeStruct(kv_shape, BF16 if number else F32) for number in range(count_chip)],
        compiler_params=params(16 + key_tiles // 4),
        name="merge",
    )(key_sum, value_sum, kv_back, *blocks)
    kv_parts = [kv_own[0]] + [swap(kv_own[number], 2 * number) for number in range(1, count_chip)]
    dq_late, dq_parts[half], dq_parts[1] = lax.optimization_barrier((dq_late, dq_parts[half], dq_parts[1]))
    for step, tile in zip(late, dq_late):
        dq_parts[step] = turn(tile, step) if step else tile

    piece_type = BF16 if share == 1 else F32
    piece_shape = (TILE + SPARE, 2 * HEAD_DIM)
    pieces = list(pl.pallas_call(
        functools.partial(collect_kernel, (count_chip, count_ka, share)),
        in_specs=in_vmem(2 + count_chip),
        out_specs=in_vmem(count_ka),
        out_shape=[jax.ShapeDtypeStruct(piece_shape, piece_type if step else F32) for step in range(count_ka)],
        compiler_params=params(24),
        name="collect",
    )(key_gain, value_gain, *kv_parts))
    pieces = [pieces[0]] + [turn(piece, -step) for step, piece in enumerate(pieces[1:], 1)]
    grad_queries = pl.pallas_call(
        functools.partial(place_kernel, (count_ka, order)),
        in_specs=in_vmem(count_ka),
        out_specs=anywhere(1)[0],
        out_shape=jax.ShapeDtypeStruct((rows_dev, feat_width), BF16),
        scratch_shapes=[VMEM((count_ka, TILE, width), BF16), pltpu.SemaphoreType.DMA((count_ka,))],
        compiler_params=params(16),
        cost_estimate=pl.CostEstimate(flops=0, bytes_accessed=4 * rows_dev * feat_width, transcendentals=0),
        name="place_queries",
    )(*[dq_parts[step] for step in order])
    pieces, grad_queries = lax.optimization_barrier((pieces, grad_queries))
    grad_keys, grad_values, gains = pl.pallas_call(
        functools.partial(finish_kernel, (count_ka, share)),
        in_specs=in_vmem(2 + count_ka),
        out_specs=in_vmem(3),
        out_shape=[
            jax.ShapeDtypeStruct(key_rows.shape, BF16),
            jax.ShapeDtypeStruct(key_rows.shape, BF16),
            jax.ShapeDtypeStruct((2, key_rows.shape[1]), F32),
        ],
        scratch_shapes=[VMEM((kv_heads, TILE + SPARE, 2 * HEAD_DIM), F32)],
        compiler_params=params(16),
        name="finish",
    )(key_gain, value_gain, *pieces)
    grad_key_gain, grad_value_gain = pl.pallas_call(
        gains_kernel,
        in_specs=in_vmem(2),
        out_specs=in_vmem(2),
        out_shape=[jax.ShapeDtypeStruct(key_gain.shape, F32)] * 2,
        compiler_params=params(4),
        name="add_gains",
    )(gains, swap(gains, 1))
    return grad_queries, grad_keys, grad_values, grad_key_gain.reshape(-1), grad_value_gain.reshape(-1)


def solution(mesh):
    placed = (
        P("pb", None),
        P(("pb", "ka"), None),
        P(("pb", "ka"), None),
        P(("pb", "ka"), None),
        P("pb", None),
        P(None, ("pb", "ka")),
        P(),
        P(),
        P(),
        P(),
        P(),
    )
    return jax.shard_map(
        shards,
        mesh=mesh,
        in_specs=placed,
        out_specs=(P(("pb", "ka"), None), P(("pb", "ka"), None), P(("pb", "ka"), None), P(), P()),
        check_vma=False,
    )
```

profile of v0, /device:TPU:0, one launch (start us, length us, event | category | flops | bytes accessed | tf_op | source)
XLA Modules:
  0.0 80.9 jit_solution(9444828836723022904)
XLA Ops:
  0.6 2.8 %prepare.1 = (bf16[144,256]{1,0:T(8,128)(2,1)}, bf16[144,256]{1,0:T(8,128)(2,1)}, bf16[144,256]{1,0:T(8,128)(2,1)}, bf16[144,256]{1,0:T(8,128)(2,1)}) custom-call(bf16[128,512]{1,0:T(8,128)(2,1)} %key_ref.1, bf16[128,512]{1,0:T(8,128)(2,1)} %value_ref.1, bf16[128,4096]{1,0:T(8,128)(2,1)} %attn_ref.1, bf16[512,4096]{1,0:T(8,128)(2,1)} %grads_ref.3, ...), custom_call_target="tpu_custom_call" | custom-call | tf_op jit(solution)/shard_map/prepare/pallas_call | solution.py:465
  3.4 3.1 %collective-permute-start = (bf16[144,256]{1,0:T(8,128)(2,1)}, bf16[144,256]{1,0:T(8,128)(2,1)S(1)}, u32[]{:S(2)}, u32[]{:S(2)}) collective-permute-start(bf16[144,256]{1,0:T(8,128)(2,1)} %get-tuple-element.61), channel_id=1, source_target_pairs={{0,1},{1,2},{2,3},{3,0},{4,5},{5,6},{6,7},{7,4},{8,9},{9,10},{10,1... | collective-permute-start | bytes 221192 | tf_op jit(solution)/shard_map/ppermute | solution.py:463
  6.5 2.6 %collective-permute-start.1 = (bf16[144,256]{1,0:T(8,128)(2,1)}, bf16[144,256]{1,0:T(8,128)(2,1)S(1)}, u32[]{:S(2)}, u32[]{:S(2)}) collective-permute-start(bf16[144,256]{1,0:T(8,128)(2,1)} %get-tuple-element.62), channel_id=1, source_target_pairs={{0,2},{1,3},{2,0},{3,1},{4,6},{5,7},{6,4},{7,5},{8,10},{9,11},{10,... | collective-permute-start | bytes 221192 | tf_op jit(solution)/shard_map/ppermute | solution.py:463
  9.1 1.3 %collective-permute-start.2 = (bf16[144,256]{1,0:T(8,128)(2,1)}, bf16[144,256]{1,0:T(8,128)(2,1)S(1)}, u32[]{:S(2)}, u32[]{:S(2)}) collective-permute-start(bf16[144,256]{1,0:T(8,128)(2,1)} %get-tuple-element.63), channel_id=1, source_target_pairs={{0,3},{1,0},{2,1},{3,2},{4,7},{5,4},{6,5},{7,6},{8,11},{9,8},{10,9... | collective-permute-start | bytes 221192 | tf_op jit(solution)/shard_map/ppermute | solution.py:463
  10.4 0.0 copy-start.3
  10.4 0.0 copy-start
  10.4 0.0 copy-start.1
  10.5 1.6 %own_heads.1.rest_3_.rest_1_ = bf16[2,512,1024]{2,1,0:T(8,128)(2,1)S(1)} custom-call(bf16[512,4096]{1,0:T(8,128)(2,1)} %queries_ref, bf16[512,4096]{1,0:T(8,128)(2,1)} %grads_ref.3), custom_call_target="tpu_custom_call" | custom-call | bytes 4194304 | tf_op jit(solution)/shard_map/own_heads/pallas_call | solution.py:480
  12.1 0.0 collective-permute-done
  12.1 2.2 %collective-permute-done.1 = bf16[144,256]{1,0:T(8,128)(2,1)S(1)} collective-permute-done((bf16[144,256]{1,0:T(8,128)(2,1)}, bf16[144,256]{1,0:T(8,128)(2,1)S(1)}, u32[]{:S(2)}, u32[]{:S(2)}) %collective-permute-start.1) | collective-permute-done | bytes 73760 | tf_op jit(solution)/shard_map/ppermute | solution.py:463
  14.3 0.2 collective-permute-done.2
  14.5 0.0 copy-done.3
  14.6 2.5 %collective-permute-start.8 = (bf16[512,256]{1,0:T(8,128)(2,1)S(1)}, bf16[512,256]{1,0:T(8,128)(2,1)S(1)}, u32[]{:S(2)}, u32[]{:S(2)}) collective-permute-start(bf16[512,256]{1,0:T(8,128)(2,1)S(1)} %pad_maximum_fusion.rest_5_.rest_0_), channel_id=1, source_target_pairs={{0,24},{4,28},{8,16},{12,20},{16,8},{20,12},{24,0},{28,4},{1,25},{... | collective-permute-start | bytes 786440 | tf_op jit(solution)/shard_map/ppermute | solution.py:460
  17.1 0.5 collective-permute-start.6
  17.6 0.5 collective-permute-start.4
  18.1 0.1 collective-permute-start.3
  18.2 3.7 %plan.1.rest_0_ = s32[528]{0:T(1024)} custom-call(s32[32]{0:T(128)} %order_ref, s32[32]{0:T(128)} %doc_ref.1, s32[32,32]{1,0:T(8,128)} %mask_ref.1), custom_call_target="tpu_custom_call" | custom-call | bytes 4194304 | tf_op jit(solution)/shard_map/plan/pallas_call | solution.py:506
  22.0 2.8 %collective-permute-done.8.rest_8_.rest_3_ = bf16[512,256]{1,0:T(8,128)(2,1)S(1)} collective-permute-done((bf16[512,256]{1,0:T(8,128)(2,1)S(1)}, bf16[512,256]{1,0:T(8,128)(2,1)S(1)}, u32[]{:S(2)}, u32[]{:S(2)}) %collective-permute-start.8) | collective-permute-done | bytes 262176 | tf_op jit(solution)/shard_map/ppermute | solution.py:460
  24.8 0.0 collective-permute-start.9
  24.8 4.3 %collective-permute-done.6.rest_7_.rest_2_ = bf16[512,256]{1,0:T(8,128)(2,1)S(1)} collective-permute-done((bf16[512,256]{1,0:T(8,128)(2,1)S(1)}, bf16[512,256]{1,0:T(8,128)(2,1)S(1)}, u32[]{:S(2)}, u32[]{:S(2)}) %collective-permute-start.6) | collective-permute-done | bytes 262176 | tf_op jit(solution)/shard_map/ppermute | solution.py:460
  29.1 0.0 collective-permute-start.7
  29.1 0.0 collective-permute-done.4.rest_6_.rest_1_
  29.1 0.5 collective-permute-start.5
  29.6 0.0 copy-done
  29.6 0.0 copy-done.1
  29.6 0.0 copy-start.2
  29.6 0.7 copy-done.2
  30.3 4.1 %attention_first.1 = (f32[4,128,1024]{2,1,0:T(8,128)S(1)}, bf16[16,128,128]{2,1,0:T(8,128)(2,1)S(1)}, bf16[16,128,128]{2,1,0:T(8,128)(2,1)S(1)}, bf16[16,128,128...) custom-call(s32[528]{0:T(1024)S(1)} %copy-done.2, f32[1,512]{1,0:T(1,128)S(1)} %bitcast.4, ...), custom_call_target="tpu_custom_call" | custom-call | flops 5368709120 | bytes 1048576 | tf_op jit(solution)/shard_map/attention_first/pallas_call | solution.py:516
  34.4 0.0 collective-permute-done.3.rest_5_
  34.4 0.0 collective-permute-done.9.rest_8_
  34.4 0.0 collective-permute-done.7.rest_7_
  34.4 0.0 collective-permute-done.5.rest_6_
  34.4 6.2 %attention_leaving.1 = (f32[4,128,1024]{2,1,0:T(8,128)S(1)}, bf16[128,1024]{1,0:T(8,128)(2,1)S(1)}, bf16[128,1024]{1,0:T(8,128)(2,1)S(1)}, bf16[16,128,128]{2,1,...) custom-call(s32[528]{0:T(1024)S(1)} %copy-done.2, ...), custom_call_target="tpu_custom_call" | custom-call | flops 5368709120 | bytes 1048576 | tf_op jit(solution)/shard_map/attention_leaving/pallas_call | solution.py:516
  40.6 1.2 %attention_other.1 = (f32[4,128,1024]{2,1,0:T(8,128)S(1)}, f32[16,128,128]{2,1,0:T(8,128)S(1)}, f32[16,128,128]{2,1,0:T(8,128)S(1)}, bf16[2048,256]{1,0:T(8,128)(2,1)S(1)}) custom-call(s32[528]{0:T(1024)S(1)} %copy-done.2, bf16[2,512,1024]{2,1,0:T(8,128)(2,1)S(1)} %own_heads.1.rest_3_.rest_1_, bf16[64,256]{1,0:T(8,128)(2,1)S(1)} %pad_maximum_fusion.1.rest_4_.rest_2_, ...), custom_call_target="tpu_custom_call" | custom-call | flops 5368709120 | bytes 1048576 | tf_op jit(solution)/shard_map/attention_other/pallas_call | solution.py:516
  41.8 0.1 collective-permute-start.10
  41.9 5.2 %collective-permute-start.17 = (bf16[128,1024]{1,0:T(8,128)(2,1)S(1)}, bf16[128,1024]{1,0:T(8,128)(2,1)S(1)}, u32[]{:S(2)}, u32[]{:S(2)}) collective-permute-start(bf16[128,1024]{1,0:T(8,128)(2,1)S(1)} %get-tuple-element.99), channel_id=1, source_target_pairs={{0,2},{1,3},{2,0},{3,1},{4,6},{5,7},{6,4},{7,5},{8,10},{9,11},{10,... | collective-permute-start | bytes 786440 | tf_op jit(solution)/shard_map/ppermute | solution.py:463
  47.1 0.2 collective-permute-start.18
  47.3 1.9 %attention_own.1 = (bf16[128,1024]{1,0:T(8,128)(2,1)S(1)}, bf16[128,1024]{1,0:T(8,128)(2,1)S(1)}, f32[16,128,128]{2,1,0:T(8,128)S(1)}, f32[16,128,128]{2,1,0:T(8,128)S(1)}) custom-call(s32[528]{0:T(1024)S(1)} %copy-done.2, bf16[2,512,1024]{2,1,0:T(8,128)(2,1)S(1)} %own_heads.1.rest_3_.rest_1_, bf16[64,256]{1,0:T(8,128)(2,1)S(1)} %pad_maximum_fusion.1.rest_4_.rest_2_, ...), custom_call_target="tpu_custom_call" | custom-call | flops 5368709120 | bytes 1048576 | tf_op jit(solution)/shard_map/attention_own/pallas_call | solution.py:516
  49.2 0.0 collective-permute-done.10.kv_back
  49.2 0.5 merge.1
  49.7 1.7 %collective-permute-start.11 = (bf16[528,256]{1,0:T(8,128)(2,1)S(1)}, bf16[528,256]{1,0:T(8,128)(2,1)S(1)}, u32[]{:S(2)}, u32[]{:S(2)}) collective-permute-start(bf16[528,256]{1,0:T(8,128)(2,1)S(1)} %get-tuple-element.90), channel_id=1, source_target_pairs={{0,8},{4,12},{8,0},{12,4},{16,24},{20,28},{24,16},{28,20},{1,9},{5... | collective-permute-start | bytes 811016 | tf_op jit(solution)/shard_map/ppermute | solution.py:460
  51.4 2.6 %collective-permute-start.12 = (bf16[528,256]{1,0:T(8,128)(2,1)S(1)}, bf16[528,256]{1,0:T(8,128)(2,1)S(1)}, u32[]{:S(2)}, u32[]{:S(2)}) collective-permute-start(bf16[528,256]{1,0:T(8,128)(2,1)S(1)} %get-tuple-element.91), channel_id=1, source_target_pairs={{0,16},{4,20},{8,24},{12,28},{16,0},{20,4},{24,8},{28,12},{1,17},{... | collective-permute-start | bytes 811016 | tf_op jit(solution)/shard_map/ppermute | solution.py:460
  54.0 0.0 collective-permute-start.13
  54.0 10.9 %collective-permute-done.17.rest_0_ = bf16[128,1024]{1,0:T(8,128)(2,1)S(1)} collective-permute-done((bf16[128,1024]{1,0:T(8,128)(2,1)S(1)}, bf16[128,1024]{1,0:T(8,128)(2,1)S(1)}, u32[]{:S(2)}, u32[]{:S(2)}) %collective-permute-start.17) | collective-permute-done | bytes 262176 | tf_op jit(solution)/shard_map/ppermute | solution.py:463
  64.9 0.0 collective-permute-done.18.rest_1_
  64.9 0.0 collective-permute-start.19
  64.9 0.0 collective-permute-done.11.rest_1_
  64.9 1.5 %collective-permute-done.12.rest_2_ = bf16[528,256]{1,0:T(8,128)(2,1)S(1)} collective-permute-done((bf16[528,256]{1,0:T(8,128)(2,1)S(1)}, bf16[528,256]{1,0:T(8,128)(2,1)S(1)}, u32[]{:S(2)}, u32[]{:S(2)}) %collective-permute-start.12) | collective-permute-done | bytes 270368 | tf_op jit(solution)/shard_map/ppermute | solution.py:460
  66.4 0.0 collective-permute-done.13.rest_3_
  66.4 0.1 collect.1
  66.5 3.8 %collective-permute-start.14 = (bf16[144,256]{1,0:T(8,128)(2,1)S(1)}, bf16[144,256]{1,0:T(8,128)(2,1)S(1)}, u32[]{:S(2)}, u32[]{:S(2)}) collective-permute-start(bf16[144,256]{1,0:T(8,128)(2,1)S(1)} %get-tuple-element.94), channel_id=1, source_target_pairs={{0,3},{1,0},{2,1},{3,2},{4,7},{5,4},{6,5},{7,6},{8,11},{9,8},{10,9... | collective-permute-start | bytes 221192 | tf_op jit(solution)/shard_map/ppermute | solution.py:463
  70.3 0.9 %collective-permute-start.15 = (bf16[144,256]{1,0:T(8,128)(2,1)S(1)}, bf16[144,256]{1,0:T(8,128)(2,1)S(1)}, u32[]{:S(2)}, u32[]{:S(2)}) collective-permute-start(bf16[144,256]{1,0:T(8,128)(2,1)S(1)} %get-tuple-element.95), channel_id=1, source_target_pairs={{0,2},{1,3},{2,0},{3,1},{4,6},{5,7},{6,4},{7,5},{8,10},{9,11},{10,... | collective-permute-start | bytes 221192 | tf_op jit(solution)/shard_map/ppermute | solution.py:463
  71.3 1.9 %collective-permute-start.16 = (bf16[144,256]{1,0:T(8,128)(2,1)S(1)}, bf16[144,256]{1,0:T(8,128)(2,1)S(1)}, u32[]{:S(2)}, u32[]{:S(2)}) collective-permute-start(bf16[144,256]{1,0:T(8,128)(2,1)S(1)} %get-tuple-element.96), channel_id=1, source_target_pairs={{0,1},{1,2},{2,3},{3,0},{4,5},{5,6},{6,7},{7,4},{8,9},{9,10},{10,1... | collective-permute-start | bytes 221192 | tf_op jit(solution)/shard_map/ppermute | solution.py:463
  73.2 1.0 %collective-permute-done.19.rest_3_ = bf16[128,1024]{1,0:T(8,128)(2,1)S(1)} collective-permute-done((bf16[128,1024]{1,0:T(8,128)(2,1)S(1)}, bf16[128,1024]{1,0:T(8,128)(2,1)S(1)}, u32[]{:S(2)}, u32[]{:S(2)}) %collective-permute-start.19) | collective-permute-done | bytes 262176 | tf_op jit(solution)/shard_map/ppermute | solution.py:463
  74.2 1.1 %place_queries.1 = bf16[128,4096]{1,0:T(8,128)(2,1)} custom-call(bf16[128,1024]{1,0:T(8,128)(2,1)S(1)} %collective-permute-done.17.rest_0_, bf16[128,1024]{1,0:T(8,128)(2,1)S(1)} %collective-permute-done.18.rest_1_, bf16[128,1024]{1,0:T(8,128)(2,1)S(1)} %get-tuple-element.103.rest_2_, bf16[128,1024]{1,0:T(8,128)(2,1)S(1)} %collective-permute-done.19.rest_3_), custom_call_target="tpu_custom_call" | custom-call | bytes 2097152 | tf_op jit(solution)/shard_map/place_queries/pallas_call | solution.py:579
  75.4 0.2 collective-permute-done.14.rest_1_
  75.5 2.8 %collective-permute-done.15.rest_2_ = bf16[144,256]{1,0:T(8,128)(2,1)S(1)} collective-permute-done((bf16[144,256]{1,0:T(8,128)(2,1)S(1)}, bf16[144,256]{1,0:T(8,128)(2,1)S(1)}, u32[]{:S(2)}, u32[]{:S(2)}) %collective-permute-start.15) | collective-permute-done | bytes 73760 | tf_op jit(solution)/shard_map/ppermute | solution.py:463
  78.3 0.0 collective-permute-done.16.rest_3_
  78.3 0.8 %finish.1 = (bf16[128,512]{1,0:T(8,128)(2,1)}, bf16[128,512]{1,0:T(8,128)(2,1)}, f32[2,512]{1,0:T(2,128)S(1)}) custom-call(f32[1,512]{1,0:T(1,128)S(1)} %bitcast.7, f32[1,512]{1,0:T(1,128)S(1)} %bitcast.11, f32[144,256]{1,0:T(8,128)S(1)} %get-tuple-element.106.rest_0_, bf16[144,256]{1,0:T(8,128)(2,1)S(1)} %collective-permute-done.14.rest_1_, ...), custom_call_target="tpu_custom_call" | custom-call | tf_op jit(solution)/shard_map/finish/pallas_call | solution.py:590
  79.1 0.0 collective-permute-start.20
  79.1 1.2 %collective-permute-done.20.other_ref = f32[2,512]{1,0:T(2,128)S(1)} collective-permute-done((f32[2,512]{1,0:T(2,128)S(1)}, f32[2,512]{1,0:T(2,128)S(1)}, u32[]{:S(2)}, u32[]{:S(2)}) %collective-permute-start.20) | collective-permute-done | bytes 4128 | tf_op jit(solution)/shard_map/ppermute | solution.py:460
  80.3 0.6 add_gains.1
  (10 shorter events, 0.1 us)
Async XLA Ops:
  3.4 8.6 %collective-permute-start = (bf16[144,256]{1,0:T(8,128)(2,1)}, bf16[144,256]{1,0:T(8,128)(2,1)S(1)}, u32[]{:S(2)}, u32[]{:S(2)}) collective-permute-start(bf16[144,256]{1,0:T(8,128)(2,1)} %get-tuple-element.61), channel_id=1, source_target_pairs={{0,1},{1,2},{2,3},{3,0},{4,5},{5,6},{6,7},{7,4},{8,9},{9,10},{10,1... | collective-permute-start | bytes 221192 | tf_op jit(solution)/shard_map/ppermute | solution.py:463
  6.5 7.8 %collective-permute-start.1 = (bf16[144,256]{1,0:T(8,128)(2,1)}, bf16[144,256]{1,0:T(8,128)(2,1)S(1)}, u32[]{:S(2)}, u32[]{:S(2)}) collective-permute-start(bf16[144,256]{1,0:T(8,128)(2,1)} %get-tuple-element.62), channel_id=1, source_target_pairs={{0,2},{1,3},{2,0},{3,1},{4,6},{5,7},{6,4},{7,5},{8,10},{9,11},{10,... | collective-permute-start | bytes 221192 | tf_op jit(solution)/shard_map/ppermute | solution.py:463
  9.1 5.4 %collective-permute-start.2 = (bf16[144,256]{1,0:T(8,128)(2,1)}, bf16[144,256]{1,0:T(8,128)(2,1)S(1)}, u32[]{:S(2)}, u32[]{:S(2)}) collective-permute-start(bf16[144,256]{1,0:T(8,128)(2,1)} %get-tuple-element.63), channel_id=1, source_target_pairs={{0,3},{1,0},{2,1},{3,2},{4,7},{5,4},{6,5},{7,6},{8,11},{9,8},{10,9... | collective-permute-start | bytes 221192 | tf_op jit(solution)/shard_map/ppermute | solution.py:463
  10.4 4.0 %copy-start.3 = (bf16[144,256]{1,0:T(8,128)(2,1)S(1)}, bf16[144,256]{1,0:T(8,128)(2,1)}, u32[]{:S(2)}) copy-start(bf16[144,256]{1,0:T(8,128)(2,1)} %get-tuple-element.65) | copy-start | bytes 221188
  10.4 19.1 %copy-start = (f32[512]{0:T(512)S(1)}, f32[512]{0:T(512)}, u32[]{:S(2)}) copy-start(f32[512]{0:T(512)} %param.17) | copy-start | bytes 6148
  10.4 19.1 %copy-start.1 = (f32[512]{0:T(512)S(1)}, f32[512]{0:T(512)}, u32[]{:S(2)}) copy-start(f32[512]{0:T(512)} %param.18) | copy-start | bytes 6148
  14.6 10.2 %collective-permute-start.8 = (bf16[512,256]{1,0:T(8,128)(2,1)S(1)}, bf16[512,256]{1,0:T(8,128)(2,1)S(1)}, u32[]{:S(2)}, u32[]{:S(2)}) collective-permute-start(bf16[512,256]{1,0:T(8,128)(2,1)S(1)} %pad_maximum_fusion.rest_5_.rest_0_), channel_id=1, source_target_pairs={{0,24},{4,28},{8,16},{12,20},{16,8},{20,12},{24,0},{28,4},{1,25},{... | collective-permute-start | bytes 786440 | tf_op jit(solution)/shard_map/ppermute | solution.py:460
  17.1 12.0 %collective-permute-start.6 = (bf16[512,256]{1,0:T(8,128)(2,1)S(1)}, bf16[512,256]{1,0:T(8,128)(2,1)S(1)}, u32[]{:S(2)}, u32[]{:S(2)}) collective-permute-start(bf16[512,256]{1,0:T(8,128)(2,1)S(1)} %pad_maximum_fusion.rest_5_.rest_0_), channel_id=1, source_target_pairs={{0,16},{4,20},{8,24},{12,28},{16,0},{20,4},{24,8},{28,12},{1,17},{... | collective-permute-start | bytes 786440 | tf_op jit(solution)/shard_map/ppermute | solution.py:460
  17.6 11.5 %collective-permute-start.4 = (bf16[512,256]{1,0:T(8,128)(2,1)S(1)}, bf16[512,256]{1,0:T(8,128)(2,1)S(1)}, u32[]{:S(2)}, u32[]{:S(2)}) collective-permute-start(bf16[512,256]{1,0:T(8,128)(2,1)S(1)} %pad_maximum_fusion.rest_5_.rest_0_), channel_id=1, source_target_pairs={{0,8},{4,12},{8,0},{12,4},{16,24},{20,28},{24,16},{28,20},{1,9},{5... | collective-permute-start | bytes 786440 | tf_op jit(solution)/shard_map/ppermute | solution.py:460
  18.1 16.3 %collective-permute-start.3 = (bf16[512,256]{1,0:T(8,128)(2,1)S(1)}, bf16[512,256]{1,0:T(8,128)(2,1)S(1)}, u32[]{:S(2)}, u32[]{:S(2)}) collective-permute-start(bf16[512,256]{1,0:T(8,128)(2,1)S(1)} %pad_maximum_fusion.rest_5_.rest_0_), channel_id=1, source_target_pairs={{0,4},{4,0},{8,12},{12,8},{16,20},{20,16},{24,28},{28,24},{1,5},{5... | collective-permute-start | bytes 786440 | tf_op jit(solution)/shard_map/ppermute | solution.py:460
  24.8 9.6 %collective-permute-start.9 = (bf16[512,256]{1,0:T(8,128)(2,1)S(1)}, bf16[512,256]{1,0:T(8,128)(2,1)S(1)}, u32[]{:S(2)}, u32[]{:S(2)}) collective-permute-start(bf16[512,256]{1,0:T(8,128)(2,1)S(1)} %collective-permute-done.8.rest_8_.rest_3_), channel_id=1, source_target_pairs={{0,4},{4,0},{8,12},{12,8},{16,20},{20,16},{24,28},{28,24},{1,5},{5... | collective-permute-start | bytes 786440 | tf_op jit(solution)/shard_map/ppermute | solution.py:460
  29.1 5.4 %collective-permute-start.7 = (bf16[512,256]{1,0:T(8,128)(2,1)S(1)}, bf16[512,256]{1,0:T(8,128)(2,1)S(1)}, u32[]{:S(2)}, u32[]{:S(2)}) collective-permute-start(bf16[512,256]{1,0:T(8,128)(2,1)S(1)} %collective-permute-done.6.rest_7_.rest_2_), channel_id=1, source_target_pairs={{0,4},{4,0},{8,12},{12,8},{16,20},{20,16},{24,28},{28,24},{1,5},{5... | collective-permute-start | bytes 786440 | tf_op jit(solution)/shard_map/ppermute | solution.py:460
  29.1 5.3 %collective-permute-start.5 = (bf16[512,256]{1,0:T(8,128)(2,1)S(1)}, bf16[512,256]{1,0:T(8,128)(2,1)S(1)}, u32[]{:S(2)}, u32[]{:S(2)}) collective-permute-start(bf16[512,256]{1,0:T(8,128)(2,1)S(1)} %collective-permute-done.4.rest_6_.rest_1_), channel_id=1, source_target_pairs={{0,4},{4,0},{8,12},{12,8},{16,20},{20,16},{24,28},{28,24},{1,5},{5... | collective-permute-start | bytes 786440 | tf_op jit(solution)/shard_map/ppermute | solution.py:460
  29.6 0.7 copy-start.2
  41.8 7.4 %collective-permute-start.10 = (bf16[2048,256]{1,0:T(8,128)(2,1)S(1)}, bf16[2048,256]{1,0:T(8,128)(2,1)S(1)}, u32[]{:S(2)}, u32[]{:S(2)}) collective-permute-start(bf16[2048,256]{1,0:T(8,128)(2,1)S(1)} %get-tuple-element.88), channel_id=1, source_target_pairs={{0,4},{4,0},{8,12},{12,8},{16,20},{20,16},{24,28},{28,24},{1,5},{5... | collective-permute-start | bytes 3145736 | tf_op jit(solution)/shard_map/ppermute | solution.py:460
  41.9 22.9 %collective-permute-start.17 = (bf16[128,1024]{1,0:T(8,128)(2,1)S(1)}, bf16[128,1024]{1,0:T(8,128)(2,1)S(1)}, u32[]{:S(2)}, u32[]{:S(2)}) collective-permute-start(bf16[128,1024]{1,0:T(8,128)(2,1)S(1)} %get-tuple-element.99), channel_id=1, source_target_pairs={{0,2},{1,3},{2,0},{3,1},{4,6},{5,7},{6,4},{7,5},{8,10},{9,11},{10,... | collective-permute-start | bytes 786440 | tf_op jit(solution)/shard_map/ppermute | solution.py:463
  47.1 17.8 %collective-permute-start.18 = (bf16[128,1024]{1,0:T(8,128)(2,1)S(1)}, bf16[128,1024]{1,0:T(8,128)(2,1)S(1)}, u32[]{:S(2)}, u32[]{:S(2)}) collective-permute-start(bf16[128,1024]{1,0:T(8,128)(2,1)S(1)} %get-tuple-element.100), channel_id=1, source_target_pairs={{0,1},{1,2},{2,3},{3,0},{4,5},{5,6},{6,7},{7,4},{8,9},{9,10},{10,1... | collective-permute-start | bytes 786440 | tf_op jit(solution)/shard_map/ppermute | solution.py:463
  49.7 15.2 %collective-permute-start.11 = (bf16[528,256]{1,0:T(8,128)(2,1)S(1)}, bf16[528,256]{1,0:T(8,128)(2,1)S(1)}, u32[]{:S(2)}, u32[]{:S(2)}) collective-permute-start(bf16[528,256]{1,0:T(8,128)(2,1)S(1)} %get-tuple-element.90), channel_id=1, source_target_pairs={{0,8},{4,12},{8,0},{12,4},{16,24},{20,28},{24,16},{28,20},{1,9},{5... | collective-permute-start | bytes 811016 | tf_op jit(solution)/shard_map/ppermute | solution.py:460
  51.4 15.0 %collective-permute-start.12 = (bf16[528,256]{1,0:T(8,128)(2,1)S(1)}, bf16[528,256]{1,0:T(8,128)(2,1)S(1)}, u32[]{:S(2)}, u32[]{:S(2)}) collective-permute-start(bf16[528,256]{1,0:T(8,128)(2,1)S(1)} %get-tuple-element.91), channel_id=1, source_target_pairs={{0,16},{4,20},{8,24},{12,28},{16,0},{20,4},{24,8},{28,12},{1,17},{... | collective-permute-start | bytes 811016 | tf_op jit(solution)/shard_map/ppermute | solution.py:460
  54.0 12.4 %collective-permute-start.13 = (bf16[528,256]{1,0:T(8,128)(2,1)S(1)}, bf16[528,256]{1,0:T(8,128)(2,1)S(1)}, u32[]{:S(2)}, u32[]{:S(2)}) collective-permute-start(bf16[528,256]{1,0:T(8,128)(2,1)S(1)} %get-tuple-element.92), channel_id=1, source_target_pairs={{0,24},{4,28},{8,16},{12,20},{16,8},{20,12},{24,0},{28,4},{1,25},{... | collective-permute-start | bytes 811016 | tf_op jit(solution)/shard_map/ppermute | solution.py:460
  64.9 9.3 %collective-permute-start.19 = (bf16[128,1024]{1,0:T(8,128)(2,1)S(1)}, bf16[128,1024]{1,0:T(8,128)(2,1)S(1)}, u32[]{:S(2)}, u32[]{:S(2)}) collective-permute-start(bf16[128,1024]{1,0:T(8,128)(2,1)S(1)} %get-tuple-element.104), channel_id=1, source_target_pairs={{0,3},{1,0},{2,1},{3,2},{4,7},{5,4},{6,5},{7,6},{8,11},{9,8},{10,9... | collective-permute-start | bytes 786440 | tf_op jit(solution)/shard_map/ppermute | solution.py:463
  66.5 9.0 %collective-permute-start.14 = (bf16[144,256]{1,0:T(8,128)(2,1)S(1)}, bf16[144,256]{1,0:T(8,128)(2,1)S(1)}, u32[]{:S(2)}, u32[]{:S(2)}) collective-permute-start(bf16[144,256]{1,0:T(8,128)(2,1)S(1)} %get-tuple-element.94), channel_id=1, source_target_pairs={{0,3},{1,0},{2,1},{3,2},{4,7},{5,4},{6,5},{7,6},{8,11},{9,8},{10,9... | collective-permute-start | bytes 221192 | tf_op jit(solution)/shard_map/ppermute | solution.py:463
  70.3 8.0 %collective-permute-start.15 = (bf16[144,256]{1,0:T(8,128)(2,1)S(1)}, bf16[144,256]{1,0:T(8,128)(2,1)S(1)}, u32[]{:S(2)}, u32[]{:S(2)}) collective-permute-start(bf16[144,256]{1,0:T(8,128)(2,1)S(1)} %get-tuple-element.95), channel_id=1, source_target_pairs={{0,2},{1,3},{2,0},{3,1},{4,6},{5,7},{6,4},{7,5},{8,10},{9,11},{10,... | collective-permute-start | bytes 221192 | tf_op jit(solution)/shard_map/ppermute | solution.py:463
  71.3 7.0 %collective-permute-start.16 = (bf16[144,256]{1,0:T(8,128)(2,1)S(1)}, bf16[144,256]{1,0:T(8,128)(2,1)S(1)}, u32[]{:S(2)}, u32[]{:S(2)}) collective-permute-start(bf16[144,256]{1,0:T(8,128)(2,1)S(1)} %get-tuple-element.96), channel_id=1, source_target_pairs={{0,1},{1,2},{2,3},{3,0},{4,5},{5,6},{6,7},{7,4},{8,9},{9,10},{10,1... | collective-permute-start | bytes 221192 | tf_op jit(solution)/shard_map/ppermute | solution.py:463
  79.1 1.2 %collective-permute-start.20 = (f32[2,512]{1,0:T(2,128)S(1)}, f32[2,512]{1,0:T(2,128)S(1)}, u32[]{:S(2)}, u32[]{:S(2)}) collective-permute-start(f32[2,512]{1,0:T(2,128)S(1)} %get-tuple-element.112.gains_ref), channel_id=1, source_target_pairs={{0,4},{4,0},{8,12},{12,8},{16,20},{20,16},{24,28},{28,24},{1,5},{5... | collective-permute-start | bytes 12296 | tf_op jit(solution)/shard_map/ppermute | solution.py:460
where the time goes:
time: 81.3 us; the launch traced here: 80.9 us
  starting transfers between devices  27.6 us (34%)
  waiting for transfers between devices  27 us (33%)
  Pallas kernels  24.7 us (30%)
  between operations  0.83 us (1%)
    ppermute x9, starting transfers between devices, turn(): lax.ppermute(array, 'ka', [(at, (at + step) % count_ka) for at in range(c...  19.1 us
    ppermute x9, waiting for transfers between devices, turn(): lax.ppermute(array, 'ka', [(at, (at + step) % count_ka) for at in range(c...  17.3 us
    pallas_call x4, Pallas kernels, attend(): pl.pallas_call(functools.partial(attention_kernel, (count_chip, count_ka,...  13.4 us
    ppermute x12, waiting for transfers between devices, swap(): lax.ppermute(array, 'pb', [(at, at ^ number) for at in range(count_pb)])  9.74 us
    ppermute x12, starting transfers between devices, swap(): lax.ppermute(array, 'pb', [(at, at ^ number) for at in range(count_pb)])  8.52 us
    pallas_call x1, Pallas kernels, shards(): pl.pallas_call(functools.partial(plan_kernel, (count_chip, count_ka, orde...  3.73 us
    pallas_call x1, Pallas kernels, shards(): pl.pallas_call(functools.partial(prepare_kernel, (count_ka, heads, heads_...  2.79 us
  transfers between devices with their start and end apart: 21, of which 10 were waited for; matrix products, arithmetic and copies ran while one was open for 0% of the time, Pallas kernels for 16%

commit v1 on v0

--- a/solution.py
+++ b/solution.py
@@ -14,7 +14,6 @@
 ENTRY = 4
 PARTS = 4
 STAT_TERMS = 2
-EARLY = 2
 LAST_DIMS = (((1,), (1,)), ((), ()))
 VMEM = pltpu.VMEM
 SMEM = pltpu.SMEM
@@ -107,13 +106,14 @@
     return 3 + count_ka * key_tiles
 
 
-def plan_kernel(dims, order_ref, doc_ref, mask_ref, table):
+def plan_kernel(dims, order_ref, doc_ref, mask_ref, table, counts):
     count_chip, count_ka, order = dims
     place_pb, place_ka = places()
     own_at = own_start(count_chip * count_ka, count_ka)
 
-    def walk(start, query_pb, key_pb, steps, units):
+    def walk(start, query_pb, key_pb, steps, units, count_at=None):
         def query_step(turn_q, units):
+            before = units
             step_q = jnp.int32(order[0])
             for number, step in enumerate(order):
                 step_q = jnp.where(turn_q == number, step, step_q)
@@ -137,7 +137,10 @@
                     units = units + live.astype(jnp.int32)
                 return units
 
-            return lax.fori_loop(0, count_chip, collect, units)
+            units = lax.fori_loop(0, count_chip, collect, units)
+            if count_at is not None:
+                counts[count_at + tile_at] = units - before
+            return units
 
         return lax.fori_loop(*steps, query_step, units)
 
@@ -154,17 +157,27 @@
 
     none = jnp.int32(0)
     sibling = place_pb ^ 1
-    other_first = walk(2, place_pb, sibling, (0, EARLY), none)
-    other = close(2, walk(2, place_pb, sibling, (EARLY, count_ka), other_first))
-    own_first = walk(own_at, place_pb, place_pb, (0, EARLY), none)
-    own = close(own_at, walk(own_at, place_pb, place_pb, (EARLY, count_ka), own_first))
-    there = steps_of(walk(None, sibling, sibling, (0, EARLY), none))
-    there = there + steps_of(walk(None, sibling, place_pb, (0, count_ka), none))
-    lead = jnp.maximum(there - other - steps_of(own_first), 0)
-    table[0] = steps_of(own_first)
-    table[1] = jnp.minimum(steps_of(own_first) + lead, own)
+    every = (0, count_ka)
+    other = close(2, walk(2, place_pb, sibling, every, none, 2 * count_ka))
+    own = close(own_at, walk(own_at, place_pb, place_pb, every, none, 0))
+    walk(None, sibling, sibling, every, none, count_ka)
+    sibling_other = steps_of(walk(None, sibling, place_pb, every, none))
+
+    def first_steps(place):
+        tile = lax.rem(place + order[0], count_ka)
+        return steps_of(counts[tile]), steps_of(counts[2 * count_ka + tile])
+
+    first, second = none, none
+    for place in range(count_ka):
+        first = jnp.maximum(first, sum(first_steps(place)))
+        for core, others in enumerate((other, sibling_other)):
+            units = sum([counts[core * count_ka + (place + step) % count_ka] for step in order[:2]])
+            second = jnp.maximum(second, others + steps_of(units))
+    own_first, other_first = first_steps(place_ka)
+    table[0] = own_first
+    table[1] = jnp.minimum(second - other, own)
     table[2] = own
-    table[ENTRY] = steps_of(other_first)
+    table[ENTRY] = jnp.clip(first - own_first, other_first, other)
     table[ENTRY + 1] = other
 
 
@@ -179,16 +192,16 @@
     if stage == 0:
         (dq_sum, *own), rest = rest[:6], rest[6:]
     elif stage == 1:
-        (dq_start, dq_sum, *dq_early), other, rest = rest[:2 + EARLY], rest[2 + EARLY:7 + EARLY], rest[7 + EARLY:]
+        (dq_start, dq_sum, *dq_halves), other, rest = rest[:4], rest[4:9], rest[9:]
     elif stage == 2:
         (dq_start, *own_start_refs), rest = rest[:6], rest[6:]
         other_refs, rest = rest[:5], rest[5:]
-        (dq_sum, *own_sums, kv_other, other_key_sum, other_value_sum), rest = rest[:6], rest[6:]
+        (dq_sum, *own_sums, kv_other, dq_out, other_key_sum, other_value_sum), rest = rest[:7], rest[7:]
         own = own_start_refs[:3] + own_sums
         other = other_refs[:3] + (other_key_sum, other_value_sum)
     else:
         (dq_start, *own_start_refs), rest = rest[:6], rest[6:]
-        dq_outs, rest = rest[:count_ka - EARLY], rest[count_ka - EARLY:]
+        dq_outs, rest = rest[:count_ka - 2], rest[count_ka - 2:]
         (*own_sums, dq_sum), rest = rest[:3], rest[3:]
         own = own_start_refs[:3] + own_sums
     lse_delta, weights_low, dscores_low = rest
@@ -291,18 +304,20 @@
         run(own_at, own, 0, table[0])
     elif stage == 1:
         run(2, other, 0, table[ENTRY])
-        for number, dq_out in enumerate(dq_early):
-            dq_out[...] = (dq_sum[number] * score_scale).astype(BF16)
+        for number, dq_half in enumerate(dq_halves):
+            part = pl.ds(number * dq_half.shape[1], dq_half.shape[1])
+            dq_half[...] = (dq_sum[0, :, part] * score_scale).astype(BF16)
     elif stage == 2:
         run(2, other, table[ENTRY], table[ENTRY + 1])
         run(own_at, own, table[0], table[1])
+        dq_out[...] = (dq_sum[1] * score_scale).astype(BF16)
         for local in range(count_chip * count_ka):
             part = pl.ds(local * TILE, TILE)
             kv_other[part, :HEAD_DIM] = (other_key_sum[local] * score_scale).astype(BF16)
             kv_other[part, HEAD_DIM:] = other_value_sum[local].astype(BF16)
     else:
         run(own_at, own, table[1], table[2])
-        for number, dq_out in enumerate(dq_outs, EARLY):
+        for number, dq_out in enumerate(dq_outs, 2):
             dq_out[...] = (dq_sum[number] * score_scale).astype(BF16)
 
 
@@ -366,17 +381,17 @@
 
 
 def place_kernel(dims, *rest):
-    count_ka, steps = dims
-    pieces, (dq_out, turned, sems) = rest[:count_ka], rest[count_ka:]
+    count_ka, heads_dev, where = dims
+    pieces, (dq_out, turned, sems) = rest[:len(where)], rest[len(where):]
     copies = []
-    for number, (step, piece) in enumerate(zip(steps, pieces)):
-        width = piece.shape[1]
+    for number, ((step, first), piece) in enumerate(zip(where, pieces)):
         source = lax.rem(places()[1] - step + count_ka, count_ka)
-        columns = pl.ds(pl.multiple_of(source * width, HEAD_DIM), width)
-        for head in range(width // HEAD_DIM):
+        columns = pl.ds(pl.multiple_of((source * heads_dev + first) * HEAD_DIM, HEAD_DIM), piece.shape[1])
+        here = pl.ds(first * HEAD_DIM, piece.shape[1])
+        for head in range(piece.shape[1] // HEAD_DIM):
             part = pl.ds(head * HEAD_DIM, HEAD_DIM)
-            turned[number, :, part] = piece[:, part].T
-        copies.append(pltpu.make_async_copy(turned.at[number], dq_out.at[:, columns], sems.at[number]))
+            turned[step, :, pl.ds((first + head) * HEAD_DIM, HEAD_DIM)] = piece[:, part].T
+        copies.append(pltpu.make_async_copy(turned.at[step, :, here], dq_out.at[:, columns], sems.at[number]))
         copies[-1].start()
     for copy in copies:
         copy.wait()
@@ -508,6 +523,7 @@
         in_specs=in_smem(3),
         out_specs=in_smem(1)[0],
         out_shape=jax.ShapeDtypeStruct((ENTRY * entries,), jnp.int32),
+        scratch_shapes=[SMEM((3 * count_ka,), jnp.int32)],
         cost_estimate=pl.CostEstimate(flops=0, bytes_accessed=1 << 22, transcendentals=0),
         name="plan",
     )(later_order, doc_ids, tile_mask)
@@ -535,19 +551,21 @@
     state = [key_shape] * 3 + [sum_shape] * 2
     dq_sum, *own = attend(0, [dq_sums] + state, [], key_gain, value_gain, own_queries, own_stats, *blocks)
     dq_sum, *other = attend(
-        1, [dq_sums] + [dq_tile] * EARLY + state, [],
+        1, [dq_sums] + [jax.ShapeDtypeStruct((HEAD_DIM, width // 2), BF16)] * 2 + state, [],
         key_gain, value_gain, own_queries, own_stats, *other_blocks, dq_sum,
     )
     dq_parts = [None] * count_ka
-    for step, tile in zip(early, other):
-        dq_parts[step] = turn(tile, step)
-    other = other[EARLY:]
-    dq_sum, *own[3:], kv_other = attend(
-        2, [dq_sums] + [sum_shape] * 2 + [jax.ShapeDtypeStruct((key_tiles * TILE, 2 * HEAD_DIM), BF16)],
+    dq_halves, other = [turn(part, half) for part in other[:2]], other[2:]
+    dq_sum, *own[3:], kv_other, dq_second = attend(
+        2,
+        [dq_sums] + [sum_shape] * 2
+        + [jax.ShapeDtypeStruct((key_tiles * TILE, 2 * HEAD_DIM), BF16), dq_tile],
         [VMEM(sum_shape.shape, F32)] * 2,
         own_queries, own_stats, dq_sum, *own, *other,
     )
+    kv_other, dq_halves[0] = lax.optimization_barrier((kv_other, dq_halves[0]))
     kv_back = swap(kv_other, 1)
+    dq_parts[1] = turn(dq_second, 1)
     *dq_late, key_sum, value_sum = attend(
         3, [dq_tile] * len(late) + [sum_shape] * 2, [VMEM(dq_sums.shape, F32)],
         own_queries, own_stats, dq_sum, *own,
@@ -561,7 +579,7 @@
         name="merge",
     )(key_sum, value_sum, kv_back, *blocks)
     kv_parts = [kv_own[0]] + [swap(kv_own[number], 2 * number) for number in range(1, count_chip)]
-    dq_late, dq_parts[half], dq_parts[1] = lax.optimization_barrier((dq_late, dq_parts[half], dq_parts[1]))
+    dq_late, dq_parts[1], dq_halves[1] = lax.optimization_barrier((dq_late, dq_parts[1], dq_halves[1]))
     for step, tile in zip(late, dq_late):
         dq_parts[step] = turn(tile, step) if step else tile
 
@@ -576,16 +594,17 @@
         name="collect",
     )(key_gain, value_gain, *kv_parts))
     pieces = [pieces[0]] + [turn(piece, -step) for step, piece in enumerate(pieces[1:], 1)]
+    where = ((half, 0), (half, heads_dev // 2)) + tuple((step, 0) for step in order[1:])
     grad_queries = pl.pallas_call(
-        functools.partial(place_kernel, (count_ka, order)),
-        in_specs=in_vmem(count_ka),
+        functools.partial(place_kernel, (count_ka, heads_dev, where)),
+        in_specs=in_vmem(len(where)),
         out_specs=anywhere(1)[0],
         out_shape=jax.ShapeDtypeStruct((rows_dev, feat_width), BF16),
-        scratch_shapes=[VMEM((count_ka, TILE, width), BF16), pltpu.SemaphoreType.DMA((count_ka,))],
+        scratch_shapes=[VMEM((count_ka, TILE, width), BF16), pltpu.SemaphoreType.DMA((len(where),))],
         compiler_params=params(16),
         cost_estimate=pl.CostEstimate(flops=0, bytes_accessed=4 * rows_dev * feat_width, transcendentals=0),
         name="place_queries",
-    )(*[dq_parts[step] for step in order])
+    )(*dq_halves, *[dq_parts[step] for step in order[1:]])
     pieces, grad_queries = lax.optimization_barrier((pieces, grad_queries))
     grad_keys, grad_values, gains = pl.pallas_call(
         functools.partial(finish_kernel, (count_ka, share)),

time: 81.3 us -> 82.4 us (1.014)
  Pallas kernels: 24.7 us -> 32.2 us
  starting transfers between devices: 27.6 us -> 23.7 us
  waiting for transfers between devices: 27 us -> 24.3 us
    pallas_call x4, Pallas kernels: 13.4 us -> 20.4 us  [attend(): pl.pallas_call(functools.partial(attention_kernel, (count_chip, count_ka,...]
    ppermute x9 -> x10, waiting for transfers between devices: 17.3 us -> 12.5 us  [turn(): lax.ppermute(array, 'ka', [(at, (at + step) % count_ka) for at in range(c...]
    ppermute x9 -> x10, starting transfers between devices: 19.1 us -> 15.9 us  [turn(): lax.ppermute(array, 'ka', [(at, (at + step) % count_ka) for at in range(c...]
    ppermute x12, waiting for transfers between devices: 9.74 us -> 11.7 us  [swap(): lax.ppermute(array, 'pb', [(at, at ^ number) for at in range(count_pb)])]
  transfers between devices with their start and end apart: 21 -> 22, of which waited for: 10 -> 10; matrix products, arithmetic and copies ran while one was open for 0% -> 0% of each run, Pallas kernels for 16% -> 26%
where the time goes in v1:
time: 82.4 us; the launch traced here: 81.7 us
  Pallas kernels  32.2 us (39%)
  waiting for transfers between devices  24.3 us (29%)
  starting transfers between devices  23.7 us (29%)
  between operations  0.86 us (1%)
    pallas_call x4, Pallas kernels, attend(): pl.pallas_call(functools.partial(attention_kernel, (count_chip, count_ka,...  20.4 us
    ppermute x10, starting transfers between devices, turn(): lax.ppermute(array, 'ka', [(at, (at + step) % count_ka) for at in range(c...  15.9 us
    ppermute x10, waiting for transfers between devices, turn(): lax.ppermute(array, 'ka', [(at, (at + step) % count_ka) for at in range(c...  12.5 us
    ppermute x12, waiting for transfers between devices, swap(): lax.ppermute(array, 'pb', [(at, at ^ number) for at in range(count_pb)])  11.7 us
    ppermute x12, starting transfers between devices, swap(): lax.ppermute(array, 'pb', [(at, at ^ number) for at in range(count_pb)])  7.75 us
    pallas_call x1, Pallas kernels, shards(): pl.pallas_call(functools.partial(plan_kernel, (count_chip, count_ka, orde...  4.18 us
    pallas_call x1, Pallas kernels, shards(): pl.pallas_call(functools.partial(prepare_kernel, (count_ka, heads, heads_...  2.79 us
  transfers between devices with their start and end apart: 22, of which 10 were waited for; matrix products, arithmetic and copies ran while one was open for 0% of the time, Pallas kernels for 26%

profile of v1, /device:TPU:0, one launch (start us, length us, event | category | flops | bytes accessed | tf_op | source)
XLA Modules:
  0.0 81.7 jit_solution(3362905979402845683)
XLA Ops:
  0.6 2.8 %prepare.1 = (bf16[144,256]{1,0:T(8,128)(2,1)}, bf16[144,256]{1,0:T(8,128)(2,1)}, bf16[144,256]{1,0:T(8,128)(2,1)}, bf16[144,256]{1,0:T(8,128)(2,1)}) custom-call(bf16[128,512]{1,0:T(8,128)(2,1)} %key_ref.1, bf16[128,512]{1,0:T(8,128)(2,1)} %value_ref.1, bf16[128,4096]{1,0:T(8,128)(2,1)} %attn_ref.1, bf16[512,4096]{1,0:T(8,128)(2,1)} %grads_ref.3, ...), custom_call_target="tpu_custom_call" | custom-call | tf_op jit(solution)/shard_map/prepare/pallas_call | solution.py:480
  3.4 3.1 %collective-permute-start = (bf16[144,256]{1,0:T(8,128)(2,1)}, bf16[144,256]{1,0:T(8,128)(2,1)S(1)}, u32[]{:S(2)}, u32[]{:S(2)}) collective-permute-start(bf16[144,256]{1,0:T(8,128)(2,1)} %get-tuple-element.64), channel_id=1, source_target_pairs={{0,1},{1,2},{2,3},{3,0},{4,5},{5,6},{6,7},{7,4},{8,9},{9,10},{10,1... | collective-permute-start | bytes 221192 | tf_op jit(solution)/shard_map/ppermute | solution.py:478
  6.5 2.6 %collective-permute-start.1 = (bf16[144,256]{1,0:T(8,128)(2,1)}, bf16[144,256]{1,0:T(8,128)(2,1)S(1)}, u32[]{:S(2)}, u32[]{:S(2)}) collective-permute-start(bf16[144,256]{1,0:T(8,128)(2,1)} %get-tuple-element.65), channel_id=1, source_target_pairs={{0,2},{1,3},{2,0},{3,1},{4,6},{5,7},{6,4},{7,5},{8,10},{9,11},{10,... | collective-permute-start | bytes 221192 | tf_op jit(solution)/shard_map/ppermute | solution.py:478
  9.1 1.3 %collective-permute-start.2 = (bf16[144,256]{1,0:T(8,128)(2,1)}, bf16[144,256]{1,0:T(8,128)(2,1)S(1)}, u32[]{:S(2)}, u32[]{:S(2)}) collective-permute-start(bf16[144,256]{1,0:T(8,128)(2,1)} %get-tuple-element.66), channel_id=1, source_target_pairs={{0,3},{1,0},{2,1},{3,2},{4,7},{5,4},{6,5},{7,6},{8,11},{9,8},{10,9... | collective-permute-start | bytes 221192 | tf_op jit(solution)/shard_map/ppermute | solution.py:478
  10.4 0.0 copy-start.3
  10.4 0.0 copy-start
  10.5 0.0 copy-start.1
  10.5 1.6 %own_heads.1.rest_3_.rest_1_ = bf16[2,512,1024]{2,1,0:T(8,128)(2,1)S(1)} custom-call(bf16[512,4096]{1,0:T(8,128)(2,1)} %queries_ref, bf16[512,4096]{1,0:T(8,128)(2,1)} %grads_ref.3), custom_call_target="tpu_custom_call" | custom-call | bytes 4194304 | tf_op jit(solution)/shard_map/own_heads/pallas_call | solution.py:495
  12.1 0.0 collective-permute-done
  12.1 2.2 %collective-permute-done.1 = bf16[144,256]{1,0:T(8,128)(2,1)S(1)} collective-permute-done((bf16[144,256]{1,0:T(8,128)(2,1)}, bf16[144,256]{1,0:T(8,128)(2,1)S(1)}, u32[]{:S(2)}, u32[]{:S(2)}) %collective-permute-start.1) | collective-permute-done | bytes 73760 | tf_op jit(solution)/shard_map/ppermute | solution.py:478
  14.3 0.2 collective-permute-done.2
  14.5 0.0 copy-done.3
  14.6 2.5 %collective-permute-start.8 = (bf16[512,256]{1,0:T(8,128)(2,1)S(1)}, bf16[512,256]{1,0:T(8,128)(2,1)S(1)}, u32[]{:S(2)}, u32[]{:S(2)}) collective-permute-start(bf16[512,256]{1,0:T(8,128)(2,1)S(1)} %pad_maximum_fusion.rest_5_.rest_0_), channel_id=1, source_target_pairs={{0,24},{4,28},{8,16},{12,20},{16,8},{20,12},{24,0},{28,4},{1,25},{... | collective-permute-start | bytes 786440 | tf_op jit(solution)/shard_map/ppermute | solution.py:475
  17.1 0.5 collective-permute-start.6
  17.6 0.5 collective-permute-start.4
  18.1 0.1 collective-permute-start.3
  18.2 4.2 %plan.1.rest_0_ = s32[528]{0:T(1024)} custom-call(s32[32]{0:T(128)} %order_ref, s32[32]{0:T(128)} %doc_ref.1, s32[32,32]{1,0:T(8,128)} %mask_ref.1), custom_call_target="tpu_custom_call" | custom-call | bytes 4194304 | tf_op jit(solution)/shard_map/plan/pallas_call | solution.py:521
  22.4 2.4 %collective-permute-done.8.rest_8_.rest_3_ = bf16[512,256]{1,0:T(8,128)(2,1)S(1)} collective-permute-done((bf16[512,256]{1,0:T(8,128)(2,1)S(1)}, bf16[512,256]{1,0:T(8,128)(2,1)S(1)}, u32[]{:S(2)}, u32[]{:S(2)}) %collective-permute-start.8) | collective-permute-done | bytes 262176 | tf_op jit(solution)/shard_map/ppermute | solution.py:475
  24.8 0.0 collective-permute-start.9
  24.8 4.3 %collective-permute-done.6.rest_7_.rest_2_ = bf16[512,256]{1,0:T(8,128)(2,1)S(1)} collective-permute-done((bf16[512,256]{1,0:T(8,128)(2,1)S(1)}, bf16[512,256]{1,0:T(8,128)(2,1)S(1)}, u32[]{:S(2)}, u32[]{:S(2)}) %collective-permute-start.6) | collective-permute-done | bytes 262176 | tf_op jit(solution)/shard_map/ppermute | solution.py:475
  29.1 0.0 collective-permute-start.7
  29.1 0.0 collective-permute-done.4.rest_6_.rest_1_
  29.1 0.5 collective-permute-start.5
  29.6 0.0 copy-done
  29.6 0.0 copy-done.1
  29.6 0.0 copy-start.2
  29.6 0.7 copy-done.2
  30.3 2.1 %attention_first.1 = (f32[4,128,1024]{2,1,0:T(8,128)S(1)}, bf16[16,128,128]{2,1,0:T(8,128)(2,1)S(1)}, bf16[16,128,128]{2,1,0:T(8,128)(2,1)S(1)}, bf16[16,128,128...) custom-call(s32[528]{0:T(1024)S(1)} %copy-done.2, f32[1,512]{1,0:T(1,128)S(1)} %bitcast.4, ...), custom_call_target="tpu_custom_call" | custom-call | flops 5368709120 | bytes 1048576 | tf_op jit(solution)/shard_map/attention_first/pallas_call | solution.py:532
  32.4 0.0 collective-permute-done.3.rest_5_
  32.4 0.0 collective-permute-done.9.rest_8_
  32.4 0.0 collective-permute-done.7.rest_7_
  32.4 0.0 collective-permute-done.5.rest_6_
  32.4 7.1 %attention_leaving.1 = (f32[4,128,1024]{2,1,0:T(8,128)S(1)}, bf16[128,512]{1,0:T(8,128)(2,1)S(1)}, bf16[128,512]{1,0:T(8,128)(2,1)S(1)}, bf16[16,128,128]{2,1,0:...) custom-call(s32[528]{0:T(1024)S(1)} %copy-done.2, ...), custom_call_target="tpu_custom_call" | custom-call | flops 5368709120 | bytes 1048576 | tf_op jit(solution)/shard_map/attention_leaving/pallas_call | solution.py:532
  39.6 1.3 %collective-permute-start.10 = (bf16[128,512]{1,0:T(8,128)(2,1)S(1)}, bf16[128,512]{1,0:T(8,128)(2,1)S(1)}, u32[]{:S(2)}, u32[]{:S(2)}) collective-permute-start(bf16[128,512]{1,0:T(8,128)(2,1)S(1)} %get-tuple-element.92), channel_id=1, source_target_pairs={{0,2},{1,3},{2,0},{3,1},{4,6},{5,7},{6,4},{7,5},{8,10},{9,11},{10,... | collective-permute-start | bytes 393224 | tf_op jit(solution)/shard_map/ppermute | solution.py:478
  40.8 8.3 %attention_other.1 = (f32[4,128,1024]{2,1,0:T(8,128)S(1)}, f32[16,128,128]{2,1,0:T(8,128)S(1)}, f32[16,128,128]{2,1,0:T(8,128)S(1)}, bf16[2048,256]{1,0:T(8,128)(2,1)S(1)}, bf16[128,1024]{1,0:T(8,128)(2,1)S(1)}) custom-call(s32[528]{0:T(1024)S(1)} %copy-done.2, bf16[2,512,1024]{2,1,0:T(8,128)(2,1)S(1)} %own_heads.1.rest_3_.rest_1_, ...), custom_call_target="tpu_custom_call" | custom-call | flops 5368709120 | bytes 1048576 | tf_op jit(solution)/shard_map/attention_other/pallas_call | solution.py:532
  49.2 0.0 collective-permute-done.10.rest_0_
  49.2 0.1 collective-permute-start.11
  49.2 1.8 %collective-permute-start.19 = (bf16[128,512]{1,0:T(8,128)(2,1)S(1)}, bf16[128,512]{1,0:T(8,128)(2,1)S(1)}, u32[]{:S(2)}, u32[]{:S(2)}) collective-permute-start(bf16[128,512]{1,0:T(8,128)(2,1)S(1)} %get-tuple-element.106), channel_id=1, source_target_pairs={{0,2},{1,3},{2,0},{3,1},{4,6},{5,7},{6,4},{7,5},{8,10},{9,11},{10,... | collective-permute-start | bytes 393224 | tf_op jit(solution)/shard_map/ppermute | solution.py:478
  51.1 2.1 %collective-permute-start.18 = (bf16[128,1024]{1,0:T(8,128)(2,1)S(1)}, bf16[128,1024]{1,0:T(8,128)(2,1)S(1)}, u32[]{:S(2)}, u32[]{:S(2)}) collective-permute-start(bf16[128,1024]{1,0:T(8,128)(2,1)S(1)} %get-tuple-element.105), channel_id=1, source_target_pairs={{0,1},{1,2},{2,3},{3,0},{4,5},{5,6},{6,7},{7,4},{8,9},{9,10},{10,1... | collective-permute-start | bytes 786440 | tf_op jit(solution)/shard_map/ppermute | solution.py:478
  53.2 2.9 %attention_own.1 = (bf16[128,1024]{1,0:T(8,128)(2,1)S(1)}, bf16[128,1024]{1,0:T(8,128)(2,1)S(1)}, f32[16,128,128]{2,1,0:T(8,128)S(1)}, f32[16,128,128]{2,1,0:T(8,128)S(1)}) custom-call(s32[528]{0:T(1024)S(1)} %copy-done.2, bf16[2,512,1024]{2,1,0:T(8,128)(2,1)S(1)} %own_heads.1.rest_3_.rest_1_, bf16[64,256]{1,0:T(8,128)(2,1)S(1)} %pad_maximum_fusion.1.rest_4_.rest_2_, ...), custom_call_target="tpu_custom_call" | custom-call | flops 5368709120 | bytes 1048576 | tf_op jit(solution)/shard_map/attention_own/pallas_call | solution.py:532
  56.1 0.0 collective-permute-done.11.kv_back
  56.1 0.5 merge.1
  56.6 0.1 collective-permute-start.12
  56.7 0.1 collective-permute-start.13
  56.8 3.4 %collective-permute-start.14 = (bf16[528,256]{1,0:T(8,128)(2,1)S(1)}, bf16[528,256]{1,0:T(8,128)(2,1)S(1)}, u32[]{:S(2)}, u32[]{:S(2)}) collective-permute-start(bf16[528,256]{1,0:T(8,128)(2,1)S(1)} %get-tuple-element.97), channel_id=1, source_target_pairs={{0,24},{4,28},{8,16},{12,20},{16,8},{20,12},{24,0},{28,4},{1,25},{... | collective-permute-start | bytes 811016 | tf_op jit(solution)/shard_map/ppermute | solution.py:475
  60.2 4.3 %collective-permute-done.19.rest_1_ = bf16[128,512]{1,0:T(8,128)(2,1)S(1)} collective-permute-done((bf16[128,512]{1,0:T(8,128)(2,1)S(1)}, bf16[128,512]{1,0:T(8,128)(2,1)S(1)}, u32[]{:S(2)}, u32[]{:S(2)}) %collective-permute-start.19) | collective-permute-done | bytes 131104 | tf_op jit(solution)/shard_map/ppermute | solution.py:478
  64.5 0.0 collective-permute-done.18.rest_2_
  64.5 0.5 collective-permute-start.20
  65.0 0.9 %collective-permute-done.12.rest_1_ = bf16[528,256]{1,0:T(8,128)(2,1)S(1)} collective-permute-done((bf16[528,256]{1,0:T(8,128)(2,1)S(1)}, bf16[528,256]{1,0:T(8,128)(2,1)S(1)}, u32[]{:S(2)}, u32[]{:S(2)}) %collective-permute-start.12) | collective-permute-done | bytes 270368 | tf_op jit(solution)/shard_map/ppermute | solution.py:475
  65.9 3.0 %collective-permute-done.13.rest_2_ = bf16[528,256]{1,0:T(8,128)(2,1)S(1)} collective-permute-done((bf16[528,256]{1,0:T(8,128)(2,1)S(1)}, bf16[528,256]{1,0:T(8,128)(2,1)S(1)}, u32[]{:S(2)}, u32[]{:S(2)}) %collective-permute-start.13) | collective-permute-done | bytes 270368 | tf_op jit(solution)/shard_map/ppermute | solution.py:475
  68.8 0.0 collective-permute-done.14.rest_3_
  68.9 0.1 collect.1
  69.0 1.7 %collective-permute-start.15 = (bf16[144,256]{1,0:T(8,128)(2,1)S(1)}, bf16[144,256]{1,0:T(8,128)(2,1)S(1)}, u32[]{:S(2)}, u32[]{:S(2)}) collective-permute-start(bf16[144,256]{1,0:T(8,128)(2,1)S(1)} %get-tuple-element.99), channel_id=1, source_target_pairs={{0,3},{1,0},{2,1},{3,2},{4,7},{5,4},{6,5},{7,6},{8,11},{9,8},{10,9... | collective-permute-start | bytes 221192 | tf_op jit(solution)/shard_map/ppermute | solution.py:478
  70.7 0.1 collective-permute-start.16
  70.8 1.4 %collective-permute-start.17 = (bf16[144,256]{1,0:T(8,128)(2,1)S(1)}, bf16[144,256]{1,0:T(8,128)(2,1)S(1)}, u32[]{:S(2)}, u32[]{:S(2)}) collective-permute-start(bf16[144,256]{1,0:T(8,128)(2,1)S(1)} %get-tuple-element.101), channel_id=1, source_target_pairs={{0,1},{1,2},{2,3},{3,0},{4,5},{5,6},{6,7},{7,4},{8,9},{9,10},{10,1... | collective-permute-start | bytes 221192 | tf_op jit(solution)/shard_map/ppermute | solution.py:478
  72.2 0.9 %collective-permute-done.20.rest_4_ = bf16[128,1024]{1,0:T(8,128)(2,1)S(1)} collective-permute-done((bf16[128,1024]{1,0:T(8,128)(2,1)S(1)}, bf16[128,1024]{1,0:T(8,128)(2,1)S(1)}, u32[]{:S(2)}, u32[]{:S(2)}) %collective-permute-start.20) | collective-permute-done | bytes 262176 | tf_op jit(solution)/shard_map/ppermute | solution.py:478
  73.2 1.1 %place_queries.1 = bf16[128,4096]{1,0:T(8,128)(2,1)} custom-call(bf16[128,512]{1,0:T(8,128)(2,1)S(1)} %collective-permute-done.10.rest_0_, bf16[128,512]{1,0:T(8,128)(2,1)S(1)} %collective-permute-done.19.rest_1_, bf16[128,1024]{1,0:T(8,128)(2,1)S(1)} %collective-permute-done.18.rest_2_, bf16[128,1024]{1,0:T(8,128)(2,1)S(1)} %get-tuple-element.109.rest_3_, ...), custom_call_target="tpu_custom_call" | custom-call | bytes 2097152 | tf_op jit(solution)/shard_map/place_queries/pallas_call | solution.py:598
  74.3 0.0 collective-permute-done.15.rest_1_
  74.3 4.8 %collective-permute-done.16.rest_2_ = bf16[144,256]{1,0:T(8,128)(2,1)S(1)} collective-permute-done((bf16[144,256]{1,0:T(8,128)(2,1)S(1)}, bf16[144,256]{1,0:T(8,128)(2,1)S(1)}, u32[]{:S(2)}, u32[]{:S(2)}) %collective-permute-start.16) | collective-permute-done | bytes 73760 | tf_op jit(solution)/shard_map/ppermute | solution.py:478
  79.1 0.0 collective-permute-done.17.rest_3_
  79.1 0.8 %finish.1 = (bf16[128,512]{1,0:T(8,128)(2,1)}, bf16[128,512]{1,0:T(8,128)(2,1)}, f32[2,512]{1,0:T(2,128)S(1)}) custom-call(f32[1,512]{1,0:T(1,128)S(1)} %bitcast.7, f32[1,512]{1,0:T(1,128)S(1)} %bitcast.11, f32[144,256]{1,0:T(8,128)S(1)} %get-tuple-element.112.rest_0_, bf16[144,256]{1,0:T(8,128)(2,1)S(1)} %collective-permute-done.15.rest_1_, ...), custom_call_target="tpu_custom_call" | custom-call | tf_op jit(solution)/shard_map/finish/pallas_call | solution.py:609
  80.0 0.0 collective-permute-start.21
  80.0 1.2 %collective-permute-done.21.other_ref = f32[2,512]{1,0:T(2,128)S(1)} collective-permute-done((f32[2,512]{1,0:T(2,128)S(1)}, f32[2,512]{1,0:T(2,128)S(1)}, u32[]{:S(2)}, u32[]{:S(2)}) %collective-permute-start.21) | collective-permute-done | bytes 4128 | tf_op jit(solution)/shard_map/ppermute | solution.py:475
  81.1 0.6 add_gains.1
  (10 shorter events, 0.1 us)
Async XLA Ops:
  3.4 8.6 %collective-permute-start = (bf16[144,256]{1,0:T(8,128)(2,1)}, bf16[144,256]{1,0:T(8,128)(2,1)S(1)}, u32[]{:S(2)}, u32[]{:S(2)}) collective-permute-start(bf16[144,256]{1,0:T(8,128)(2,1)} %get-tuple-element.64), channel_id=1, source_target_pairs={{0,1},{1,2},{2,3},{3,0},{4,5},{5,6},{6,7},{7,4},{8,9},{9,10},{10,1... | collective-permute-start | bytes 221192 | tf_op jit(solution)/shard_map/ppermute | solution.py:478
  6.5 7.8 %collective-permute-start.1 = (bf16[144,256]{1,0:T(8,128)(2,1)}, bf16[144,256]{1,0:T(8,128)(2,1)S(1)}, u32[]{:S(2)}, u32[]{:S(2)}) collective-permute-start(bf16[144,256]{1,0:T(8,128)(2,1)} %get-tuple-element.65), channel_id=1, source_target_pairs={{0,2},{1,3},{2,0},{3,1},{4,6},{5,7},{6,4},{7,5},{8,10},{9,11},{10,... | collective-permute-start | bytes 221192 | tf_op jit(solution)/shard_map/ppermute | solution.py:478
  9.1 5.4 %collective-permute-start.2 = (bf16[144,256]{1,0:T(8,128)(2,1)}, bf16[144,256]{1,0:T(8,128)(2,1)S(1)}, u32[]{:S(2)}, u32[]{:S(2)}) collective-permute-start(bf16[144,256]{1,0:T(8,128)(2,1)} %get-tuple-element.66), channel_id=1, source_target_pairs={{0,3},{1,0},{2,1},{3,2},{4,7},{5,4},{6,5},{7,6},{8,11},{9,8},{10,9... | collective-permute-start | bytes 221192 | tf_op jit(solution)/shard_map/ppermute | solution.py:478
  10.4 4.0 %copy-start.3 = (bf16[144,256]{1,0:T(8,128)(2,1)S(1)}, bf16[144,256]{1,0:T(8,128)(2,1)}, u32[]{:S(2)}) copy-start(bf16[144,256]{1,0:T(8,128)(2,1)} %get-tuple-element.68) | copy-start | bytes 221188
  10.4 19.1 %copy-start = (f32[512]{0:T(512)S(1)}, f32[512]{0:T(512)}, u32[]{:S(2)}) copy-start(f32[512]{0:T(512)} %param.17) | copy-start | bytes 6148
  10.5 19.1 %copy-start.1 = (f32[512]{0:T(512)S(1)}, f32[512]{0:T(512)}, u32[]{:S(2)}) copy-start(f32[512]{0:T(512)} %param.18) | copy-start | bytes 6148
  14.6 10.2 %collective-permute-start.8 = (bf16[512,256]{1,0:T(8,128)(2,1)S(1)}, bf16[512,256]{1,0:T(8,128)(2,1)S(1)}, u32[]{:S(2)}, u32[]{:S(2)}) collective-permute-start(bf16[512,256]{1,0:T(8,128)(2,1)S(1)} %pad_maximum_fusion.rest_5_.rest_0_), channel_id=1, source_target_pairs={{0,24},{4,28},{8,16},{12,20},{16,8},{20,12},{24,0},{28,4},{1,25},{... | collective-permute-start | bytes 786440 | tf_op jit(solution)/shard_map/ppermute | solution.py:475
  17.1 12.0 %collective-permute-start.6 = (bf16[512,256]{1,0:T(8,128)(2,1)S(1)}, bf16[512,256]{1,0:T(8,128)(2,1)S(1)}, u32[]{:S(2)}, u32[]{:S(2)}) collective-permute-start(bf16[512,256]{1,0:T(8,128)(2,1)S(1)} %pad_maximum_fusion.rest_5_.rest_0_), channel_id=1, source_target_pairs={{0,16},{4,20},{8,24},{12,28},{16,0},{20,4},{24,8},{28,12},{1,17},{... | collective-permute-start | bytes 786440 | tf_op jit(solution)/shard_map/ppermute | solution.py:475
  17.6 11.5 %collective-permute-start.4 = (bf16[512,256]{1,0:T(8,128)(2,1)S(1)}, bf16[512,256]{1,0:T(8,128)(2,1)S(1)}, u32[]{:S(2)}, u32[]{:S(2)}) collective-permute-start(bf16[512,256]{1,0:T(8,128)(2,1)S(1)} %pad_maximum_fusion.rest_5_.rest_0_), channel_id=1, source_target_pairs={{0,8},{4,12},{8,0},{12,4},{16,24},{20,28},{24,16},{28,20},{1,9},{5... | collective-permute-start | bytes 786440 | tf_op jit(solution)/shard_map/ppermute | solution.py:475
  18.1 14.3 %collective-permute-start.3 = (bf16[512,256]{1,0:T(8,128)(2,1)S(1)}, bf16[512,256]{1,0:T(8,128)(2,1)S(1)}, u32[]{:S(2)}, u32[]{:S(2)}) collective-permute-start(bf16[512,256]{1,0:T(8,128)(2,1)S(1)} %pad_maximum_fusion.rest_5_.rest_0_), channel_id=1, source_target_pairs={{0,4},{4,0},{8,12},{12,8},{16,20},{20,16},{24,28},{28,24},{1,5},{5... | collective-permute-start | bytes 786440 | tf_op jit(solution)/shard_map/ppermute | solution.py:475
  24.8 7.6 %collective-permute-start.9 = (bf16[512,256]{1,0:T(8,128)(2,1)S(1)}, bf16[512,256]{1,0:T(8,128)(2,1)S(1)}, u32[]{:S(2)}, u32[]{:S(2)}) collective-permute-start(bf16[512,256]{1,0:T(8,128)(2,1)S(1)} %collective-permute-done.8.rest_8_.rest_3_), channel_id=1, source_target_pairs={{0,4},{4,0},{8,12},{12,8},{16,20},{20,16},{24,28},{28,24},{1,5},{5... | collective-permute-start | bytes 786440 | tf_op jit(solution)/shard_map/ppermute | solution.py:475
  29.1 3.3 %collective-permute-start.7 = (bf16[512,256]{1,0:T(8,128)(2,1)S(1)}, bf16[512,256]{1,0:T(8,128)(2,1)S(1)}, u32[]{:S(2)}, u32[]{:S(2)}) collective-permute-start(bf16[512,256]{1,0:T(8,128)(2,1)S(1)} %collective-permute-done.6.rest_7_.rest_2_), channel_id=1, source_target_pairs={{0,4},{4,0},{8,12},{12,8},{16,20},{20,16},{24,28},{28,24},{1,5},{5... | collective-permute-start | bytes 786440 | tf_op jit(solution)/shard_map/ppermute | solution.py:475
  29.1 3.3 %collective-permute-start.5 = (bf16[512,256]{1,0:T(8,128)(2,1)S(1)}, bf16[512,256]{1,0:T(8,128)(2,1)S(1)}, u32[]{:S(2)}, u32[]{:S(2)}) collective-permute-start(bf16[512,256]{1,0:T(8,128)(2,1)S(1)} %collective-permute-done.4.rest_6_.rest_1_), channel_id=1, source_target_pairs={{0,4},{4,0},{8,12},{12,8},{16,20},{20,16},{24,28},{28,24},{1,5},{5... | collective-permute-start | bytes 786440 | tf_op jit(solution)/shard_map/ppermute | solution.py:475
  29.6 0.7 copy-start.2
  39.6 9.6 %collective-permute-start.10 = (bf16[128,512]{1,0:T(8,128)(2,1)S(1)}, bf16[128,512]{1,0:T(8,128)(2,1)S(1)}, u32[]{:S(2)}, u32[]{:S(2)}) collective-permute-start(bf16[128,512]{1,0:T(8,128)(2,1)S(1)} %get-tuple-element.92), channel_id=1, source_target_pairs={{0,2},{1,3},{2,0},{3,1},{4,6},{5,7},{6,4},{7,5},{8,10},{9,11},{10,... | collective-permute-start | bytes 393224 | tf_op jit(solution)/shard_map/ppermute | solution.py:478
  49.2 6.9 %collective-permute-start.11 = (bf16[2048,256]{1,0:T(8,128)(2,1)S(1)}, bf16[2048,256]{1,0:T(8,128)(2,1)S(1)}, u32[]{:S(2)}, u32[]{:S(2)}) collective-permute-start(bf16[2048,256]{1,0:T(8,128)(2,1)S(1)} %get-tuple-element.93), channel_id=1, source_target_pairs={{0,4},{4,0},{8,12},{12,8},{16,20},{20,16},{24,28},{28,24},{1,5},{5... | collective-permute-start | bytes 3145736 | tf_op jit(solution)/shard_map/ppermute | solution.py:475
  49.2 15.2 %collective-permute-start.19 = (bf16[128,512]{1,0:T(8,128)(2,1)S(1)}, bf16[128,512]{1,0:T(8,128)(2,1)S(1)}, u32[]{:S(2)}, u32[]{:S(2)}) collective-permute-start(bf16[128,512]{1,0:T(8,128)(2,1)S(1)} %get-tuple-element.106), channel_id=1, source_target_pairs={{0,2},{1,3},{2,0},{3,1},{4,6},{5,7},{6,4},{7,5},{8,10},{9,11},{10,... | collective-permute-start | bytes 393224 | tf_op jit(solution)/shard_map/ppermute | solution.py:478
  51.1 13.4 %collective-permute-start.18 = (bf16[128,1024]{1,0:T(8,128)(2,1)S(1)}, bf16[128,1024]{1,0:T(8,128)(2,1)S(1)}, u32[]{:S(2)}, u32[]{:S(2)}) collective-permute-start(bf16[128,1024]{1,0:T(8,128)(2,1)S(1)} %get-tuple-element.105), channel_id=1, source_target_pairs={{0,1},{1,2},{2,3},{3,0},{4,5},{5,6},{6,7},{7,4},{8,9},{9,10},{10,1... | collective-permute-start | bytes 786440 | tf_op jit(solution)/shard_map/ppermute | solution.py:478
  56.6 9.3 %collective-permute-start.12 = (bf16[528,256]{1,0:T(8,128)(2,1)S(1)}, bf16[528,256]{1,0:T(8,128)(2,1)S(1)}, u32[]{:S(2)}, u32[]{:S(2)}) collective-permute-start(bf16[528,256]{1,0:T(8,128)(2,1)S(1)} %get-tuple-element.95), channel_id=1, source_target_pairs={{0,8},{4,12},{8,0},{12,4},{16,24},{20,28},{24,16},{28,20},{1,9},{5... | collective-permute-start | bytes 811016 | tf_op jit(solution)/shard_map/ppermute | solution.py:475
  56.7 12.2 %collective-permute-start.13 = (bf16[528,256]{1,0:T(8,128)(2,1)S(1)}, bf16[528,256]{1,0:T(8,128)(2,1)S(1)}, u32[]{:S(2)}, u32[]{:S(2)}) collective-permute-start(bf16[528,256]{1,0:T(8,128)(2,1)S(1)} %get-tuple-element.96), channel_id=1, source_target_pairs={{0,16},{4,20},{8,24},{12,28},{16,0},{20,4},{24,8},{28,12},{1,17},{... | collective-permute-start | bytes 811016 | tf_op jit(solution)/shard_map/ppermute | solution.py:475
  56.8 12.1 %collective-permute-start.14 = (bf16[528,256]{1,0:T(8,128)(2,1)S(1)}, bf16[528,256]{1,0:T(8,128)(2,1)S(1)}, u32[]{:S(2)}, u32[]{:S(2)}) collective-permute-start(bf16[528,256]{1,0:T(8,128)(2,1)S(1)} %get-tuple-element.97), channel_id=1, source_target_pairs={{0,24},{4,28},{8,16},{12,20},{16,8},{20,12},{24,0},{28,4},{1,25},{... | collective-permute-start | bytes 811016 | tf_op jit(solution)/shard_map/ppermute | solution.py:475
  64.5 8.7 %collective-permute-start.20 = (bf16[128,1024]{1,0:T(8,128)(2,1)S(1)}, bf16[128,1024]{1,0:T(8,128)(2,1)S(1)}, u32[]{:S(2)}, u32[]{:S(2)}) collective-permute-start(bf16[128,1024]{1,0:T(8,128)(2,1)S(1)} %get-tuple-element.110), channel_id=1, source_target_pairs={{0,3},{1,0},{2,1},{3,2},{4,7},{5,4},{6,5},{7,6},{8,11},{9,8},{10,9... | collective-permute-start | bytes 786440 | tf_op jit(solution)/shard_map/ppermute | solution.py:478
  69.0 5.3 %collective-permute-start.15 = (bf16[144,256]{1,0:T(8,128)(2,1)S(1)}, bf16[144,256]{1,0:T(8,128)(2,1)S(1)}, u32[]{:S(2)}, u32[]{:S(2)}) collective-permute-start(bf16[144,256]{1,0:T(8,128)(2,1)S(1)} %get-tuple-element.99), channel_id=1, source_target_pairs={{0,3},{1,0},{2,1},{3,2},{4,7},{5,4},{6,5},{7,6},{8,11},{9,8},{10,9... | collective-permute-start | bytes 221192 | tf_op jit(solution)/shard_map/ppermute | solution.py:478
  70.7 8.4 %collective-permute-start.16 = (bf16[144,256]{1,0:T(8,128)(2,1)S(1)}, bf16[144,256]{1,0:T(8,128)(2,1)S(1)}, u32[]{:S(2)}, u32[]{:S(2)}) collective-permute-start(bf16[144,256]{1,0:T(8,128)(2,1)S(1)} %get-tuple-element.100), channel_id=1, source_target_pairs={{0,2},{1,3},{2,0},{3,1},{4,6},{5,7},{6,4},{7,5},{8,10},{9,11},{10,... | collective-permute-start | bytes 221192 | tf_op jit(solution)/shard_map/ppermute | solution.py:478
  70.8 8.3 %collective-permute-start.17 = (bf16[144,256]{1,0:T(8,128)(2,1)S(1)}, bf16[144,256]{1,0:T(8,128)(2,1)S(1)}, u32[]{:S(2)}, u32[]{:S(2)}) collective-permute-start(bf16[144,256]{1,0:T(8,128)(2,1)S(1)} %get-tuple-element.101), channel_id=1, source_target_pairs={{0,1},{1,2},{2,3},{3,0},{4,5},{5,6},{6,7},{7,4},{8,9},{9,10},{10,1... | collective-permute-start | bytes 221192 | tf_op jit(solution)/shard_map/ppermute | solution.py:478
  80.0 1.2 %collective-permute-start.21 = (f32[2,512]{1,0:T(2,128)S(1)}, f32[2,512]{1,0:T(2,128)S(1)}, u32[]{:S(2)}, u32[]{:S(2)}) collective-permute-start(f32[2,512]{1,0:T(2,128)S(1)} %get-tuple-element.118.gains_ref), channel_id=1, source_target_pairs={{0,4},{4,0},{8,12},{12,8},{16,20},{20,16},{24,28},{28,24},{1,5},{5... | collective-permute-start | bytes 12296 | tf_op jit(solution)/shard_map/ppermute | solution.py:475

commit v2 on v1

--- a/solution.py
+++ b/solution.py
@@ -138,28 +138,27 @@
                 return units
 
             units = lax.fori_loop(0, count_chip, collect, units)
+            if start is not None:
+                base = ENTRY * (start + units)
+                table[base] = turn_q
+                table[base + 1] = tile_at
+                table[base + 2] = 0
+                table[base + 3] = TILE
+            units = 2 * ((units + 1) // 2)
             if count_at is not None:
                 counts[count_at + tile_at] = units - before
             return units
 
         return lax.fori_loop(*steps, query_step, units)
 
-    def close(start, units):
-        base = ENTRY * (start + units)
-        table[base] = 0
-        table[base + 1] = 0
-        table[base + 2] = 0
-        table[base + 3] = TILE
-        return (units + 1) // 2
-
     def steps_of(units):
-        return (units + 1) // 2
+        return units // 2
 
     none = jnp.int32(0)
     sibling = place_pb ^ 1
     every = (0, count_ka)
-    other = close(2, walk(2, place_pb, sibling, every, none, 2 * count_ka))
-    own = close(own_at, walk(own_at, place_pb, place_pb, every, none, 0))
+    other = steps_of(walk(2, place_pb, sibling, every, none, 2 * count_ka))
+    own = steps_of(walk(own_at, place_pb, place_pb, every, none, 0))
     walk(None, sibling, sibling, every, none, count_ka)
     sibling_other = steps_of(walk(None, sibling, place_pb, every, none))
 
@@ -246,7 +245,8 @@
 
     reach = (lax.broadcasted_iota(jnp.int32, (TILE, TILE), 1)
              - lax.broadcasted_iota(jnp.int32, (TILE, TILE), 0))
-    reach = jnp.concatenate([reach, reach], axis=1)
+    reach = jnp.concatenate([jnp.concatenate([reach, reach], axis=1)] * 2, axis=0)
+    lower = lax.broadcasted_iota(jnp.int32, (2 * TILE, 2 * TILE), 0) < TILE
 
     def run(start, refs, first, last):
         keys, values, keys_t, key_sum, value_sum = refs
@@ -257,47 +257,43 @@
                 [heads_ref[kind, rows, pl.ds(head * HEAD_DIM, HEAD_DIM)] for head in heads], axis=0
             )
 
-        def unit_step(at, carry):
-            terms = []
-            for lane in range(2):
-                base = ENTRY * (start + 2 * at + lane)
-                turn_q, tile_at, key_at = table[base], table[base + 1], table[base + 2]
-                slot = lax.rem(place_ka - tile_at + count_ka, count_ka)
-                allowed = reach >= table[base + 3]
-                for head in range(0, heads_dev, 2):
-                    part = pl.ds(head * HEAD_DIM, 2 * HEAD_DIM)
-                    both = (head, head + 1)
-                    scores = lax.dot_general(
-                        keys[key_at], heads_of(0, tile_at, both), LAST_DIMS, preferred_element_type=F32
-                    )
-                    dweights = lax.dot_general(
-                        values[key_at], heads_of(1, tile_at, both), LAST_DIMS, preferred_element_type=F32
-                    )
-                    lse_row, delta_row = [
-                        jnp.concatenate(
-                            [lse_delta[slot, number:number + 1, lanes] for number in both], axis=1
-                        )
-                        for lanes in (slice(0, TILE), slice(TILE, 2 * TILE))
-                    ]
-                    weights = jnp.exp2(scores * (score_scale * LOG2E) - lse_row)
-                    weights = jnp.where(allowed, weights, 0.0)
-                    weights_low[lane, :, part] = weights.astype(BF16)
-                    dscores_low[lane, :, part] = (weights * (dweights - delta_row)).astype(BF16)
-                every = range(heads_dev)
-                terms.append((
-                    turn_q,
-                    key_at,
-                    jnp.dot(weights_low[lane], heads_of(1, tile_at, every), preferred_element_type=F32),
-                    jnp.dot(dscores_low[lane], heads_of(0, tile_at, every), preferred_element_type=F32),
-                    jnp.dot(keys_t[key_at], dscores_low[lane], preferred_element_type=F32),
-                ))
-            for turn_q, key_at, value_term, key_term, dq_term in terms:
-                value_sum[key_at] += value_term
-                key_sum[key_at] += key_term
-                dq_sum[turn_q] += dq_term
+        def pair_step(at, carry):
+            base = ENTRY * (start + 2 * at)
+            turn_q, tile_at, one = table[base], table[base + 1], table[base + 2]
+            two = table[base + ENTRY + 2]
+            slot = lax.rem(place_ka - tile_at + count_ka, count_ka)
+            allowed = reach >= jnp.where(lower, table[base + 3], table[base + ENTRY + 3])
+            key_pair = jnp.concatenate([keys[one], keys[two]], axis=0)
+            value_pair = jnp.concatenate([values[one], values[two]], axis=0)
+            key_turn = jnp.concatenate([keys_t[one], keys_t[two]], axis=1)
+            for head in range(0, heads_dev, 2):
+                part = pl.ds(head * HEAD_DIM, 2 * HEAD_DIM)
+                both = (head, head + 1)
+                scores = lax.dot_general(
+                    key_pair, heads_of(0, tile_at, both), LAST_DIMS, preferred_element_type=F32
+                )
+                dweights = lax.dot_general(
+                    value_pair, heads_of(1, tile_at, both), LAST_DIMS, preferred_element_type=F32
+                )
+                lse_row, delta_row = [
+                    jnp.concatenate([lse_delta[slot, number:number + 1, lanes] for number in both], axis=1)
+                    for lanes in (slice(0, TILE), slice(TILE, 2 * TILE))
+                ]
+                weights = jnp.exp2(scores * (score_scale * LOG2E) - lse_row)
+                weights = jnp.where(allowed, weights, 0.0)
+                weights_low[:, part] = weights.astype(BF16)
+                dscores_low[:, part] = (weights * (dweights - delta_row)).astype(BF16)
+            every = range(heads_dev)
+            value_term = jnp.dot(weights_low[...], heads_of(1, tile_at, every), preferred_element_type=F32)
+            key_term = jnp.dot(dscores_low[...], heads_of(0, tile_at, every), preferred_element_type=F32)
+            dq_sum[turn_q] += jnp.dot(key_turn, dscores_low[...], preferred_element_type=F32)
+            value_sum[one] += value_term[:TILE]
+            key_sum[one] += key_term[:TILE]
+            value_sum[two] += value_term[TILE:]
+            key_sum[two] += key_term[TILE:]
             return carry
 
-        lax.fori_loop(first, last, unit_step, 0)
+        lax.fori_loop(first, last, pair_step, 0)
 
     own_at = own_start(count_chip * count_ka, count_ka)
     if stage == 0:
@@ -536,8 +532,8 @@
             out_shape=outs,
             scratch_shapes=scratch + [
                 VMEM((count_ka, head_rows(heads_dev), 2 * TILE), F32),
-                VMEM((2, TILE, width), BF16),
-                VMEM((2, TILE, width), BF16),
+                VMEM((2 * TILE, width), BF16),
+                VMEM((2 * TILE, width), BF16),
             ],
             compiler_params=params(14 + key_tiles * 11 // 16),
             cost_estimate=pl.CostEstimate(

time: 82.4 us -> 81.8 us (level)
  Pallas kernels: 32.2 us -> 29.3 us
  waiting for transfers between devices: 24.3 us -> 26.1 us
    pallas_call x4, Pallas kernels: 20.4 us -> 17.4 us  [attend(): pl.pallas_call(functools.partial(attention_kernel, (count_chip, count_ka,...]
    ppermute x12, waiting for transfers between devices: 11.7 us -> 12.9 us  [swap(): lax.ppermute(array, 'pb', [(at, at ^ number) for at in range(count_pb)])]
  transfers between devices with their start and end apart: 22 -> 22, of which waited for: 10 -> 9; matrix products, arithmetic and copies ran while one was open for 0% -> 0% of each run, Pallas kernels for 26% -> 26%
where the time goes in v2:
time: 81.8 us; the launch traced here: 81 us
  Pallas kernels  29.3 us (36%)
  waiting for transfers between devices  26.1 us (32%)
  starting transfers between devices  24 us (29%)
  between operations  0.85 us (1%)
    pallas_call x4, Pallas kernels, attend(): pl.pallas_call(functools.partial(attention_kernel, (count_chip, count_ka,...  17.4 us
    ppermute x10, starting transfers between devices, turn(): lax.ppermute(array, 'ka', [(at, (at + step) % count_ka) for at in range(c...  16.2 us
    ppermute x10, waiting for transfers between devices, turn(): lax.ppermute(array, 'ka', [(at, (at + step) % count_ka) for at in range(c...  13.3 us
    ppermute x12, waiting for transfers between devices, swap(): lax.ppermute(array, 'pb', [(at, at ^ number) for at in range(count_pb)])  12.9 us
    ppermute x12, starting transfers between devices, swap(): lax.ppermute(array, 'pb', [(at, at ^ number) for at in range(count_pb)])  7.88 us
    pallas_call x1, Pallas kernels, shards(): pl.pallas_call(functools.partial(plan_kernel, (count_chip, count_ka, orde...  4.27 us
    pallas_call x1, Pallas kernels, shards(): pl.pallas_call(functools.partial(prepare_kernel, (count_ka, heads, heads_...  2.79 us
  transfers between devices with their start and end apart: 22, of which 9 were waited for; matrix products, arithmetic and copies ran while one was open for 0% of the time, Pallas kernels for 26%

profile of v2, /device:TPU:0, one launch (start us, length us, event | category | flops | bytes accessed | tf_op | source)
XLA Modules:
  0.0 81.0 jit_solution(12386386527528141298)
XLA Ops:
  0.6 2.8 %prepare.1 = (bf16[144,256]{1,0:T(8,128)(2,1)}, bf16[144,256]{1,0:T(8,128)(2,1)}, bf16[144,256]{1,0:T(8,128)(2,1)}, bf16[144,256]{1,0:T(8,128)(2,1)}) custom-call(bf16[128,512]{1,0:T(8,128)(2,1)} %key_ref.1, bf16[128,512]{1,0:T(8,128)(2,1)} %value_ref.1, bf16[128,4096]{1,0:T(8,128)(2,1)} %attn_ref.1, bf16[512,4096]{1,0:T(8,128)(2,1)} %grads_ref.3, ...), custom_call_target="tpu_custom_call" | custom-call | tf_op jit(solution)/shard_map/prepare/pallas_call | solution.py:476
  3.4 3.1 %collective-permute-start = (bf16[144,256]{1,0:T(8,128)(2,1)}, bf16[144,256]{1,0:T(8,128)(2,1)S(1)}, u32[]{:S(2)}, u32[]{:S(2)}) collective-permute-start(bf16[144,256]{1,0:T(8,128)(2,1)} %get-tuple-element.64), channel_id=1, source_target_pairs={{0,1},{1,2},{2,3},{3,0},{4,5},{5,6},{6,7},{7,4},{8,9},{9,10},{10,1... | collective-permute-start | bytes 221192 | tf_op jit(solution)/shard_map/ppermute | solution.py:474
  6.5 2.6 %collective-permute-start.1 = (bf16[144,256]{1,0:T(8,128)(2,1)}, bf16[144,256]{1,0:T(8,128)(2,1)S(1)}, u32[]{:S(2)}, u32[]{:S(2)}) collective-permute-start(bf16[144,256]{1,0:T(8,128)(2,1)} %get-tuple-element.65), channel_id=1, source_target_pairs={{0,2},{1,3},{2,0},{3,1},{4,6},{5,7},{6,4},{7,5},{8,10},{9,11},{10,... | collective-permute-start | bytes 221192 | tf_op jit(solution)/shard_map/ppermute | solution.py:474
  9.1 1.3 %collective-permute-start.2 = (bf16[144,256]{1,0:T(8,128)(2,1)}, bf16[144,256]{1,0:T(8,128)(2,1)S(1)}, u32[]{:S(2)}, u32[]{:S(2)}) collective-permute-start(bf16[144,256]{1,0:T(8,128)(2,1)} %get-tuple-element.66), channel_id=1, source_target_pairs={{0,3},{1,0},{2,1},{3,2},{4,7},{5,4},{6,5},{7,6},{8,11},{9,8},{10,9... | collective-permute-start | bytes 221192 | tf_op jit(solution)/shard_map/ppermute | solution.py:474
  10.4 0.0 copy-start.3
  10.4 0.0 copy-start
  10.5 0.0 copy-start.1
  10.5 1.6 %own_heads.1.rest_3_.rest_1_ = bf16[2,512,1024]{2,1,0:T(8,128)(2,1)S(1)} custom-call(bf16[512,4096]{1,0:T(8,128)(2,1)} %queries_ref, bf16[512,4096]{1,0:T(8,128)(2,1)} %grads_ref.3), custom_call_target="tpu_custom_call" | custom-call | bytes 4194304 | tf_op jit(solution)/shard_map/own_heads/pallas_call | solution.py:491
  12.1 0.0 collective-permute-done
  12.1 2.2 %collective-permute-done.1 = bf16[144,256]{1,0:T(8,128)(2,1)S(1)} collective-permute-done((bf16[144,256]{1,0:T(8,128)(2,1)}, bf16[144,256]{1,0:T(8,128)(2,1)S(1)}, u32[]{:S(2)}, u32[]{:S(2)}) %collective-permute-start.1) | collective-permute-done | bytes 73760 | tf_op jit(solution)/shard_map/ppermute | solution.py:474
  14.3 0.2 collective-permute-done.2
  14.5 0.0 copy-done.3
  14.6 2.5 %collective-permute-start.8 = (bf16[512,256]{1,0:T(8,128)(2,1)S(1)}, bf16[512,256]{1,0:T(8,128)(2,1)S(1)}, u32[]{:S(2)}, u32[]{:S(2)}) collective-permute-start(bf16[512,256]{1,0:T(8,128)(2,1)S(1)} %pad_maximum_fusion.rest_5_.rest_0_), channel_id=1, source_target_pairs={{0,24},{4,28},{8,16},{12,20},{16,8},{20,12},{24,0},{28,4},{1,25},{... | collective-permute-start | bytes 786440 | tf_op jit(solution)/shard_map/ppermute | solution.py:471
  17.1 0.5 collective-permute-start.6
  17.6 0.5 collective-permute-start.4
  18.1 0.1 collective-permute-start.3
  18.2 4.3 %plan.1.rest_0_ = s32[528]{0:T(1024)} custom-call(s32[32]{0:T(128)} %order_ref, s32[32]{0:T(128)} %doc_ref.1, s32[32,32]{1,0:T(8,128)} %mask_ref.1), custom_call_target="tpu_custom_call" | custom-call | bytes 4194304 | tf_op jit(solution)/shard_map/plan/pallas_call | solution.py:517
  22.5 2.3 %collective-permute-done.8.rest_8_.rest_3_ = bf16[512,256]{1,0:T(8,128)(2,1)S(1)} collective-permute-done((bf16[512,256]{1,0:T(8,128)(2,1)S(1)}, bf16[512,256]{1,0:T(8,128)(2,1)S(1)}, u32[]{:S(2)}, u32[]{:S(2)}) %collective-permute-start.8) | collective-permute-done | bytes 262176 | tf_op jit(solution)/shard_map/ppermute | solution.py:471
  24.8 0.0 collective-permute-start.9
  24.8 4.3 %collective-permute-done.6.rest_7_.rest_2_ = bf16[512,256]{1,0:T(8,128)(2,1)S(1)} collective-permute-done((bf16[512,256]{1,0:T(8,128)(2,1)S(1)}, bf16[512,256]{1,0:T(8,128)(2,1)S(1)}, u32[]{:S(2)}, u32[]{:S(2)}) %collective-permute-start.6) | collective-permute-done | bytes 262176 | tf_op jit(solution)/shard_map/ppermute | solution.py:471
  29.1 0.0 collective-permute-start.7
  29.1 0.0 collective-permute-done.4.rest_6_.rest_1_
  29.1 0.5 collective-permute-start.5
  29.6 0.0 copy-done
  29.6 0.0 copy-done.1
  29.6 0.0 copy-start.2
  29.6 0.7 copy-done.2
  30.3 3.6 %attention_first.1 = (f32[4,128,1024]{2,1,0:T(8,128)S(1)}, bf16[16,128,128]{2,1,0:T(8,128)(2,1)S(1)}, bf16[16,128,128]{2,1,0:T(8,128)(2,1)S(1)}, bf16[16,128,128...) custom-call(s32[528]{0:T(1024)S(1)} %copy-done.2, f32[1,512]{1,0:T(1,128)S(1)} %bitcast.4, ...), custom_call_target="tpu_custom_call" | custom-call | flops 5368709120 | bytes 1048576 | tf_op jit(solution)/shard_map/attention_first/pallas_call | solution.py:528
  33.9 0.0 collective-permute-done.3.rest_5_
  33.9 0.0 collective-permute-done.9.rest_8_
  33.9 0.0 collective-permute-done.7.rest_7_
  33.9 0.0 collective-permute-done.5.rest_6_
  33.9 4.4 %attention_leaving.1 = (f32[4,128,1024]{2,1,0:T(8,128)S(1)}, bf16[128,512]{1,0:T(8,128)(2,1)S(1)}, bf16[128,512]{1,0:T(8,128)(2,1)S(1)}, bf16[16,128,128]{2,1,0:...) custom-call(s32[528]{0:T(1024)S(1)} %copy-done.2, ...), custom_call_target="tpu_custom_call" | custom-call | flops 5368709120 | bytes 1048576 | tf_op jit(solution)/shard_map/attention_leaving/pallas_call | solution.py:528
  38.3 1.3 %collective-permute-start.10 = (bf16[128,512]{1,0:T(8,128)(2,1)S(1)}, bf16[128,512]{1,0:T(8,128)(2,1)S(1)}, u32[]{:S(2)}, u32[]{:S(2)}) collective-permute-start(bf16[128,512]{1,0:T(8,128)(2,1)S(1)} %get-tuple-element.92), channel_id=1, source_target_pairs={{0,2},{1,3},{2,0},{3,1},{4,6},{5,7},{6,4},{7,5},{8,10},{9,11},{10,... | collective-permute-start | bytes 393224 | tf_op jit(solution)/shard_map/ppermute | solution.py:474
  39.6 6.9 %attention_other.1 = (f32[4,128,1024]{2,1,0:T(8,128)S(1)}, f32[16,128,128]{2,1,0:T(8,128)S(1)}, f32[16,128,128]{2,1,0:T(8,128)S(1)}, bf16[2048,256]{1,0:T(8,128)(2,1)S(1)}, bf16[128,1024]{1,0:T(8,128)(2,1)S(1)}) custom-call(s32[528]{0:T(1024)S(1)} %copy-done.2, bf16[2,512,1024]{2,1,0:T(8,128)(2,1)S(1)} %own_heads.1.rest_3_.rest_1_, ...), custom_call_target="tpu_custom_call" | custom-call | flops 5368709120 | bytes 1048576 | tf_op jit(solution)/shard_map/attention_other/pallas_call | solution.py:528
  46.5 0.0 collective-permute-done.10.rest_0_
  46.5 0.1 collective-permute-start.11
  46.6 1.8 %collective-permute-start.19 = (bf16[128,512]{1,0:T(8,128)(2,1)S(1)}, bf16[128,512]{1,0:T(8,128)(2,1)S(1)}, u32[]{:S(2)}, u32[]{:S(2)}) collective-permute-start(bf16[128,512]{1,0:T(8,128)(2,1)S(1)} %get-tuple-element.106), channel_id=1, source_target_pairs={{0,2},{1,3},{2,0},{3,1},{4,6},{5,7},{6,4},{7,5},{8,10},{9,11},{10,... | collective-permute-start | bytes 393224 | tf_op jit(solution)/shard_map/ppermute | solution.py:474
  48.4 2.1 %collective-permute-start.18 = (bf16[128,1024]{1,0:T(8,128)(2,1)S(1)}, bf16[128,1024]{1,0:T(8,128)(2,1)S(1)}, u32[]{:S(2)}, u32[]{:S(2)}) collective-permute-start(bf16[128,1024]{1,0:T(8,128)(2,1)S(1)} %get-tuple-element.105), channel_id=1, source_target_pairs={{0,1},{1,2},{2,3},{3,0},{4,5},{5,6},{6,7},{7,4},{8,9},{9,10},{10,1... | collective-permute-start | bytes 786440 | tf_op jit(solution)/shard_map/ppermute | solution.py:474
  50.5 2.6 %attention_own.1 = (bf16[128,1024]{1,0:T(8,128)(2,1)S(1)}, bf16[128,1024]{1,0:T(8,128)(2,1)S(1)}, f32[16,128,128]{2,1,0:T(8,128)S(1)}, f32[16,128,128]{2,1,0:T(8,128)S(1)}) custom-call(s32[528]{0:T(1024)S(1)} %copy-done.2, bf16[2,512,1024]{2,1,0:T(8,128)(2,1)S(1)} %own_heads.1.rest_3_.rest_1_, bf16[64,256]{1,0:T(8,128)(2,1)S(1)} %pad_maximum_fusion.1.rest_4_.rest_2_, ...), custom_call_target="tpu_custom_call" | custom-call | flops 5368709120 | bytes 1048576 | tf_op jit(solution)/shard_map/attention_own/pallas_call | solution.py:528
  53.1 0.0 collective-permute-done.11.kv_back
  53.1 0.5 merge.1
  53.6 0.3 collective-permute-start.12
  53.9 0.0 collective-permute-start.13
  53.9 3.3 %collective-permute-start.14 = (bf16[528,256]{1,0:T(8,128)(2,1)S(1)}, bf16[528,256]{1,0:T(8,128)(2,1)S(1)}, u32[]{:S(2)}, u32[]{:S(2)}) collective-permute-start(bf16[528,256]{1,0:T(8,128)(2,1)S(1)} %get-tuple-element.97), channel_id=1, source_target_pairs={{0,24},{4,28},{8,16},{12,20},{16,8},{20,12},{24,0},{28,4},{1,25},{... | collective-permute-start | bytes 811016 | tf_op jit(solution)/shard_map/ppermute | solution.py:471
  57.1 4.7 %collective-permute-done.19.rest_1_ = bf16[128,512]{1,0:T(8,128)(2,1)S(1)} collective-permute-done((bf16[128,512]{1,0:T(8,128)(2,1)S(1)}, bf16[128,512]{1,0:T(8,128)(2,1)S(1)}, u32[]{:S(2)}, u32[]{:S(2)}) %collective-permute-start.19) | collective-permute-done | bytes 131104 | tf_op jit(solution)/shard_map/ppermute | solution.py:474
  61.8 0.0 collective-permute-done.18.rest_2_
  61.8 0.5 collective-permute-start.20
  62.3 0.4 collective-permute-done.12.rest_1_
  62.7 4.8 %collective-permute-done.13.rest_2_ = bf16[528,256]{1,0:T(8,128)(2,1)S(1)} collective-permute-done((bf16[528,256]{1,0:T(8,128)(2,1)S(1)}, bf16[528,256]{1,0:T(8,128)(2,1)S(1)}, u32[]{:S(2)}, u32[]{:S(2)}) %collective-permute-start.13) | collective-permute-done | bytes 270368 | tf_op jit(solution)/shard_map/ppermute | solution.py:471
  67.5 0.0 collective-permute-done.14.rest_3_
  67.5 0.1 collect.1
  67.7 1.7 %collective-permute-start.15 = (bf16[144,256]{1,0:T(8,128)(2,1)S(1)}, bf16[144,256]{1,0:T(8,128)(2,1)S(1)}, u32[]{:S(2)}, u32[]{:S(2)}) collective-permute-start(bf16[144,256]{1,0:T(8,128)(2,1)S(1)} %get-tuple-element.99), channel_id=1, source_target_pairs={{0,3},{1,0},{2,1},{3,2},{4,7},{5,4},{6,5},{7,6},{8,11},{9,8},{10,9... | collective-permute-start | bytes 221192 | tf_op jit(solution)/shard_map/ppermute | solution.py:474
  69.4 0.0 collective-permute-start.16
  69.4 1.8 %collective-permute-start.17 = (bf16[144,256]{1,0:T(8,128)(2,1)S(1)}, bf16[144,256]{1,0:T(8,128)(2,1)S(1)}, u32[]{:S(2)}, u32[]{:S(2)}) collective-permute-start(bf16[144,256]{1,0:T(8,128)(2,1)S(1)} %get-tuple-element.101), channel_id=1, source_target_pairs={{0,1},{1,2},{2,3},{3,0},{4,5},{5,6},{6,7},{7,4},{8,9},{9,10},{10,1... | collective-permute-start | bytes 221192 | tf_op jit(solution)/shard_map/ppermute | solution.py:474
  71.2 0.0 collective-permute-done.20.rest_4_
  71.2 1.1 %place_queries.1 = bf16[128,4096]{1,0:T(8,128)(2,1)} custom-call(bf16[128,512]{1,0:T(8,128)(2,1)S(1)} %collective-permute-done.10.rest_0_, bf16[128,512]{1,0:T(8,128)(2,1)S(1)} %collective-permute-done.19.rest_1_, bf16[128,1024]{1,0:T(8,128)(2,1)S(1)} %collective-permute-done.18.rest_2_, bf16[128,1024]{1,0:T(8,128)(2,1)S(1)} %get-tuple-element.109.rest_3_, ...), custom_call_target="tpu_custom_call" | custom-call | bytes 2097152 | tf_op jit(solution)/shard_map/place_queries/pallas_call | solution.py:594
  72.3 0.0 collective-permute-done.15.rest_1_
  72.3 6.1 %collective-permute-done.16.rest_2_ = bf16[144,256]{1,0:T(8,128)(2,1)S(1)} collective-permute-done((bf16[144,256]{1,0:T(8,128)(2,1)S(1)}, bf16[144,256]{1,0:T(8,128)(2,1)S(1)}, u32[]{:S(2)}, u32[]{:S(2)}) %collective-permute-start.16) | collective-permute-done | bytes 73760 | tf_op jit(solution)/shard_map/ppermute | solution.py:474
  78.4 0.0 collective-permute-done.17.rest_3_
  78.4 0.8 %finish.1 = (bf16[128,512]{1,0:T(8,128)(2,1)}, bf16[128,512]{1,0:T(8,128)(2,1)}, f32[2,512]{1,0:T(2,128)S(1)}) custom-call(f32[1,512]{1,0:T(1,128)S(1)} %bitcast.7, f32[1,512]{1,0:T(1,128)S(1)} %bitcast.11, f32[144,256]{1,0:T(8,128)S(1)} %get-tuple-element.112.rest_0_, bf16[144,256]{1,0:T(8,128)(2,1)S(1)} %collective-permute-done.15.rest_1_, ...), custom_call_target="tpu_custom_call" | custom-call | tf_op jit(solution)/shard_map/finish/pallas_call | solution.py:605
  79.3 0.1 collective-permute-start.21
  79.4 1.1 %collective-permute-done.21.other_ref = f32[2,512]{1,0:T(2,128)S(1)} collective-permute-done((f32[2,512]{1,0:T(2,128)S(1)}, f32[2,512]{1,0:T(2,128)S(1)}, u32[]{:S(2)}, u32[]{:S(2)}) %collective-permute-start.21) | collective-permute-done | bytes 4128 | tf_op jit(solution)/shard_map/ppermute | solution.py:471
  80.4 0.6 add_gains.1
  (10 shorter events, 0.1 us)
Async XLA Ops:
  3.4 8.6 %collective-permute-start = (bf16[144,256]{1,0:T(8,128)(2,1)}, bf16[144,256]{1,0:T(8,128)(2,1)S(1)}, u32[]{:S(2)}, u32[]{:S(2)}) collective-permute-start(bf16[144,256]{1,0:T(8,128)(2,1)} %get-tuple-element.64), channel_id=1, source_target_pairs={{0,1},{1,2},{2,3},{3,0},{4,5},{5,6},{6,7},{7,4},{8,9},{9,10},{10,1... | collective-permute-start | bytes 221192 | tf_op jit(solution)/shard_map/ppermute | solution.py:474
  6.5 7.8 %collective-permute-start.1 = (bf16[144,256]{1,0:T(8,128)(2,1)}, bf16[144,256]{1,0:T(8,128)(2,1)S(1)}, u32[]{:S(2)}, u32[]{:S(2)}) collective-permute-start(bf16[144,256]{1,0:T(8,128)(2,1)} %get-tuple-element.65), channel_id=1, source_target_pairs={{0,2},{1,3},{2,0},{3,1},{4,6},{5,7},{6,4},{7,5},{8,10},{9,11},{10,... | collective-permute-start | bytes 221192 | tf_op jit(solution)/shard_map/ppermute | solution.py:474
  9.1 5.4 %collective-permute-start.2 = (bf16[144,256]{1,0:T(8,128)(2,1)}, bf16[144,256]{1,0:T(8,128)(2,1)S(1)}, u32[]{:S(2)}, u32[]{:S(2)}) collective-permute-start(bf16[144,256]{1,0:T(8,128)(2,1)} %get-tuple-element.66), channel_id=1, source_target_pairs={{0,3},{1,0},{2,1},{3,2},{4,7},{5,4},{6,5},{7,6},{8,11},{9,8},{10,9... | collective-permute-start | bytes 221192 | tf_op jit(solution)/shard_map/ppermute | solution.py:474
  10.4 4.0 %copy-start.3 = (bf16[144,256]{1,0:T(8,128)(2,1)S(1)}, bf16[144,256]{1,0:T(8,128)(2,1)}, u32[]{:S(2)}) copy-start(bf16[144,256]{1,0:T(8,128)(2,1)} %get-tuple-element.68) | copy-start | bytes 221188
  10.4 19.1 %copy-start = (f32[512]{0:T(512)S(1)}, f32[512]{0:T(512)}, u32[]{:S(2)}) copy-start(f32[512]{0:T(512)} %param.17) | copy-start | bytes 6148
  10.5 19.1 %copy-start.1 = (f32[512]{0:T(512)S(1)}, f32[512]{0:T(512)}, u32[]{:S(2)}) copy-start(f32[512]{0:T(512)} %param.18) | copy-start | bytes 6148
  14.6 10.2 %collective-permute-start.8 = (bf16[512,256]{1,0:T(8,128)(2,1)S(1)}, bf16[512,256]{1,0:T(8,128)(2,1)S(1)}, u32[]{:S(2)}, u32[]{:S(2)}) collective-permute-start(bf16[512,256]{1,0:T(8,128)(2,1)S(1)} %pad_maximum_fusion.rest_5_.rest_0_), channel_id=1, source_target_pairs={{0,24},{4,28},{8,16},{12,20},{16,8},{20,12},{24,0},{28,4},{1,25},{... | collective-permute-start | bytes 786440 | tf_op jit(solution)/shard_map/ppermute | solution.py:471
  17.1 12.0 %collective-permute-start.6 = (bf16[512,256]{1,0:T(8,128)(2,1)S(1)}, bf16[512,256]{1,0:T(8,128)(2,1)S(1)}, u32[]{:S(2)}, u32[]{:S(2)}) collective-permute-start(bf16[512,256]{1,0:T(8,128)(2,1)S(1)} %pad_maximum_fusion.rest_5_.rest_0_), channel_id=1, source_target_pairs={{0,16},{4,20},{8,24},{12,28},{16,0},{20,4},{24,8},{28,12},{1,17},{... | collective-permute-start | bytes 786440 | tf_op jit(solution)/shard_map/ppermute | solution.py:471
  17.6 11.5 %collective-permute-start.4 = (bf16[512,256]{1,0:T(8,128)(2,1)S(1)}, bf16[512,256]{1,0:T(8,128)(2,1)S(1)}, u32[]{:S(2)}, u32[]{:S(2)}) collective-permute-start(bf16[512,256]{1,0:T(8,128)(2,1)S(1)} %pad_maximum_fusion.rest_5_.rest_0_), channel_id=1, source_target_pairs={{0,8},{4,12},{8,0},{12,4},{16,24},{20,28},{24,16},{28,20},{1,9},{5... | collective-permute-start | bytes 786440 | tf_op jit(solution)/shard_map/ppermute | solution.py:471
  18.1 15.7 %collective-permute-start.3 = (bf16[512,256]{1,0:T(8,128)(2,1)S(1)}, bf16[512,256]{1,0:T(8,128)(2,1)S(1)}, u32[]{:S(2)}, u32[]{:S(2)}) collective-permute-start(bf16[512,256]{1,0:T(8,128)(2,1)S(1)} %pad_maximum_fusion.rest_5_.rest_0_), channel_id=1, source_target_pairs={{0,4},{4,0},{8,12},{12,8},{16,20},{20,16},{24,28},{28,24},{1,5},{5... | collective-permute-start | bytes 786440 | tf_op jit(solution)/shard_map/ppermute | solution.py:471
  24.8 9.1 %collective-permute-start.9 = (bf16[512,256]{1,0:T(8,128)(2,1)S(1)}, bf16[512,256]{1,0:T(8,128)(2,1)S(1)}, u32[]{:S(2)}, u32[]{:S(2)}) collective-permute-start(bf16[512,256]{1,0:T(8,128)(2,1)S(1)} %collective-permute-done.8.rest_8_.rest_3_), channel_id=1, source_target_pairs={{0,4},{4,0},{8,12},{12,8},{16,20},{20,16},{24,28},{28,24},{1,5},{5... | collective-permute-start | bytes 786440 | tf_op jit(solution)/shard_map/ppermute | solution.py:471
  29.1 4.8 %collective-permute-start.7 = (bf16[512,256]{1,0:T(8,128)(2,1)S(1)}, bf16[512,256]{1,0:T(8,128)(2,1)S(1)}, u32[]{:S(2)}, u32[]{:S(2)}) collective-permute-start(bf16[512,256]{1,0:T(8,128)(2,1)S(1)} %collective-permute-done.6.rest_7_.rest_2_), channel_id=1, source_target_pairs={{0,4},{4,0},{8,12},{12,8},{16,20},{20,16},{24,28},{28,24},{1,5},{5... | collective-permute-start | bytes 786440 | tf_op jit(solution)/shard_map/ppermute | solution.py:471
  29.1 4.8 %collective-permute-start.5 = (bf16[512,256]{1,0:T(8,128)(2,1)S(1)}, bf16[512,256]{1,0:T(8,128)(2,1)S(1)}, u32[]{:S(2)}, u32[]{:S(2)}) collective-permute-start(bf16[512,256]{1,0:T(8,128)(2,1)S(1)} %collective-permute-done.4.rest_6_.rest_1_), channel_id=1, source_target_pairs={{0,4},{4,0},{8,12},{12,8},{16,20},{20,16},{24,28},{28,24},{1,5},{5... | collective-permute-start | bytes 786440 | tf_op jit(solution)/shard_map/ppermute | solution.py:471
  29.6 0.7 copy-start.2
  38.3 8.2 %collective-permute-start.10 = (bf16[128,512]{1,0:T(8,128)(2,1)S(1)}, bf16[128,512]{1,0:T(8,128)(2,1)S(1)}, u32[]{:S(2)}, u32[]{:S(2)}) collective-permute-start(bf16[128,512]{1,0:T(8,128)(2,1)S(1)} %get-tuple-element.92), channel_id=1, source_target_pairs={{0,2},{1,3},{2,0},{3,1},{4,6},{5,7},{6,4},{7,5},{8,10},{9,11},{10,... | collective-permute-start | bytes 393224 | tf_op jit(solution)/shard_map/ppermute | solution.py:474
  46.5 6.6 %collective-permute-start.11 = (bf16[2048,256]{1,0:T(8,128)(2,1)S(1)}, bf16[2048,256]{1,0:T(8,128)(2,1)S(1)}, u32[]{:S(2)}, u32[]{:S(2)}) collective-permute-start(bf16[2048,256]{1,0:T(8,128)(2,1)S(1)} %get-tuple-element.93), channel_id=1, source_target_pairs={{0,4},{4,0},{8,12},{12,8},{16,20},{20,16},{24,28},{28,24},{1,5},{5... | collective-permute-start | bytes 3145736 | tf_op jit(solution)/shard_map/ppermute | solution.py:471
  46.6 15.2 %collective-permute-start.19 = (bf16[128,512]{1,0:T(8,128)(2,1)S(1)}, bf16[128,512]{1,0:T(8,128)(2,1)S(1)}, u32[]{:S(2)}, u32[]{:S(2)}) collective-permute-start(bf16[128,512]{1,0:T(8,128)(2,1)S(1)} %get-tuple-element.106), channel_id=1, source_target_pairs={{0,2},{1,3},{2,0},{3,1},{4,6},{5,7},{6,4},{7,5},{8,10},{9,11},{10,... | collective-permute-start | bytes 393224 | tf_op jit(solution)/shard_map/ppermute | solution.py:474
  48.4 13.5 %collective-permute-start.18 = (bf16[128,1024]{1,0:T(8,128)(2,1)S(1)}, bf16[128,1024]{1,0:T(8,128)(2,1)S(1)}, u32[]{:S(2)}, u32[]{:S(2)}) collective-permute-start(bf16[128,1024]{1,0:T(8,128)(2,1)S(1)} %get-tuple-element.105), channel_id=1, source_target_pairs={{0,1},{1,2},{2,3},{3,0},{4,5},{5,6},{6,7},{7,4},{8,9},{9,10},{10,1... | collective-permute-start | bytes 786440 | tf_op jit(solution)/shard_map/ppermute | solution.py:474
  53.6 9.1 %collective-permute-start.12 = (bf16[528,256]{1,0:T(8,128)(2,1)S(1)}, bf16[528,256]{1,0:T(8,128)(2,1)S(1)}, u32[]{:S(2)}, u32[]{:S(2)}) collective-permute-start(bf16[528,256]{1,0:T(8,128)(2,1)S(1)} %get-tuple-element.95), channel_id=1, source_target_pairs={{0,8},{4,12},{8,0},{12,4},{16,24},{20,28},{24,16},{28,20},{1,9},{5... | collective-permute-start | bytes 811016 | tf_op jit(solution)/shard_map/ppermute | solution.py:471
  53.9 13.7 %collective-permute-start.13 = (bf16[528,256]{1,0:T(8,128)(2,1)S(1)}, bf16[528,256]{1,0:T(8,128)(2,1)S(1)}, u32[]{:S(2)}, u32[]{:S(2)}) collective-permute-start(bf16[528,256]{1,0:T(8,128)(2,1)S(1)} %get-tuple-element.96), channel_id=1, source_target_pairs={{0,16},{4,20},{8,24},{12,28},{16,0},{20,4},{24,8},{28,12},{1,17},{... | collective-permute-start | bytes 811016 | tf_op jit(solution)/shard_map/ppermute | solution.py:471
  53.9 13.7 %collective-permute-start.14 = (bf16[528,256]{1,0:T(8,128)(2,1)S(1)}, bf16[528,256]{1,0:T(8,128)(2,1)S(1)}, u32[]{:S(2)}, u32[]{:S(2)}) collective-permute-start(bf16[528,256]{1,0:T(8,128)(2,1)S(1)} %get-tuple-element.97), channel_id=1, source_target_pairs={{0,24},{4,28},{8,16},{12,20},{16,8},{20,12},{24,0},{28,4},{1,25},{... | collective-permute-start | bytes 811016 | tf_op jit(solution)/shard_map/ppermute | solution.py:471
  61.8 9.3 %collective-permute-start.20 = (bf16[128,1024]{1,0:T(8,128)(2,1)S(1)}, bf16[128,1024]{1,0:T(8,128)(2,1)S(1)}, u32[]{:S(2)}, u32[]{:S(2)}) collective-permute-start(bf16[128,1024]{1,0:T(8,128)(2,1)S(1)} %get-tuple-element.110), channel_id=1, source_target_pairs={{0,3},{1,0},{2,1},{3,2},{4,7},{5,4},{6,5},{7,6},{8,11},{9,8},{10,9... | collective-permute-start | bytes 786440 | tf_op jit(solution)/shard_map/ppermute | solution.py:474
  67.7 4.6 %collective-permute-start.15 = (bf16[144,256]{1,0:T(8,128)(2,1)S(1)}, bf16[144,256]{1,0:T(8,128)(2,1)S(1)}, u32[]{:S(2)}, u32[]{:S(2)}) collective-permute-start(bf16[144,256]{1,0:T(8,128)(2,1)S(1)} %get-tuple-element.99), channel_id=1, source_target_pairs={{0,3},{1,0},{2,1},{3,2},{4,7},{5,4},{6,5},{7,6},{8,11},{9,8},{10,9... | collective-permute-start | bytes 221192 | tf_op jit(solution)/shard_map/ppermute | solution.py:474
  69.4 9.0 %collective-permute-start.16 = (bf16[144,256]{1,0:T(8,128)(2,1)S(1)}, bf16[144,256]{1,0:T(8,128)(2,1)S(1)}, u32[]{:S(2)}, u32[]{:S(2)}) collective-permute-start(bf16[144,256]{1,0:T(8,128)(2,1)S(1)} %get-tuple-element.100), channel_id=1, source_target_pairs={{0,2},{1,3},{2,0},{3,1},{4,6},{5,7},{6,4},{7,5},{8,10},{9,11},{10,... | collective-permute-start | bytes 221192 | tf_op jit(solution)/shard_map/ppermute | solution.py:474
  69.4 9.0 %collective-permute-start.17 = (bf16[144,256]{1,0:T(8,128)(2,1)S(1)}, bf16[144,256]{1,0:T(8,128)(2,1)S(1)}, u32[]{:S(2)}, u32[]{:S(2)}) collective-permute-start(bf16[144,256]{1,0:T(8,128)(2,1)S(1)} %get-tuple-element.101), channel_id=1, source_target_pairs={{0,1},{1,2},{2,3},{3,0},{4,5},{5,6},{6,7},{7,4},{8,9},{9,10},{10,1... | collective-permute-start | bytes 221192 | tf_op jit(solution)/shard_map/ppermute | solution.py:474
  79.3 1.2 %collective-permute-start.21 = (f32[2,512]{1,0:T(2,128)S(1)}, f32[2,512]{1,0:T(2,128)S(1)}, u32[]{:S(2)}, u32[]{:S(2)}) collective-permute-start(f32[2,512]{1,0:T(2,128)S(1)} %get-tuple-element.118.gains_ref), channel_id=1, source_target_pairs={{0,4},{4,0},{8,12},{12,8},{16,20},{20,16},{24,28},{28,24},{1,5},{5... | collective-permute-start | bytes 12296 | tf_op jit(solution)/shard_map/ppermute | solution.py:471

commit v3 on v2

--- a/solution.py
+++ b/solution.py
@@ -170,7 +170,7 @@
     for place in range(count_ka):
         first = jnp.maximum(first, sum(first_steps(place)))
         for core, others in enumerate((other, sibling_other)):
-            units = sum([counts[core * count_ka + (place + step) % count_ka] for step in order[:2]])
+            units = sum([counts[core * count_ka + (place + step) % count_ka] for step in order[:1]])
             second = jnp.maximum(second, others + steps_of(units))
     own_first, other_first = first_steps(place_ka)
     table[0] = own_first
@@ -195,12 +195,12 @@
     elif stage == 2:
         (dq_start, *own_start_refs), rest = rest[:6], rest[6:]
         other_refs, rest = rest[:5], rest[5:]
-        (dq_sum, *own_sums, kv_other, dq_out, other_key_sum, other_value_sum), rest = rest[:7], rest[7:]
+        (dq_sum, *own_sums, kv_other, other_key_sum, other_value_sum), rest = rest[:6], rest[6:]
         own = own_start_refs[:3] + own_sums
         other = other_refs[:3] + (other_key_sum, other_value_sum)
     else:
         (dq_start, *own_start_refs), rest = rest[:6], rest[6:]
-        dq_outs, rest = rest[:count_ka - 2], rest[count_ka - 2:]
+        dq_outs, rest = rest[:count_ka - 1], rest[count_ka - 1:]
         (*own_sums, dq_sum), rest = rest[:3], rest[3:]
         own = own_start_refs[:3] + own_sums
     lse_delta, weights_low, dscores_low = rest
@@ -306,14 +306,13 @@
     elif stage == 2:
         run(2, other, table[ENTRY], table[ENTRY + 1])
         run(own_at, own, table[0], table[1])
-        dq_out[...] = (dq_sum[1] * score_scale).astype(BF16)
         for local in range(count_chip * count_ka):
             part = pl.ds(local * TILE, TILE)
             kv_other[part, :HEAD_DIM] = (other_key_sum[local] * score_scale).astype(BF16)
             kv_other[part, HEAD_DIM:] = other_value_sum[local].astype(BF16)
     else:
         run(own_at, own, table[1], table[2])
-        for number, dq_out in enumerate(dq_outs, 2):
+        for number, dq_out in enumerate(dq_outs, 1):
             dq_out[...] = (dq_sum[number] * score_scale).astype(BF16)
 
 
@@ -510,9 +509,8 @@
     key_shape = jax.ShapeDtypeStruct((key_tiles, TILE, HEAD_DIM), BF16)
     kv_shape = (query_rows + SPARE, 2 * HEAD_DIM)
     half = count_ka // 2
-    early = (half, 1)
-    late = tuple(step for step in range(count_ka) if step not in early)
-    order = early + late
+    late = tuple(step for step in range(count_ka) if step != half)
+    order = (half,) + late
     entries = own_start(key_tiles, count_ka) + 1 + count_ka * key_tiles
     table = pl.pallas_call(
         functools.partial(plan_kernel, (count_chip, count_ka, order)),
@@ -552,16 +550,15 @@
     )
     dq_parts = [None] * count_ka
     dq_halves, other = [turn(part, half) for part in other[:2]], other[2:]
-    dq_sum, *own[3:], kv_other, dq_second = attend(
+    dq_sum, *own[3:], kv_other = attend(
         2,
         [dq_sums] + [sum_shape] * 2
-        + [jax.ShapeDtypeStruct((key_tiles * TILE, 2 * HEAD_DIM), BF16), dq_tile],
+        + [jax.ShapeDtypeStruct((key_tiles * TILE, 2 * HEAD_DIM), BF16)],
         [VMEM(sum_shape.shape, F32)] * 2,
         own_queries, own_stats, dq_sum, *own, *other,
     )
     kv_other, dq_halves[0] = lax.optimization_barrier((kv_other, dq_halves[0]))
     kv_back = swap(kv_other, 1)
-    dq_parts[1] = turn(dq_second, 1)
     *dq_late, key_sum, value_sum = attend(
         3, [dq_tile] * len(late) + [sum_shape] * 2, [VMEM(dq_sums.shape, F32)],
         own_queries, own_stats, dq_sum, *own,
@@ -575,7 +572,7 @@
         name="merge",
     )(key_sum, value_sum, kv_back, *blocks)
     kv_parts = [kv_own[0]] + [swap(kv_own[number], 2 * number) for number in range(1, count_chip)]
-    dq_late, dq_parts[1], dq_halves[1] = lax.optimization_barrier((dq_late, dq_parts[1], dq_halves[1]))
+    dq_late, dq_halves[1] = lax.optimization_barrier((dq_late, dq_halves[1]))
     for step, tile in zip(late, dq_late):
         dq_parts[step] = turn(tile, step) if step else tile
 

time: 81.8 us -> 80.9 us (0.989)
  waiting for transfers between devices: 26.1 us -> 20.9 us
  Pallas kernels: 29.3 us -> 31.7 us
  starting transfers between devices: 24 us -> 26.1 us
    ppermute x10, waiting for transfers between devices: 13.3 us -> 7.31 us  [turn(): lax.ppermute(array, 'ka', [(at, (at + step) % count_ka) for at in range(c...]
    pallas_call x4, Pallas kernels: 17.4 us -> 19.9 us  [attend(): pl.pallas_call(functools.partial(attention_kernel, (count_chip, count_ka,...]
    ppermute x10, starting transfers between devices: 16.2 us -> 18.4 us  [turn(): lax.ppermute(array, 'ka', [(at, (at + step) % count_ka) for at in range(c...]
  transfers between devices with their start and end apart: 22 -> 22, of which waited for: 9 -> 8; matrix products, arithmetic and copies ran while one was open for 0% -> 0% of each run, Pallas kernels for 26% -> 28%
where the time goes in v3:
time: 80.9 us; the launch traced here: 80.3 us
  Pallas kernels  31.7 us (39%)
  starting transfers between devices  26.1 us (32%)
  waiting for transfers between devices  20.9 us (26%)
  between operations  0.86 us (1%)
    pallas_call x4, Pallas kernels, attend(): pl.pallas_call(functools.partial(attention_kernel, (count_chip, count_ka,...  19.9 us
    ppermute x10, starting transfers between devices, turn(): lax.ppermute(array, 'ka', [(at, (at + step) % count_ka) for at in range(c...  18.4 us
    ppermute x12, waiting for transfers between devices, swap(): lax.ppermute(array, 'pb', [(at, at ^ number) for at in range(count_pb)])  13.6 us
    ppermute x12, starting transfers between devices, swap(): lax.ppermute(array, 'pb', [(at, at ^ number) for at in range(count_pb)])  7.75 us
    ppermute x10, waiting for transfers between devices, turn(): lax.ppermute(array, 'ka', [(at, (at + step) % count_ka) for at in range(c...  7.31 us
    pallas_call x1, Pallas kernels, shards(): pl.pallas_call(functools.partial(plan_kernel, (count_chip, count_ka, orde...  4.25 us
    pallas_call x1, Pallas kernels, shards(): pl.pallas_call(functools.partial(prepare_kernel, (count_ka, heads, heads_...  2.79 us
  transfers between devices with their start and end apart: 22, of which 8 were waited for; matrix products, arithmetic and copies ran while one was open for 0% of the time, Pallas kernels for 28%

profile of v3, /device:TPU:0, one launch (start us, length us, event | category | flops | bytes accessed | tf_op | source)
XLA Modules:
  0.0 80.3 jit_solution(17211265859615274727)
XLA Ops:
  0.6 2.8 %prepare.1 = (bf16[144,256]{1,0:T(8,128)(2,1)}, bf16[144,256]{1,0:T(8,128)(2,1)}, bf16[144,256]{1,0:T(8,128)(2,1)}, bf16[144,256]{1,0:T(8,128)(2,1)}) custom-call(bf16[128,512]{1,0:T(8,128)(2,1)} %key_ref.1, bf16[128,512]{1,0:T(8,128)(2,1)} %value_ref.1, bf16[128,4096]{1,0:T(8,128)(2,1)} %attn_ref.1, bf16[512,4096]{1,0:T(8,128)(2,1)} %grads_ref.3, ...), custom_call_target="tpu_custom_call" | custom-call | tf_op jit(solution)/shard_map/prepare/pallas_call | solution.py:475
  3.4 3.1 %collective-permute-start = (bf16[144,256]{1,0:T(8,128)(2,1)}, bf16[144,256]{1,0:T(8,128)(2,1)S(1)}, u32[]{:S(2)}, u32[]{:S(2)}) collective-permute-start(bf16[144,256]{1,0:T(8,128)(2,1)} %get-tuple-element.64), channel_id=1, source_target_pairs={{0,1},{1,2},{2,3},{3,0},{4,5},{5,6},{6,7},{7,4},{8,9},{9,10},{10,1... | collective-permute-start | bytes 221192 | tf_op jit(solution)/shard_map/ppermute | solution.py:473
  6.5 2.6 %collective-permute-start.1 = (bf16[144,256]{1,0:T(8,128)(2,1)}, bf16[144,256]{1,0:T(8,128)(2,1)S(1)}, u32[]{:S(2)}, u32[]{:S(2)}) collective-permute-start(bf16[144,256]{1,0:T(8,128)(2,1)} %get-tuple-element.65), channel_id=1, source_target_pairs={{0,2},{1,3},{2,0},{3,1},{4,6},{5,7},{6,4},{7,5},{8,10},{9,11},{10,... | collective-permute-start | bytes 221192 | tf_op jit(solution)/shard_map/ppermute | solution.py:473
  9.1 1.3 %collective-permute-start.2 = (bf16[144,256]{1,0:T(8,128)(2,1)}, bf16[144,256]{1,0:T(8,128)(2,1)S(1)}, u32[]{:S(2)}, u32[]{:S(2)}) collective-permute-start(bf16[144,256]{1,0:T(8,128)(2,1)} %get-tuple-element.66), channel_id=1, source_target_pairs={{0,3},{1,0},{2,1},{3,2},{4,7},{5,4},{6,5},{7,6},{8,11},{9,8},{10,9... | collective-permute-start | bytes 221192 | tf_op jit(solution)/shard_map/ppermute | solution.py:473
  10.4 0.0 copy-start.3
  10.4 0.0 copy-start
  10.5 0.0 copy-start.1
  10.5 1.6 %own_heads.1.rest_3_.rest_1_ = bf16[2,512,1024]{2,1,0:T(8,128)(2,1)S(1)} custom-call(bf16[512,4096]{1,0:T(8,128)(2,1)} %queries_ref, bf16[512,4096]{1,0:T(8,128)(2,1)} %grads_ref.3), custom_call_target="tpu_custom_call" | custom-call | bytes 4194304 | tf_op jit(solution)/shard_map/own_heads/pallas_call | solution.py:490
  12.1 0.0 collective-permute-done
  12.1 2.2 %collective-permute-done.1 = bf16[144,256]{1,0:T(8,128)(2,1)S(1)} collective-permute-done((bf16[144,256]{1,0:T(8,128)(2,1)}, bf16[144,256]{1,0:T(8,128)(2,1)S(1)}, u32[]{:S(2)}, u32[]{:S(2)}) %collective-permute-start.1) | collective-permute-done | bytes 73760 | tf_op jit(solution)/shard_map/ppermute | solution.py:473
  14.3 0.2 collective-permute-done.2
  14.5 0.0 copy-done.3
  14.6 2.5 %collective-permute-start.8 = (bf16[512,256]{1,0:T(8,128)(2,1)S(1)}, bf16[512,256]{1,0:T(8,128)(2,1)S(1)}, u32[]{:S(2)}, u32[]{:S(2)}) collective-permute-start(bf16[512,256]{1,0:T(8,128)(2,1)S(1)} %pad_maximum_fusion.rest_5_.rest_0_), channel_id=1, source_target_pairs={{0,24},{4,28},{8,16},{12,20},{16,8},{20,12},{24,0},{28,4},{1,25},{... | collective-permute-start | bytes 786440 | tf_op jit(solution)/shard_map/ppermute | solution.py:470
  17.1 0.5 collective-permute-start.6
  17.6 0.5 collective-permute-start.4
  18.1 0.1 collective-permute-start.3
  18.2 4.2 %plan.1.rest_0_ = s32[528]{0:T(1024)} custom-call(s32[32]{0:T(128)} %order_ref, s32[32]{0:T(128)} %doc_ref.1, s32[32,32]{1,0:T(8,128)} %mask_ref.1), custom_call_target="tpu_custom_call" | custom-call | bytes 4194304 | tf_op jit(solution)/shard_map/plan/pallas_call | solution.py:515
  22.5 2.3 %collective-permute-done.8.rest_8_.rest_3_ = bf16[512,256]{1,0:T(8,128)(2,1)S(1)} collective-permute-done((bf16[512,256]{1,0:T(8,128)(2,1)S(1)}, bf16[512,256]{1,0:T(8,128)(2,1)S(1)}, u32[]{:S(2)}, u32[]{:S(2)}) %collective-permute-start.8) | collective-permute-done | bytes 262176 | tf_op jit(solution)/shard_map/ppermute | solution.py:470
  24.8 0.0 collective-permute-start.9
  24.8 4.3 %collective-permute-done.6.rest_7_.rest_2_ = bf16[512,256]{1,0:T(8,128)(2,1)S(1)} collective-permute-done((bf16[512,256]{1,0:T(8,128)(2,1)S(1)}, bf16[512,256]{1,0:T(8,128)(2,1)S(1)}, u32[]{:S(2)}, u32[]{:S(2)}) %collective-permute-start.6) | collective-permute-done | bytes 262176 | tf_op jit(solution)/shard_map/ppermute | solution.py:470
  29.1 0.0 collective-permute-start.7
  29.1 0.0 collective-permute-done.4.rest_6_.rest_1_
  29.1 0.5 collective-permute-start.5
  29.6 0.0 copy-done
  29.6 0.0 copy-done.1
  29.6 0.0 copy-start.2
  29.6 0.7 copy-done.2
  30.3 2.8 %attention_first.1 = (f32[4,128,1024]{2,1,0:T(8,128)S(1)}, bf16[16,128,128]{2,1,0:T(8,128)(2,1)S(1)}, bf16[16,128,128]{2,1,0:T(8,128)(2,1)S(1)}, bf16[16,128,128...) custom-call(s32[528]{0:T(1024)S(1)} %copy-done.2, f32[1,512]{1,0:T(1,128)S(1)} %bitcast.4, ...), custom_call_target="tpu_custom_call" | custom-call | flops 5368709120 | bytes 1048576 | tf_op jit(solution)/shard_map/attention_first/pallas_call | solution.py:526
  33.0 0.0 collective-permute-done.3.rest_5_
  33.0 0.0 collective-permute-done.9.rest_8_
  33.1 0.0 collective-permute-done.7.rest_7_
  33.1 0.0 collective-permute-done.5.rest_6_
  33.1 5.2 %attention_leaving.1 = (f32[4,128,1024]{2,1,0:T(8,128)S(1)}, bf16[128,512]{1,0:T(8,128)(2,1)S(1)}, bf16[128,512]{1,0:T(8,128)(2,1)S(1)}, bf16[16,128,128]{2,1,0:...) custom-call(s32[528]{0:T(1024)S(1)} %copy-done.2, ...), custom_call_target="tpu_custom_call" | custom-call | flops 5368709120 | bytes 1048576 | tf_op jit(solution)/shard_map/attention_leaving/pallas_call | solution.py:526
  38.3 1.3 %collective-permute-start.10 = (bf16[128,512]{1,0:T(8,128)(2,1)S(1)}, bf16[128,512]{1,0:T(8,128)(2,1)S(1)}, u32[]{:S(2)}, u32[]{:S(2)}) collective-permute-start(bf16[128,512]{1,0:T(8,128)(2,1)S(1)} %get-tuple-element.92), channel_id=1, source_target_pairs={{0,2},{1,3},{2,0},{3,1},{4,6},{5,7},{6,4},{7,5},{8,10},{9,11},{10,... | collective-permute-start | bytes 393224 | tf_op jit(solution)/shard_map/ppermute | solution.py:473
  39.6 6.0 %attention_other.1 = (f32[4,128,1024]{2,1,0:T(8,128)S(1)}, f32[16,128,128]{2,1,0:T(8,128)S(1)}, f32[16,128,128]{2,1,0:T(8,128)S(1)}, bf16[2048,256]{1,0:T(8,128)(2,1)S(1)}) custom-call(s32[528]{0:T(1024)S(1)} %copy-done.2, bf16[2,512,1024]{2,1,0:T(8,128)(2,1)S(1)} %own_heads.1.rest_3_.rest_1_, bf16[64,256]{1,0:T(8,128)(2,1)S(1)} %pad_maximum_fusion.1.rest_4_.rest_2_, ...), custom_call_target="tpu_custom_call" | custom-call | flops 5368709120 | bytes 1048576 | tf_op jit(solution)/shard_map/attention_other/pallas_call | solution.py:526
  45.6 0.0 collective-permute-done.10.rest_0_
  45.6 0.1 collective-permute-start.11
  45.7 1.8 %collective-permute-start.18 = (bf16[128,512]{1,0:T(8,128)(2,1)S(1)}, bf16[128,512]{1,0:T(8,128)(2,1)S(1)}, u32[]{:S(2)}, u32[]{:S(2)}) collective-permute-start(bf16[128,512]{1,0:T(8,128)(2,1)S(1)} %get-tuple-element.106), channel_id=1, source_target_pairs={{0,2},{1,3},{2,0},{3,1},{4,6},{5,7},{6,4},{7,5},{8,10},{9,11},{10,... | collective-permute-start | bytes 393224 | tf_op jit(solution)/shard_map/ppermute | solution.py:473
  47.5 5.9 %attention_own.1 = (bf16[128,1024]{1,0:T(8,128)(2,1)S(1)}, bf16[128,1024]{1,0:T(8,128)(2,1)S(1)}, bf16[128,1024]{1,0:T(8,128)(2,1)S(1)}, f32[16,128,128]{2,1,0:T(8,128)S(1)}, f32[16,128,128]{2,1,0:T(8,128)S(1)}) custom-call(s32[528]{0:T(1024)S(1)} %copy-done.2, bf16[2,512,1024]{2,1,0:T(8,128)(2,1)S(1)} %own_heads.1.rest_3_.rest_1_, ...), custom_call_target="tpu_custom_call" | custom-call | flops 5368709120 | bytes 1048576 | tf_op jit(solution)/shard_map/attention_own/pallas_call | solution.py:526
  53.4 0.0 collective-permute-done.11.kv_back
  53.4 0.5 merge.1
  53.9 0.1 collective-permute-start.12
  54.0 0.1 collective-permute-start.13
  54.0 3.4 %collective-permute-start.14 = (bf16[528,256]{1,0:T(8,128)(2,1)S(1)}, bf16[528,256]{1,0:T(8,128)(2,1)S(1)}, u32[]{:S(2)}, u32[]{:S(2)}) collective-permute-start(bf16[528,256]{1,0:T(8,128)(2,1)S(1)} %get-tuple-element.97), channel_id=1, source_target_pairs={{0,24},{4,28},{8,16},{12,20},{16,8},{20,12},{24,0},{28,4},{1,25},{... | collective-permute-start | bytes 811016 | tf_op jit(solution)/shard_map/ppermute | solution.py:470
  57.4 0.0 collective-permute-done.18.rest_1_
  57.4 2.1 %collective-permute-start.19 = (bf16[128,1024]{1,0:T(8,128)(2,1)S(1)}, bf16[128,1024]{1,0:T(8,128)(2,1)S(1)}, u32[]{:S(2)}, u32[]{:S(2)}) collective-permute-start(bf16[128,1024]{1,0:T(8,128)(2,1)S(1)} %get-tuple-element.109), channel_id=1, source_target_pairs={{0,1},{1,2},{2,3},{3,0},{4,5},{5,6},{6,7},{7,4},{8,9},{9,10},{10,1... | collective-permute-start | bytes 786440 | tf_op jit(solution)/shard_map/ppermute | solution.py:473
  59.6 1.7 %collective-permute-start.20 = (bf16[128,1024]{1,0:T(8,128)(2,1)S(1)}, bf16[128,1024]{1,0:T(8,128)(2,1)S(1)}, u32[]{:S(2)}, u32[]{:S(2)}) collective-permute-start(bf16[128,1024]{1,0:T(8,128)(2,1)S(1)} %get-tuple-element.110), channel_id=1, source_target_pairs={{0,3},{1,0},{2,1},{3,2},{4,7},{5,4},{6,5},{7,6},{8,11},{9,8},{10,9... | collective-permute-start | bytes 786440 | tf_op jit(solution)/shard_map/ppermute | solution.py:473
  61.3 1.2 %collective-permute-done.12.rest_1_ = bf16[528,256]{1,0:T(8,128)(2,1)S(1)} collective-permute-done((bf16[528,256]{1,0:T(8,128)(2,1)S(1)}, bf16[528,256]{1,0:T(8,128)(2,1)S(1)}, u32[]{:S(2)}, u32[]{:S(2)}) %collective-permute-start.12) | collective-permute-done | bytes 270368 | tf_op jit(solution)/shard_map/ppermute | solution.py:470
  62.5 4.6 %collective-permute-done.13.rest_2_ = bf16[528,256]{1,0:T(8,128)(2,1)S(1)} collective-permute-done((bf16[528,256]{1,0:T(8,128)(2,1)S(1)}, bf16[528,256]{1,0:T(8,128)(2,1)S(1)}, u32[]{:S(2)}, u32[]{:S(2)}) %collective-permute-start.13) | collective-permute-done | bytes 270368 | tf_op jit(solution)/shard_map/ppermute | solution.py:470
  67.1 0.0 collective-permute-done.14.rest_3_
  67.1 0.1 collect.1
  67.3 2.7 %collective-permute-start.15 = (bf16[144,256]{1,0:T(8,128)(2,1)S(1)}, bf16[144,256]{1,0:T(8,128)(2,1)S(1)}, u32[]{:S(2)}, u32[]{:S(2)}) collective-permute-start(bf16[144,256]{1,0:T(8,128)(2,1)S(1)} %get-tuple-element.99), channel_id=1, source_target_pairs={{0,3},{1,0},{2,1},{3,2},{4,7},{5,4},{6,5},{7,6},{8,11},{9,8},{10,9... | collective-permute-start | bytes 221192 | tf_op jit(solution)/shard_map/ppermute | solution.py:473
  70.0 1.4 %collective-permute-start.16 = (bf16[144,256]{1,0:T(8,128)(2,1)S(1)}, bf16[144,256]{1,0:T(8,128)(2,1)S(1)}, u32[]{:S(2)}, u32[]{:S(2)}) collective-permute-start(bf16[144,256]{1,0:T(8,128)(2,1)S(1)} %get-tuple-element.100), channel_id=1, source_target_pairs={{0,2},{1,3},{2,0},{3,1},{4,6},{5,7},{6,4},{7,5},{8,10},{9,11},{10,... | collective-permute-start | bytes 221192 | tf_op jit(solution)/shard_map/ppermute | solution.py:473
  71.4 0.3 collective-permute-start.17
  71.7 0.0 collective-permute-done.19.rest_3_
  71.7 0.0 collective-permute-done.20.rest_4_
  71.7 1.1 %place_queries.1 = bf16[128,4096]{1,0:T(8,128)(2,1)} custom-call(bf16[128,512]{1,0:T(8,128)(2,1)S(1)} %collective-permute-done.10.rest_0_, bf16[128,512]{1,0:T(8,128)(2,1)S(1)} %collective-permute-done.18.rest_1_, bf16[128,1024]{1,0:T(8,128)(2,1)S(1)} %get-tuple-element.108.rest_2_, bf16[128,1024]{1,0:T(8,128)(2,1)S(1)} %collective-permute-done.19.rest_3_, ...), custom_call_target="tpu_custom_call" | custom-call | bytes 2097152 | tf_op jit(solution)/shard_map/place_queries/pallas_call | solution.py:591
  72.9 0.0 collective-permute-done.15.rest_1_
  72.9 4.9 %collective-permute-done.16.rest_2_ = bf16[144,256]{1,0:T(8,128)(2,1)S(1)} collective-permute-done((bf16[144,256]{1,0:T(8,128)(2,1)S(1)}, bf16[144,256]{1,0:T(8,128)(2,1)S(1)}, u32[]{:S(2)}, u32[]{:S(2)}) %collective-permute-start.16) | collective-permute-done | bytes 73760 | tf_op jit(solution)/shard_map/ppermute | solution.py:473
  77.7 0.0 collective-permute-done.17.rest_3_
  77.7 0.8 %finish.1 = (bf16[128,512]{1,0:T(8,128)(2,1)}, bf16[128,512]{1,0:T(8,128)(2,1)}, f32[2,512]{1,0:T(2,128)S(1)}) custom-call(f32[1,512]{1,0:T(1,128)S(1)} %bitcast.7, f32[1,512]{1,0:T(1,128)S(1)} %bitcast.11, f32[144,256]{1,0:T(8,128)S(1)} %get-tuple-element.112.rest_0_, bf16[144,256]{1,0:T(8,128)(2,1)S(1)} %collective-permute-done.15.rest_1_, ...), custom_call_target="tpu_custom_call" | custom-call | tf_op jit(solution)/shard_map/finish/pallas_call | solution.py:602
  78.6 0.0 collective-permute-start.21
  78.6 1.2 %collective-permute-done.21.other_ref = f32[2,512]{1,0:T(2,128)S(1)} collective-permute-done((f32[2,512]{1,0:T(2,128)S(1)}, f32[2,512]{1,0:T(2,128)S(1)}, u32[]{:S(2)}, u32[]{:S(2)}) %collective-permute-start.21) | collective-permute-done | bytes 4128 | tf_op jit(solution)/shard_map/ppermute | solution.py:470
  79.7 0.6 add_gains.1
  (10 shorter events, 0.1 us)
Async XLA Ops:
  3.4 8.6 %collective-permute-start = (bf16[144,256]{1,0:T(8,128)(2,1)}, bf16[144,256]{1,0:T(8,128)(2,1)S(1)}, u32[]{:S(2)}, u32[]{:S(2)}) collective-permute-start(bf16[144,256]{1,0:T(8,128)(2,1)} %get-tuple-element.64), channel_id=1, source_target_pairs={{0,1},{1,2},{2,3},{3,0},{4,5},{5,6},{6,7},{7,4},{8,9},{9,10},{10,1... | collective-permute-start | bytes 221192 | tf_op jit(solution)/shard_map/ppermute | solution.py:473
  6.5 7.8 %collective-permute-start.1 = (bf16[144,256]{1,0:T(8,128)(2,1)}, bf16[144,256]{1,0:T(8,128)(2,1)S(1)}, u32[]{:S(2)}, u32[]{:S(2)}) collective-permute-start(bf16[144,256]{1,0:T(8,128)(2,1)} %get-tuple-element.65), channel_id=1, source_target_pairs={{0,2},{1,3},{2,0},{3,1},{4,6},{5,7},{6,4},{7,5},{8,10},{9,11},{10,... | collective-permute-start | bytes 221192 | tf_op jit(solution)/shard_map/ppermute | solution.py:473
  9.1 5.4 %collective-permute-start.2 = (bf16[144,256]{1,0:T(8,128)(2,1)}, bf16[144,256]{1,0:T(8,128)(2,1)S(1)}, u32[]{:S(2)}, u32[]{:S(2)}) collective-permute-start(bf16[144,256]{1,0:T(8,128)(2,1)} %get-tuple-element.66), channel_id=1, source_target_pairs={{0,3},{1,0},{2,1},{3,2},{4,7},{5,4},{6,5},{7,6},{8,11},{9,8},{10,9... | collective-permute-start | bytes 221192 | tf_op jit(solution)/shard_map/ppermute | solution.py:473
  10.4 4.0 %copy-start.3 = (bf16[144,256]{1,0:T(8,128)(2,1)S(1)}, bf16[144,256]{1,0:T(8,128)(2,1)}, u32[]{:S(2)}) copy-start(bf16[144,256]{1,0:T(8,128)(2,1)} %get-tuple-element.68) | copy-start | bytes 221188
  10.4 19.1 %copy-start = (f32[512]{0:T(512)S(1)}, f32[512]{0:T(512)}, u32[]{:S(2)}) copy-start(f32[512]{0:T(512)} %param.17) | copy-start | bytes 6148
  10.5 19.1 %copy-start.1 = (f32[512]{0:T(512)S(1)}, f32[512]{0:T(512)}, u32[]{:S(2)}) copy-start(f32[512]{0:T(512)} %param.18) | copy-start | bytes 6148
  14.6 10.2 %collective-permute-start.8 = (bf16[512,256]{1,0:T(8,128)(2,1)S(1)}, bf16[512,256]{1,0:T(8,128)(2,1)S(1)}, u32[]{:S(2)}, u32[]{:S(2)}) collective-permute-start(bf16[512,256]{1,0:T(8,128)(2,1)S(1)} %pad_maximum_fusion.rest_5_.rest_0_), channel_id=1, source_target_pairs={{0,24},{4,28},{8,16},{12,20},{16,8},{20,12},{24,0},{28,4},{1,25},{... | collective-permute-start | bytes 786440 | tf_op jit(solution)/shard_map/ppermute | solution.py:470
  17.1 12.0 %collective-permute-start.6 = (bf16[512,256]{1,0:T(8,128)(2,1)S(1)}, bf16[512,256]{1,0:T(8,128)(2,1)S(1)}, u32[]{:S(2)}, u32[]{:S(2)}) collective-permute-start(bf16[512,256]{1,0:T(8,128)(2,1)S(1)} %pad_maximum_fusion.rest_5_.rest_0_), channel_id=1, source_target_pairs={{0,16},{4,20},{8,24},{12,28},{16,0},{20,4},{24,8},{28,12},{1,17},{... | collective-permute-start | bytes 786440 | tf_op jit(solution)/shard_map/ppermute | solution.py:470
  17.6 11.5 %collective-permute-start.4 = (bf16[512,256]{1,0:T(8,128)(2,1)S(1)}, bf16[512,256]{1,0:T(8,128)(2,1)S(1)}, u32[]{:S(2)}, u32[]{:S(2)}) collective-permute-start(bf16[512,256]{1,0:T(8,128)(2,1)S(1)} %pad_maximum_fusion.rest_5_.rest_0_), channel_id=1, source_target_pairs={{0,8},{4,12},{8,0},{12,4},{16,24},{20,28},{24,16},{28,20},{1,9},{5... | collective-permute-start | bytes 786440 | tf_op jit(solution)/shard_map/ppermute | solution.py:470
  18.1 14.9 %collective-permute-start.3 = (bf16[512,256]{1,0:T(8,128)(2,1)S(1)}, bf16[512,256]{1,0:T(8,128)(2,1)S(1)}, u32[]{:S(2)}, u32[]{:S(2)}) collective-permute-start(bf16[512,256]{1,0:T(8,128)(2,1)S(1)} %pad_maximum_fusion.rest_5_.rest_0_), channel_id=1, source_target_pairs={{0,4},{4,0},{8,12},{12,8},{16,20},{20,16},{24,28},{28,24},{1,5},{5... | collective-permute-start | bytes 786440 | tf_op jit(solution)/shard_map/ppermute | solution.py:470
  24.8 8.3 %collective-permute-start.9 = (bf16[512,256]{1,0:T(8,128)(2,1)S(1)}, bf16[512,256]{1,0:T(8,128)(2,1)S(1)}, u32[]{:S(2)}, u32[]{:S(2)}) collective-permute-start(bf16[512,256]{1,0:T(8,128)(2,1)S(1)} %collective-permute-done.8.rest_8_.rest_3_), channel_id=1, source_target_pairs={{0,4},{4,0},{8,12},{12,8},{16,20},{20,16},{24,28},{28,24},{1,5},{5... | collective-permute-start | bytes 786440 | tf_op jit(solution)/shard_map/ppermute | solution.py:470
  29.1 4.0 %collective-permute-start.7 = (bf16[512,256]{1,0:T(8,128)(2,1)S(1)}, bf16[512,256]{1,0:T(8,128)(2,1)S(1)}, u32[]{:S(2)}, u32[]{:S(2)}) collective-permute-start(bf16[512,256]{1,0:T(8,128)(2,1)S(1)} %collective-permute-done.6.rest_7_.rest_2_), channel_id=1, source_target_pairs={{0,4},{4,0},{8,12},{12,8},{16,20},{20,16},{24,28},{28,24},{1,5},{5... | collective-permute-start | bytes 786440 | tf_op jit(solution)/shard_map/ppermute | solution.py:470
  29.1 4.0 %collective-permute-start.5 = (bf16[512,256]{1,0:T(8,128)(2,1)S(1)}, bf16[512,256]{1,0:T(8,128)(2,1)S(1)}, u32[]{:S(2)}, u32[]{:S(2)}) collective-permute-start(bf16[512,256]{1,0:T(8,128)(2,1)S(1)} %collective-permute-done.4.rest_6_.rest_1_), channel_id=1, source_target_pairs={{0,4},{4,0},{8,12},{12,8},{16,20},{20,16},{24,28},{28,24},{1,5},{5... | collective-permute-start | bytes 786440 | tf_op jit(solution)/shard_map/ppermute | solution.py:470
  29.6 0.7 copy-start.2
  38.3 7.3 %collective-permute-start.10 = (bf16[128,512]{1,0:T(8,128)(2,1)S(1)}, bf16[128,512]{1,0:T(8,128)(2,1)S(1)}, u32[]{:S(2)}, u32[]{:S(2)}) collective-permute-start(bf16[128,512]{1,0:T(8,128)(2,1)S(1)} %get-tuple-element.92), channel_id=1, source_target_pairs={{0,2},{1,3},{2,0},{3,1},{4,6},{5,7},{6,4},{7,5},{8,10},{9,11},{10,... | collective-permute-start | bytes 393224 | tf_op jit(solution)/shard_map/ppermute | solution.py:473
  45.6 7.7 %collective-permute-start.11 = (bf16[2048,256]{1,0:T(8,128)(2,1)S(1)}, bf16[2048,256]{1,0:T(8,128)(2,1)S(1)}, u32[]{:S(2)}, u32[]{:S(2)}) collective-permute-start(bf16[2048,256]{1,0:T(8,128)(2,1)S(1)} %get-tuple-element.93), channel_id=1, source_target_pairs={{0,4},{4,0},{8,12},{12,8},{16,20},{20,16},{24,28},{28,24},{1,5},{5... | collective-permute-start | bytes 3145736 | tf_op jit(solution)/shard_map/ppermute | solution.py:470
  45.7 11.7 %collective-permute-start.18 = (bf16[128,512]{1,0:T(8,128)(2,1)S(1)}, bf16[128,512]{1,0:T(8,128)(2,1)S(1)}, u32[]{:S(2)}, u32[]{:S(2)}) collective-permute-start(bf16[128,512]{1,0:T(8,128)(2,1)S(1)} %get-tuple-element.106), channel_id=1, source_target_pairs={{0,2},{1,3},{2,0},{3,1},{4,6},{5,7},{6,4},{7,5},{8,10},{9,11},{10,... | collective-permute-start | bytes 393224 | tf_op jit(solution)/shard_map/ppermute | solution.py:473
  53.9 8.6 %collective-permute-start.12 = (bf16[528,256]{1,0:T(8,128)(2,1)S(1)}, bf16[528,256]{1,0:T(8,128)(2,1)S(1)}, u32[]{:S(2)}, u32[]{:S(2)}) collective-permute-start(bf16[528,256]{1,0:T(8,128)(2,1)S(1)} %get-tuple-element.95), channel_id=1, source_target_pairs={{0,8},{4,12},{8,0},{12,4},{16,24},{20,28},{24,16},{28,20},{1,9},{5... | collective-permute-start | bytes 811016 | tf_op jit(solution)/shard_map/ppermute | solution.py:470
  54.0 13.1 %collective-permute-start.13 = (bf16[528,256]{1,0:T(8,128)(2,1)S(1)}, bf16[528,256]{1,0:T(8,128)(2,1)S(1)}, u32[]{:S(2)}, u32[]{:S(2)}) collective-permute-start(bf16[528,256]{1,0:T(8,128)(2,1)S(1)} %get-tuple-element.96), channel_id=1, source_target_pairs={{0,16},{4,20},{8,24},{12,28},{16,0},{20,4},{24,8},{28,12},{1,17},{... | collective-permute-start | bytes 811016 | tf_op jit(solution)/shard_map/ppermute | solution.py:470
  54.0 13.1 %collective-permute-start.14 = (bf16[528,256]{1,0:T(8,128)(2,1)S(1)}, bf16[528,256]{1,0:T(8,128)(2,1)S(1)}, u32[]{:S(2)}, u32[]{:S(2)}) collective-permute-start(bf16[528,256]{1,0:T(8,128)(2,1)S(1)} %get-tuple-element.97), channel_id=1, source_target_pairs={{0,24},{4,28},{8,16},{12,20},{16,8},{20,12},{24,0},{28,4},{1,25},{... | collective-permute-start | bytes 811016 | tf_op jit(solution)/shard_map/ppermute | solution.py:470
  57.4 14.3 %collective-permute-start.19 = (bf16[128,1024]{1,0:T(8,128)(2,1)S(1)}, bf16[128,1024]{1,0:T(8,128)(2,1)S(1)}, u32[]{:S(2)}, u32[]{:S(2)}) collective-permute-start(bf16[128,1024]{1,0:T(8,128)(2,1)S(1)} %get-tuple-element.109), channel_id=1, source_target_pairs={{0,1},{1,2},{2,3},{3,0},{4,5},{5,6},{6,7},{7,4},{8,9},{9,10},{10,1... | collective-permute-start | bytes 786440 | tf_op jit(solution)/shard_map/ppermute | solution.py:473
  59.6 12.2 %collective-permute-start.20 = (bf16[128,1024]{1,0:T(8,128)(2,1)S(1)}, bf16[128,1024]{1,0:T(8,128)(2,1)S(1)}, u32[]{:S(2)}, u32[]{:S(2)}) collective-permute-start(bf16[128,1024]{1,0:T(8,128)(2,1)S(1)} %get-tuple-element.110), channel_id=1, source_target_pairs={{0,3},{1,0},{2,1},{3,2},{4,7},{5,4},{6,5},{7,6},{8,11},{9,8},{10,9... | collective-permute-start | bytes 786440 | tf_op jit(solution)/shard_map/ppermute | solution.py:473
  67.3 5.6 %collective-permute-start.15 = (bf16[144,256]{1,0:T(8,128)(2,1)S(1)}, bf16[144,256]{1,0:T(8,128)(2,1)S(1)}, u32[]{:S(2)}, u32[]{:S(2)}) collective-permute-start(bf16[144,256]{1,0:T(8,128)(2,1)S(1)} %get-tuple-element.99), channel_id=1, source_target_pairs={{0,3},{1,0},{2,1},{3,2},{4,7},{5,4},{6,5},{7,6},{8,11},{9,8},{10,9... | collective-permute-start | bytes 221192 | tf_op jit(solution)/shard_map/ppermute | solution.py:473
  70.0 7.7 %collective-permute-start.16 = (bf16[144,256]{1,0:T(8,128)(2,1)S(1)}, bf16[144,256]{1,0:T(8,128)(2,1)S(1)}, u32[]{:S(2)}, u32[]{:S(2)}) collective-permute-start(bf16[144,256]{1,0:T(8,128)(2,1)S(1)} %get-tuple-element.100), channel_id=1, source_target_pairs={{0,2},{1,3},{2,0},{3,1},{4,6},{5,7},{6,4},{7,5},{8,10},{9,11},{10,... | collective-permute-start | bytes 221192 | tf_op jit(solution)/shard_map/ppermute | solution.py:473
  71.4 6.3 %collective-permute-start.17 = (bf16[144,256]{1,0:T(8,128)(2,1)S(1)}, bf16[144,256]{1,0:T(8,128)(2,1)S(1)}, u32[]{:S(2)}, u32[]{:S(2)}) collective-permute-start(bf16[144,256]{1,0:T(8,128)(2,1)S(1)} %get-tuple-element.101), channel_id=1, source_target_pairs={{0,1},{1,2},{2,3},{3,0},{4,5},{5,6},{6,7},{7,4},{8,9},{9,10},{10,1... | collective-permute-start | bytes 221192 | tf_op jit(solution)/shard_map/ppermute | solution.py:473
  78.6 1.2 %collective-permute-start.21 = (f32[2,512]{1,0:T(2,128)S(1)}, f32[2,512]{1,0:T(2,128)S(1)}, u32[]{:S(2)}, u32[]{:S(2)}) collective-permute-start(f32[2,512]{1,0:T(2,128)S(1)} %get-tuple-element.118.gains_ref), channel_id=1, source_target_pairs={{0,4},{4,0},{8,12},{12,8},{16,20},{20,16},{24,28},{28,24},{1,5},{5... | collective-permute-start | bytes 12296 | tf_op jit(solution)/shard_map/ppermute | solution.py:470

commit v4 on v3

--- a/solution.py
+++ b/solution.py
@@ -521,6 +521,7 @@
         cost_estimate=pl.CostEstimate(flops=0, bytes_accessed=1 << 22, transcendentals=0),
         name="plan",
     )(later_order, doc_ids, tile_mask)
+    table = jnp.maximum(table, -TILE)
 
     def attend(stage, outs, scratch, *operands):
         return pl.pallas_call(

time: 80.9 us -> 80.9 us (level)
  Pallas kernels: 31.7 us -> 33.8 us
  waiting for transfers between devices: 20.9 us -> 18.9 us
    ppermute x12, waiting for transfers between devices: 13.6 us -> 10.5 us  [swap(): lax.ppermute(array, 'pb', [(at, at ^ number) for at in range(count_pb)])]
    pallas_call x4, Pallas kernels: 19.9 us -> 22 us  [attend(): pl.pallas_call(functools.partial(attention_kernel, (count_chip, count_ka,...]
    ppermute x10, waiting for transfers between devices: 7.31 us -> 8.4 us  [turn(): lax.ppermute(array, 'ka', [(at, (at + step) % count_ka) for at in range(c...]
  transfers between devices with their start and end apart: 22 -> 22, of which waited for: 8 -> 7; matrix products, arithmetic and copies ran while one was open for 0% -> 1% of each run, Pallas kernels for 28% -> 30%
where the time goes in v4:
time: 80.9 us; the launch traced here: 80.6 us
  Pallas kernels  33.8 us (42%)
  starting transfers between devices  26.3 us (33%)
  waiting for transfers between devices  18.9 us (23%)
  between operations  0.87 us (1%)
    pallas_call x4, Pallas kernels, attend(): pl.pallas_call(functools.partial(attention_kernel, (count_chip, count_ka,...  22 us
    ppermute x10, starting transfers between devices, turn(): lax.ppermute(array, 'ka', [(at, (at + step) % count_ka) for at in range(c...  18.6 us
    ppermute x12, waiting for transfers between devices, swap(): lax.ppermute(array, 'pb', [(at, at ^ number) for at in range(count_pb)])  10.5 us
    ppermute x10, waiting for transfers between devices, turn(): lax.ppermute(array, 'ka', [(at, (at + step) % count_ka) for at in range(c...  8.4 us
    ppermute x12, starting transfers between devices, swap(): lax.ppermute(array, 'pb', [(at, at ^ number) for at in range(count_pb)])  7.68 us
    pallas_call x1, Pallas kernels, shards(): pl.pallas_call(functools.partial(plan_kernel, (count_chip, count_ka, orde...  4.25 us
    pallas_call x1, Pallas kernels, shards(): pl.pallas_call(functools.partial(prepare_kernel, (count_ka, heads, heads_...  2.79 us
  transfers between devices with their start and end apart: 22, of which 7 were waited for; matrix products, arithmetic and copies ran while one was open for 1% of the time, Pallas kernels for 30%

profile of v4, /device:TPU:0, one launch (start us, length us, event | category | flops | bytes accessed | tf_op | source)
XLA Modules:
  0.0 80.6 jit_solution(8315814988251897124)
XLA Ops:
  0.6 2.8 %prepare.1 = (bf16[144,256]{1,0:T(8,128)(2,1)}, bf16[144,256]{1,0:T(8,128)(2,1)}, bf16[144,256]{1,0:T(8,128)(2,1)}, bf16[144,256]{1,0:T(8,128)(2,1)}) custom-call(bf16[128,512]{1,0:T(8,128)(2,1)} %key_ref.1, bf16[128,512]{1,0:T(8,128)(2,1)} %value_ref.1, bf16[128,4096]{1,0:T(8,128)(2,1)} %attn_ref.1, bf16[512,4096]{1,0:T(8,128)(2,1)} %grads_ref.3, ...), custom_call_target="tpu_custom_call" | custom-call | tf_op jit(solution)/shard_map/prepare/pallas_call | solution.py:475
  3.4 3.1 %collective-permute-start = (bf16[144,256]{1,0:T(8,128)(2,1)}, bf16[144,256]{1,0:T(8,128)(2,1)S(1)}, u32[]{:S(2)}, u32[]{:S(2)}) collective-permute-start(bf16[144,256]{1,0:T(8,128)(2,1)} %get-tuple-element.64), channel_id=1, source_target_pairs={{0,1},{1,2},{2,3},{3,0},{4,5},{5,6},{6,7},{7,4},{8,9},{9,10},{10,1... | collective-permute-start | bytes 221192 | tf_op jit(solution)/shard_map/ppermute | solution.py:473
  6.5 2.6 %collective-permute-start.1 = (bf16[144,256]{1,0:T(8,128)(2,1)}, bf16[144,256]{1,0:T(8,128)(2,1)S(1)}, u32[]{:S(2)}, u32[]{:S(2)}) collective-permute-start(bf16[144,256]{1,0:T(8,128)(2,1)} %get-tuple-element.65), channel_id=1, source_target_pairs={{0,2},{1,3},{2,0},{3,1},{4,6},{5,7},{6,4},{7,5},{8,10},{9,11},{10,... | collective-permute-start | bytes 221192 | tf_op jit(solution)/shard_map/ppermute | solution.py:473
  9.1 1.3 %collective-permute-start.2 = (bf16[144,256]{1,0:T(8,128)(2,1)}, bf16[144,256]{1,0:T(8,128)(2,1)S(1)}, u32[]{:S(2)}, u32[]{:S(2)}) collective-permute-start(bf16[144,256]{1,0:T(8,128)(2,1)} %get-tuple-element.66), channel_id=1, source_target_pairs={{0,3},{1,0},{2,1},{3,2},{4,7},{5,4},{6,5},{7,6},{8,11},{9,8},{10,9... | collective-permute-start | bytes 221192 | tf_op jit(solution)/shard_map/ppermute | solution.py:473
  10.4 0.0 copy-start.2
  10.4 0.0 copy-start
  10.4 0.0 copy-start.1
  10.5 1.6 %own_heads.1.rest_3_.rest_1_ = bf16[2,512,1024]{2,1,0:T(8,128)(2,1)S(1)} custom-call(bf16[512,4096]{1,0:T(8,128)(2,1)} %queries_ref, bf16[512,4096]{1,0:T(8,128)(2,1)} %grads_ref.3), custom_call_target="tpu_custom_call" | custom-call | bytes 4194304 | tf_op jit(solution)/shard_map/own_heads/pallas_call | solution.py:490
  12.1 0.0 collective-permute-done
  12.1 2.2 %collective-permute-done.1 = bf16[144,256]{1,0:T(8,128)(2,1)S(1)} collective-permute-done((bf16[144,256]{1,0:T(8,128)(2,1)}, bf16[144,256]{1,0:T(8,128)(2,1)S(1)}, u32[]{:S(2)}, u32[]{:S(2)}) %collective-permute-start.1) | collective-permute-done | bytes 73760 | tf_op jit(solution)/shard_map/ppermute | solution.py:473
  14.3 0.2 collective-permute-done.2
  14.5 0.0 copy-done.2
  14.6 2.5 %collective-permute-start.8 = (bf16[512,256]{1,0:T(8,128)(2,1)S(1)}, bf16[512,256]{1,0:T(8,128)(2,1)S(1)}, u32[]{:S(2)}, u32[]{:S(2)}) collective-permute-start(bf16[512,256]{1,0:T(8,128)(2,1)S(1)} %pad_maximum_fusion.rest_5_.rest_0_), channel_id=1, source_target_pairs={{0,24},{4,28},{8,16},{12,20},{16,8},{20,12},{24,0},{28,4},{1,25},{... | collective-permute-start | bytes 786440 | tf_op jit(solution)/shard_map/ppermute | solution.py:470
  17.1 0.5 collective-permute-start.6
  17.6 0.5 collective-permute-start.4
  18.2 0.0 collective-permute-start.3
  18.2 4.2 %plan.1 = s32[528]{0:T(1024)} custom-call(s32[32]{0:T(128)} %order_ref, s32[32]{0:T(128)} %doc_ref.1, s32[32,32]{1,0:T(8,128)} %mask_ref.1), custom_call_target="tpu_custom_call" | custom-call | bytes 4194304 | tf_op jit(solution)/shard_map/plan/pallas_call | solution.py:515
  22.4 0.7 broadcast_maximum_fusion.rest_0_
  23.1 1.7 %collective-permute-done.8.rest_8_.rest_3_ = bf16[512,256]{1,0:T(8,128)(2,1)S(1)} collective-permute-done((bf16[512,256]{1,0:T(8,128)(2,1)S(1)}, bf16[512,256]{1,0:T(8,128)(2,1)S(1)}, u32[]{:S(2)}, u32[]{:S(2)}) %collective-permute-start.8) | collective-permute-done | bytes 262176 | tf_op jit(solution)/shard_map/ppermute | solution.py:470
  24.8 0.0 collective-permute-start.9
  24.8 4.3 %collective-permute-done.6.rest_7_.rest_2_ = bf16[512,256]{1,0:T(8,128)(2,1)S(1)} collective-permute-done((bf16[512,256]{1,0:T(8,128)(2,1)S(1)}, bf16[512,256]{1,0:T(8,128)(2,1)S(1)}, u32[]{:S(2)}, u32[]{:S(2)}) %collective-permute-start.6) | collective-permute-done | bytes 262176 | tf_op jit(solution)/shard_map/ppermute | solution.py:470
  29.1 0.0 collective-permute-start.7
  29.1 0.0 collective-permute-done.4.rest_6_.rest_1_
  29.1 0.5 collective-permute-start.5
  29.6 0.0 copy-done
  29.6 0.0 copy-done.1
  29.6 3.6 %attention_first.1 = (f32[4,128,1024]{2,1,0:T(8,128)S(1)}, bf16[16,128,128]{2,1,0:T(8,128)(2,1)S(1)}, bf16[16,128,128]{2,1,0:T(8,128)(2,1)S(1)}, bf16[16,128,128...) custom-call(s32[528]{0:T(1024)S(1)} %broadcast_maximum_fusion.rest_0_, ...), custom_call_target="tpu_custom_call" | custom-call | flops 5368709120 | bytes 1048576 | tf_op jit(solution)/shard_map/attention_first/pallas_call | solution.py:527
  33.3 0.0 collective-permute-done.3.rest_5_
  33.3 0.0 collective-permute-done.9.rest_8_
  33.3 0.0 collective-permute-done.7.rest_7_
  33.3 0.0 collective-permute-done.5.rest_6_
  33.3 5.3 %attention_leaving.1 = (f32[4,128,1024]{2,1,0:T(8,128)S(1)}, bf16[128,512]{1,0:T(8,128)(2,1)S(1)}, bf16[128,512]{1,0:T(8,128)(2,1)S(1)}, bf16[16,128,128]{2,1,0:...) custom-call(s32[528]{0:T(1024)S(1)} %broadcast_maximum_fusion.rest_0, ...), custom_call_target="tpu_custom_call" | custom-call | flops 5368709120 | bytes 1048576 | tf_op jit(solution)/shard_map/attention_leaving/pallas_call | solution.py:527
  38.6 1.3 %collective-permute-start.10 = (bf16[128,512]{1,0:T(8,128)(2,1)S(1)}, bf16[128,512]{1,0:T(8,128)(2,1)S(1)}, u32[]{:S(2)}, u32[]{:S(2)}) collective-permute-start(bf16[128,512]{1,0:T(8,128)(2,1)S(1)} %get-tuple-element.92), channel_id=1, source_target_pairs={{0,2},{1,3},{2,0},{3,1},{4,6},{5,7},{6,4},{7,5},{8,10},{9,11},{10,... | collective-permute-start | bytes 393224 | tf_op jit(solution)/shard_map/ppermute | solution.py:473
  39.9 7.0 %attention_other.1 = (f32[4,128,1024]{2,1,0:T(8,128)S(1)}, f32[16,128,128]{2,1,0:T(8,128)S(1)}, f32[16,128,128]{2,1,0:T(8,128)S(1)}, bf16[2048,256]{1,0:T(8,128)(2,1)S(1)}) custom-call(s32[528]{0:T(1024)S(1)} %broadcast_maximum_fusion.rest_0_, bf16[2,512,1024]{2,1,0:T(8,128)(2,1)S(1)} %own_heads.1.rest_3_.rest_1_, ...), custom_call_target="tpu_custom_call" | custom-call | flops 5368709120 | bytes 1048576 | tf_op jit(solution)/shard_map/attention_other/pallas_call | solution.py:527
  46.9 0.0 collective-permute-done.10.rest_0_
  47.0 0.1 collective-permute-start.11
  47.0 1.8 %collective-permute-start.18 = (bf16[128,512]{1,0:T(8,128)(2,1)S(1)}, bf16[128,512]{1,0:T(8,128)(2,1)S(1)}, u32[]{:S(2)}, u32[]{:S(2)}) collective-permute-start(bf16[128,512]{1,0:T(8,128)(2,1)S(1)} %get-tuple-element.106), channel_id=1, source_target_pairs={{0,2},{1,3},{2,0},{3,1},{4,6},{5,7},{6,4},{7,5},{8,10},{9,11},{10,... | collective-permute-start | bytes 393224 | tf_op jit(solution)/shard_map/ppermute | solution.py:473
  48.8 6.0 %attention_own.1 = (bf16[128,1024]{1,0:T(8,128)(2,1)S(1)}, bf16[128,1024]{1,0:T(8,128)(2,1)S(1)}, bf16[128,1024]{1,0:T(8,128)(2,1)S(1)}, f32[16,128,128]{2,1,0:T(8,128)S(1)}, f32[16,128,128]{2,1,0:T(8,128)S(1)}) custom-call(s32[528]{0:T(1024)S(1)} %broadcast_maximum_fusion.rest_0_, bf16[2,512,1024]{2,1,0:T(8,128)(2,1)S(1)} %own_heads.1.rest_3_.rest_1_, ...), custom_call_target="tpu_custom_call" | custom-call | flops 5368709120 | bytes 1048576 | tf_op jit(solution)/shard_map/attention_own/pallas_call | solution.py:527
  54.8 0.0 collective-permute-done.11.kv_back
  54.8 0.5 merge.1
  55.3 0.1 collective-permute-start.12
  55.4 0.1 collective-permute-start.13
  55.4 3.4 %collective-permute-start.14 = (bf16[528,256]{1,0:T(8,128)(2,1)S(1)}, bf16[528,256]{1,0:T(8,128)(2,1)S(1)}, u32[]{:S(2)}, u32[]{:S(2)}) collective-permute-start(bf16[528,256]{1,0:T(8,128)(2,1)S(1)} %get-tuple-element.97), channel_id=1, source_target_pairs={{0,24},{4,28},{8,16},{12,20},{16,8},{20,12},{24,0},{28,4},{1,25},{... | collective-permute-start | bytes 811016 | tf_op jit(solution)/shard_map/ppermute | solution.py:470
  58.8 0.0 collective-permute-done.18.rest_1_
  58.8 2.1 %collective-permute-start.19 = (bf16[128,1024]{1,0:T(8,128)(2,1)S(1)}, bf16[128,1024]{1,0:T(8,128)(2,1)S(1)}, u32[]{:S(2)}, u32[]{:S(2)}) collective-permute-start(bf16[128,1024]{1,0:T(8,128)(2,1)S(1)} %get-tuple-element.109), channel_id=1, source_target_pairs={{0,1},{1,2},{2,3},{3,0},{4,5},{5,6},{6,7},{7,4},{8,9},{9,10},{10,1... | collective-permute-start | bytes 786440 | tf_op jit(solution)/shard_map/ppermute | solution.py:473
  61.0 1.7 %collective-permute-start.20 = (bf16[128,1024]{1,0:T(8,128)(2,1)S(1)}, bf16[128,1024]{1,0:T(8,128)(2,1)S(1)}, u32[]{:S(2)}, u32[]{:S(2)}) collective-permute-start(bf16[128,1024]{1,0:T(8,128)(2,1)S(1)} %get-tuple-element.110), channel_id=1, source_target_pairs={{0,3},{1,0},{2,1},{3,2},{4,7},{5,4},{6,5},{7,6},{8,11},{9,8},{10,9... | collective-permute-start | bytes 786440 | tf_op jit(solution)/shard_map/ppermute | solution.py:473
  62.7 0.0 collective-permute-done.12.rest_1_
  62.7 3.3 %collective-permute-done.13.rest_2_ = bf16[528,256]{1,0:T(8,128)(2,1)S(1)} collective-permute-done((bf16[528,256]{1,0:T(8,128)(2,1)S(1)}, bf16[528,256]{1,0:T(8,128)(2,1)S(1)}, u32[]{:S(2)}, u32[]{:S(2)}) %collective-permute-start.13) | collective-permute-done | bytes 270368 | tf_op jit(solution)/shard_map/ppermute | solution.py:470
  66.0 0.0 collective-permute-done.14.rest_3_
  66.0 0.2 collect.1
  66.2 2.2 %collective-permute-start.15 = (bf16[144,256]{1,0:T(8,128)(2,1)S(1)}, bf16[144,256]{1,0:T(8,128)(2,1)S(1)}, u32[]{:S(2)}, u32[]{:S(2)}) collective-permute-start(bf16[144,256]{1,0:T(8,128)(2,1)S(1)} %get-tuple-element.99), channel_id=1, source_target_pairs={{0,3},{1,0},{2,1},{3,2},{4,7},{5,4},{6,5},{7,6},{8,11},{9,8},{10,9... | collective-permute-start | bytes 221192 | tf_op jit(solution)/shard_map/ppermute | solution.py:473
  68.3 1.7 %collective-permute-start.16 = (bf16[144,256]{1,0:T(8,128)(2,1)S(1)}, bf16[144,256]{1,0:T(8,128)(2,1)S(1)}, u32[]{:S(2)}, u32[]{:S(2)}) collective-permute-start(bf16[144,256]{1,0:T(8,128)(2,1)S(1)} %get-tuple-element.100), channel_id=1, source_target_pairs={{0,2},{1,3},{2,0},{3,1},{4,6},{5,7},{6,4},{7,5},{8,10},{9,11},{10,... | collective-permute-start | bytes 221192 | tf_op jit(solution)/shard_map/ppermute | solution.py:473
  70.1 0.8 %collective-permute-start.17 = (bf16[144,256]{1,0:T(8,128)(2,1)S(1)}, bf16[144,256]{1,0:T(8,128)(2,1)S(1)}, u32[]{:S(2)}, u32[]{:S(2)}) collective-permute-start(bf16[144,256]{1,0:T(8,128)(2,1)S(1)} %get-tuple-element.101), channel_id=1, source_target_pairs={{0,1},{1,2},{2,3},{3,0},{4,5},{5,6},{6,7},{7,4},{8,9},{9,10},{10,1... | collective-permute-start | bytes 221192 | tf_op jit(solution)/shard_map/ppermute | solution.py:473
  70.9 0.0 collective-permute-done.19.rest_3_
  70.9 0.0 collective-permute-done.20.rest_4_
  70.9 1.1 %place_queries.1 = bf16[128,4096]{1,0:T(8,128)(2,1)} custom-call(bf16[128,512]{1,0:T(8,128)(2,1)S(1)} %collective-permute-done.10.rest_0_, bf16[128,512]{1,0:T(8,128)(2,1)S(1)} %collective-permute-done.18.rest_1_, bf16[128,1024]{1,0:T(8,128)(2,1)S(1)} %get-tuple-element.108.rest_2_, bf16[128,1024]{1,0:T(8,128)(2,1)S(1)} %collective-permute-done.19.rest_3_, ...), custom_call_target="tpu_custom_call" | custom-call | bytes 2097152 | tf_op jit(solution)/shard_map/place_queries/pallas_call | solution.py:592
  72.1 0.0 collective-permute-done.15.rest_1_
  72.1 5.9 %collective-permute-done.16.rest_2_ = bf16[144,256]{1,0:T(8,128)(2,1)S(1)} collective-permute-done((bf16[144,256]{1,0:T(8,128)(2,1)S(1)}, bf16[144,256]{1,0:T(8,128)(2,1)S(1)}, u32[]{:S(2)}, u32[]{:S(2)}) %collective-permute-start.16) | collective-permute-done | bytes 73760 | tf_op jit(solution)/shard_map/ppermute | solution.py:473
  78.0 0.0 collective-permute-done.17.rest_3_
  78.0 0.8 %finish.1 = (bf16[128,512]{1,0:T(8,128)(2,1)}, bf16[128,512]{1,0:T(8,128)(2,1)}, f32[2,512]{1,0:T(2,128)S(1)}) custom-call(f32[1,512]{1,0:T(1,128)S(1)} %bitcast.7, f32[1,512]{1,0:T(1,128)S(1)} %bitcast.11, f32[144,256]{1,0:T(8,128)S(1)} %get-tuple-element.112.rest_0_, bf16[144,256]{1,0:T(8,128)(2,1)S(1)} %collective-permute-done.15.rest_1_, ...), custom_call_target="tpu_custom_call" | custom-call | tf_op jit(solution)/shard_map/finish/pallas_call | solution.py:603
  78.8 0.0 collective-permute-start.21
  78.8 1.2 %collective-permute-done.21.other_ref = f32[2,512]{1,0:T(2,128)S(1)} collective-permute-done((f32[2,512]{1,0:T(2,128)S(1)}, f32[2,512]{1,0:T(2,128)S(1)}, u32[]{:S(2)}, u32[]{:S(2)}) %collective-permute-start.21) | collective-permute-done | bytes 4128 | tf_op jit(solution)/shard_map/ppermute | solution.py:470
  80.0 0.6 add_gains.1
  (10 shorter events, 0.1 us)
Async XLA Ops:
  3.4 8.6 %collective-permute-start = (bf16[144,256]{1,0:T(8,128)(2,1)}, bf16[144,256]{1,0:T(8,128)(2,1)S(1)}, u32[]{:S(2)}, u32[]{:S(2)}) collective-permute-start(bf16[144,256]{1,0:T(8,128)(2,1)} %get-tuple-element.64), channel_id=1, source_target_pairs={{0,1},{1,2},{2,3},{3,0},{4,5},{5,6},{6,7},{7,4},{8,9},{9,10},{10,1... | collective-permute-start | bytes 221192 | tf_op jit(solution)/shard_map/ppermute | solution.py:473
  6.5 7.8 %collective-permute-start.1 = (bf16[144,256]{1,0:T(8,128)(2,1)}, bf16[144,256]{1,0:T(8,128)(2,1)S(1)}, u32[]{:S(2)}, u32[]{:S(2)}) collective-permute-start(bf16[144,256]{1,0:T(8,128)(2,1)} %get-tuple-element.65), channel_id=1, source_target_pairs={{0,2},{1,3},{2,0},{3,1},{4,6},{5,7},{6,4},{7,5},{8,10},{9,11},{10,... | collective-permute-start | bytes 221192 | tf_op jit(solution)/shard_map/ppermute | solution.py:473
  9.1 5.4 %collective-permute-start.2 = (bf16[144,256]{1,0:T(8,128)(2,1)}, bf16[144,256]{1,0:T(8,128)(2,1)S(1)}, u32[]{:S(2)}, u32[]{:S(2)}) collective-permute-start(bf16[144,256]{1,0:T(8,128)(2,1)} %get-tuple-element.66), channel_id=1, source_target_pairs={{0,3},{1,0},{2,1},{3,2},{4,7},{5,4},{6,5},{7,6},{8,11},{9,8},{10,9... | collective-permute-start | bytes 221192 | tf_op jit(solution)/shard_map/ppermute | solution.py:473
  10.4 4.0 %copy-start.2 = (bf16[144,256]{1,0:T(8,128)(2,1)S(1)}, bf16[144,256]{1,0:T(8,128)(2,1)}, u32[]{:S(2)}) copy-start(bf16[144,256]{1,0:T(8,128)(2,1)} %get-tuple-element.68) | copy-start | bytes 221188
  10.4 19.2 %copy-start = (f32[512]{0:T(512)S(1)}, f32[512]{0:T(512)}, u32[]{:S(2)}) copy-start(f32[512]{0:T(512)} %param.17) | copy-start | bytes 6148
  10.4 19.2 %copy-start.1 = (f32[512]{0:T(512)S(1)}, f32[512]{0:T(512)}, u32[]{:S(2)}) copy-start(f32[512]{0:T(512)} %param.18) | copy-start | bytes 6148
  14.6 10.2 %collective-permute-start.8 = (bf16[512,256]{1,0:T(8,128)(2,1)S(1)}, bf16[512,256]{1,0:T(8,128)(2,1)S(1)}, u32[]{:S(2)}, u32[]{:S(2)}) collective-permute-start(bf16[512,256]{1,0:T(8,128)(2,1)S(1)} %pad_maximum_fusion.rest_5_.rest_0_), channel_id=1, source_target_pairs={{0,24},{4,28},{8,16},{12,20},{16,8},{20,12},{24,0},{28,4},{1,25},{... | collective-permute-start | bytes 786440 | tf_op jit(solution)/shard_map/ppermute | solution.py:470
  17.1 12.0 %collective-permute-start.6 = (bf16[512,256]{1,0:T(8,128)(2,1)S(1)}, bf16[512,256]{1,0:T(8,128)(2,1)S(1)}, u32[]{:S(2)}, u32[]{:S(2)}) collective-permute-start(bf16[512,256]{1,0:T(8,128)(2,1)S(1)} %pad_maximum_fusion.rest_5_.rest_0_), channel_id=1, source_target_pairs={{0,16},{4,20},{8,24},{12,28},{16,0},{20,4},{24,8},{28,12},{1,17},{... | collective-permute-start | bytes 786440 | tf_op jit(solution)/shard_map/ppermute | solution.py:470
  17.6 11.5 %collective-permute-start.4 = (bf16[512,256]{1,0:T(8,128)(2,1)S(1)}, bf16[512,256]{1,0:T(8,128)(2,1)S(1)}, u32[]{:S(2)}, u32[]{:S(2)}) collective-permute-start(bf16[512,256]{1,0:T(8,128)(2,1)S(1)} %pad_maximum_fusion.rest_5_.rest_0_), channel_id=1, source_target_pairs={{0,8},{4,12},{8,0},{12,4},{16,24},{20,28},{24,16},{28,20},{1,9},{5... | collective-permute-start | bytes 786440 | tf_op jit(solution)/shard_map/ppermute | solution.py:470
  18.2 15.1 %collective-permute-start.3 = (bf16[512,256]{1,0:T(8,128)(2,1)S(1)}, bf16[512,256]{1,0:T(8,128)(2,1)S(1)}, u32[]{:S(2)}, u32[]{:S(2)}) collective-permute-start(bf16[512,256]{1,0:T(8,128)(2,1)S(1)} %pad_maximum_fusion.rest_5_.rest_0_), channel_id=1, source_target_pairs={{0,4},{4,0},{8,12},{12,8},{16,20},{20,16},{24,28},{28,24},{1,5},{5... | collective-permute-start | bytes 786440 | tf_op jit(solution)/shard_map/ppermute | solution.py:470
  24.8 8.5 %collective-permute-start.9 = (bf16[512,256]{1,0:T(8,128)(2,1)S(1)}, bf16[512,256]{1,0:T(8,128)(2,1)S(1)}, u32[]{:S(2)}, u32[]{:S(2)}) collective-permute-start(bf16[512,256]{1,0:T(8,128)(2,1)S(1)} %collective-permute-done.8.rest_8_.rest_3_), channel_id=1, source_target_pairs={{0,4},{4,0},{8,12},{12,8},{16,20},{20,16},{24,28},{28,24},{1,5},{5... | collective-permute-start | bytes 786440 | tf_op jit(solution)/shard_map/ppermute | solution.py:470
  29.1 4.2 %collective-permute-start.7 = (bf16[512,256]{1,0:T(8,128)(2,1)S(1)}, bf16[512,256]{1,0:T(8,128)(2,1)S(1)}, u32[]{:S(2)}, u32[]{:S(2)}) collective-permute-start(bf16[512,256]{1,0:T(8,128)(2,1)S(1)} %collective-permute-done.6.rest_7_.rest_2_), channel_id=1, source_target_pairs={{0,4},{4,0},{8,12},{12,8},{16,20},{20,16},{24,28},{28,24},{1,5},{5... | collective-permute-start | bytes 786440 | tf_op jit(solution)/shard_map/ppermute | solution.py:470
  29.1 4.2 %collective-permute-start.5 = (bf16[512,256]{1,0:T(8,128)(2,1)S(1)}, bf16[512,256]{1,0:T(8,128)(2,1)S(1)}, u32[]{:S(2)}, u32[]{:S(2)}) collective-permute-start(bf16[512,256]{1,0:T(8,128)(2,1)S(1)} %collective-permute-done.4.rest_6_.rest_1_), channel_id=1, source_target_pairs={{0,4},{4,0},{8,12},{12,8},{16,20},{20,16},{24,28},{28,24},{1,5},{5... | collective-permute-start | bytes 786440 | tf_op jit(solution)/shard_map/ppermute | solution.py:470
  38.6 8.3 %collective-permute-start.10 = (bf16[128,512]{1,0:T(8,128)(2,1)S(1)}, bf16[128,512]{1,0:T(8,128)(2,1)S(1)}, u32[]{:S(2)}, u32[]{:S(2)}) collective-permute-start(bf16[128,512]{1,0:T(8,128)(2,1)S(1)} %get-tuple-element.92), channel_id=1, source_target_pairs={{0,2},{1,3},{2,0},{3,1},{4,6},{5,7},{6,4},{7,5},{8,10},{9,11},{10,... | collective-permute-start | bytes 393224 | tf_op jit(solution)/shard_map/ppermute | solution.py:473
  47.0 7.9 %collective-permute-start.11 = (bf16[2048,256]{1,0:T(8,128)(2,1)S(1)}, bf16[2048,256]{1,0:T(8,128)(2,1)S(1)}, u32[]{:S(2)}, u32[]{:S(2)}) collective-permute-start(bf16[2048,256]{1,0:T(8,128)(2,1)S(1)} %get-tuple-element.93), channel_id=1, source_target_pairs={{0,4},{4,0},{8,12},{12,8},{16,20},{20,16},{24,28},{28,24},{1,5},{5... | collective-permute-start | bytes 3145736 | tf_op jit(solution)/shard_map/ppermute | solution.py:470
  47.0 11.8 %collective-permute-start.18 = (bf16[128,512]{1,0:T(8,128)(2,1)S(1)}, bf16[128,512]{1,0:T(8,128)(2,1)S(1)}, u32[]{:S(2)}, u32[]{:S(2)}) collective-permute-start(bf16[128,512]{1,0:T(8,128)(2,1)S(1)} %get-tuple-element.106), channel_id=1, source_target_pairs={{0,2},{1,3},{2,0},{3,1},{4,6},{5,7},{6,4},{7,5},{8,10},{9,11},{10,... | collective-permute-start | bytes 393224 | tf_op jit(solution)/shard_map/ppermute | solution.py:473
  55.3 7.4 %collective-permute-start.12 = (bf16[528,256]{1,0:T(8,128)(2,1)S(1)}, bf16[528,256]{1,0:T(8,128)(2,1)S(1)}, u32[]{:S(2)}, u32[]{:S(2)}) collective-permute-start(bf16[528,256]{1,0:T(8,128)(2,1)S(1)} %get-tuple-element.95), channel_id=1, source_target_pairs={{0,8},{4,12},{8,0},{12,4},{16,24},{20,28},{24,16},{28,20},{1,9},{5... | collective-permute-start | bytes 811016 | tf_op jit(solution)/shard_map/ppermute | solution.py:470
  55.4 10.6 %collective-permute-start.13 = (bf16[528,256]{1,0:T(8,128)(2,1)S(1)}, bf16[528,256]{1,0:T(8,128)(2,1)S(1)}, u32[]{:S(2)}, u32[]{:S(2)}) collective-permute-start(bf16[528,256]{1,0:T(8,128)(2,1)S(1)} %get-tuple-element.96), channel_id=1, source_target_pairs={{0,16},{4,20},{8,24},{12,28},{16,0},{20,4},{24,8},{28,12},{1,17},{... | collective-permute-start | bytes 811016 | tf_op jit(solution)/shard_map/ppermute | solution.py:470
  55.4 10.6 %collective-permute-start.14 = (bf16[528,256]{1,0:T(8,128)(2,1)S(1)}, bf16[528,256]{1,0:T(8,128)(2,1)S(1)}, u32[]{:S(2)}, u32[]{:S(2)}) collective-permute-start(bf16[528,256]{1,0:T(8,128)(2,1)S(1)} %get-tuple-element.97), channel_id=1, source_target_pairs={{0,24},{4,28},{8,16},{12,20},{16,8},{20,12},{24,0},{28,4},{1,25},{... | collective-permute-start | bytes 811016 | tf_op jit(solution)/shard_map/ppermute | solution.py:470
  58.8 12.1 %collective-permute-start.19 = (bf16[128,1024]{1,0:T(8,128)(2,1)S(1)}, bf16[128,1024]{1,0:T(8,128)(2,1)S(1)}, u32[]{:S(2)}, u32[]{:S(2)}) collective-permute-start(bf16[128,1024]{1,0:T(8,128)(2,1)S(1)} %get-tuple-element.109), channel_id=1, source_target_pairs={{0,1},{1,2},{2,3},{3,0},{4,5},{5,6},{6,7},{7,4},{8,9},{9,10},{10,1... | collective-permute-start | bytes 786440 | tf_op jit(solution)/shard_map/ppermute | solution.py:473
  61.0 10.0 %collective-permute-start.20 = (bf16[128,1024]{1,0:T(8,128)(2,1)S(1)}, bf16[128,1024]{1,0:T(8,128)(2,1)S(1)}, u32[]{:S(2)}, u32[]{:S(2)}) collective-permute-start(bf16[128,1024]{1,0:T(8,128)(2,1)S(1)} %get-tuple-element.110), channel_id=1, source_target_pairs={{0,3},{1,0},{2,1},{3,2},{4,7},{5,4},{6,5},{7,6},{8,11},{9,8},{10,9... | collective-permute-start | bytes 786440 | tf_op jit(solution)/shard_map/ppermute | solution.py:473
  66.2 5.9 %collective-permute-start.15 = (bf16[144,256]{1,0:T(8,128)(2,1)S(1)}, bf16[144,256]{1,0:T(8,128)(2,1)S(1)}, u32[]{:S(2)}, u32[]{:S(2)}) collective-permute-start(bf16[144,256]{1,0:T(8,128)(2,1)S(1)} %get-tuple-element.99), channel_id=1, source_target_pairs={{0,3},{1,0},{2,1},{3,2},{4,7},{5,4},{6,5},{7,6},{8,11},{9,8},{10,9... | collective-permute-start | bytes 221192 | tf_op jit(solution)/shard_map/ppermute | solution.py:473
  68.3 9.7 %collective-permute-start.16 = (bf16[144,256]{1,0:T(8,128)(2,1)S(1)}, bf16[144,256]{1,0:T(8,128)(2,1)S(1)}, u32[]{:S(2)}, u32[]{:S(2)}) collective-permute-start(bf16[144,256]{1,0:T(8,128)(2,1)S(1)} %get-tuple-element.100), channel_id=1, source_target_pairs={{0,2},{1,3},{2,0},{3,1},{4,6},{5,7},{6,4},{7,5},{8,10},{9,11},{10,... | collective-permute-start | bytes 221192 | tf_op jit(solution)/shard_map/ppermute | solution.py:473
  70.1 7.9 %collective-permute-start.17 = (bf16[144,256]{1,0:T(8,128)(2,1)S(1)}, bf16[144,256]{1,0:T(8,128)(2,1)S(1)}, u32[]{:S(2)}, u32[]{:S(2)}) collective-permute-start(bf16[144,256]{1,0:T(8,128)(2,1)S(1)} %get-tuple-element.101), channel_id=1, source_target_pairs={{0,1},{1,2},{2,3},{3,0},{4,5},{5,6},{6,7},{7,4},{8,9},{9,10},{10,1... | collective-permute-start | bytes 221192 | tf_op jit(solution)/shard_map/ppermute | solution.py:473
  78.8 1.2 %collective-permute-start.21 = (f32[2,512]{1,0:T(2,128)S(1)}, f32[2,512]{1,0:T(2,128)S(1)}, u32[]{:S(2)}, u32[]{:S(2)}) collective-permute-start(f32[2,512]{1,0:T(2,128)S(1)} %get-tuple-element.118.gains_ref), channel_id=1, source_target_pairs={{0,4},{4,0},{8,12},{12,8},{16,20},{20,16},{24,28},{28,24},{1,5},{5... | collective-permute-start | bytes 12296 | tf_op jit(solution)/shard_map/ppermute | solution.py:470
